TPU v7x, 256 devices: a whole 4x4x8 slice. The times are simulated.
256 devices in a mesh: seq: 64 (over z, y, core), tensor: 4 (over x).
Axes of the slice: x: 4, y: 4, z: 8, core: 2. Of those that a mesh axis runs over, the one named last changes fastest.
Arguments:
- queries: bfloat16 [8192, 4096], P('seq', 'tensor'), may hold values from -6 to 6
- rollout_suffix_keys: bfloat16 [8192, 512], P('seq', 'tensor'), may hold values from -6 to 6
- rollout_suffix_values: bfloat16 [8192, 512], P('seq', 'tensor'), may hold values from -6 to 6
- blockwise_prefix_keys: bfloat16 [8192, 512], P('seq', 'tensor'), may hold values from -6 to 6
- blockwise_prefix_values: bfloat16 [8192, 512], P('seq', 'tensor'), may hold values from -6 to 6
- block_prompt: int32 [64], P('seq'), may hold values from 0 to 7, as said below
- rollout_prompt: int32 [64], P('seq'), may hold values from 0 to 7, as said below
- suffix_length: int32 [64], P('seq'), may hold values from 32 to 128, as said below
- out_weight: bfloat16 [4096, 2560], P('tensor'), may hold values from -0.09375 to 0.09375
- out_grad: bfloat16 [8192, 2560], P('seq', 'tensor'), may hold values from -6 to 6
Outputs:
- projected: bfloat16 [8192, 2560], P('seq', 'tensor')
- d_queries: bfloat16 [8192, 4096], P('seq', 'tensor')
- d_suffix_keys: bfloat16 [8192, 512], P('seq', 'tensor')
- d_suffix_values: bfloat16 [8192, 512], P('seq', 'tensor')
- d_prefix_keys: bfloat16 [8192, 512], P('seq', 'tensor')
- d_prefix_values: bfloat16 [8192, 512], P('seq', 'tensor')
Inputs may be any that keep to these rules, and one draw needn't show every extreme that they name: `block_prompt`: each prompt owns exactly 8 blocks. `rollout_prompt`: each prompt has exactly 8 rollouts. `suffix_length`: some rollout has length 128.
All inputs are finite; a program needn't handle non-finite values.
Results may differ from a plain program's by a relative error of at most 0.039.
Values may be sent and summed in bfloat16 or wider, within the bound.
No kernel may reach another device: no remote copies, remote signals or barrier semaphores. Data moves between devices by JAX's collectives and lax.ppermute only.
A program may use at most 64 MiB of HBM per device.

v0:
```python
import jax
import jax.numpy as jnp
from jax import lax
from jax.sharding import PartitionSpec as P

HEAD_WIDTH = 128
BLOCK_TOKENS = 128
PROMPTS = 8


def scores_of(query_rows, key_block, score_scale):
    return (
        jnp.einsum("sged,kgd->sgek", query_rows, key_block, preferred_element_type=jnp.float32)
        * score_scale
    )


def grad_block(
    query_rows, d_rows, log_total, row_dots, key_block, value_block, score_scale, visible_mask
):
    logits = scores_of(query_rows, key_block, score_scale)
    if visible_mask is not None:
        logits = jnp.where(visible_mask, logits, -jnp.inf)
    probs = jnp.exp(logits - log_total[..., None])
    d_probs = jnp.einsum("sged,kgd->sgek", d_rows, value_block, preferred_element_type=jnp.float32)
    d_logits = (probs * (d_probs - row_dots[..., None])).astype(jnp.bfloat16)
    dq_add = (
        jnp.einsum("sgek,kgd->sged", d_logits, key_block, preferred_element_type=jnp.float32)
        * score_scale
    )
    dk_add = (
        jnp.einsum("sgek,sged->kgd", d_logits, query_rows, preferred_element_type=jnp.float32)
        * score_scale
    )
    dv_add = jnp.einsum(
        "sgek,sged->kgd", probs.astype(jnp.bfloat16), d_rows, preferred_element_type=jnp.float32
    )
    return (dq_add, dk_add, dv_add)


def shards(
    queries,
    rollout_suffix_keys,
    rollout_suffix_values,
    blockwise_prefix_keys,
    blockwise_prefix_values,
    block_prompt,
    rollout_prompt,
    suffix_length,
    out_weight,
    out_grad,
):
    kv_heads = rollout_suffix_keys.shape[1] // HEAD_WIDTH
    own_rollouts = rollout_prompt.shape[0]
    suffix_rows = queries.shape[0] // own_rollouts
    group_stride = queries.shape[1] // (kv_heads * HEAD_WIDTH)
    local_blocks = block_prompt.shape[0]
    all_blocks = local_blocks * lax.axis_size("seq")
    prefix_rows = all_blocks * BLOCK_TOKENS
    score_scale = HEAD_WIDTH ** (-0.5)
    query_head_rows = queries.reshape(own_rollouts, suffix_rows, kv_heads, group_stride, HEAD_WIDTH)
    key_suffix = rollout_suffix_keys.reshape(own_rollouts, suffix_rows, kv_heads, HEAD_WIDTH)
    value_suffix = rollout_suffix_values.reshape(own_rollouts, suffix_rows, kv_heads, HEAD_WIDTH)
    positions = jnp.arange(suffix_rows)
    live_rows = positions[None, :] < suffix_length[:, None]
    visible = (positions[:, None] >= positions[None, :])[None] & live_rows[:, None, :]
    group_member = 0
    logits = scores_of(query_head_rows[group_member], key_suffix[group_member], score_scale)
    suffix_logits = [jnp.where(visible[group_member][:, None, None, :], logits, -jnp.inf)]
    whole_keys, whole_values, whole_prompts = (
        lax.all_gather(blockwise_prefix_keys, "seq", axis=0, tiled=True),
        lax.all_gather(blockwise_prefix_values, "seq", axis=0, tiled=True),
        lax.all_gather(block_prompt, "seq", axis=0, tiled=True),
    )
    prompt_stride = all_blocks // PROMPTS
    block_order = jnp.argsort(whole_prompts, stable=True)
    key_blocks = whole_keys.reshape(all_blocks, BLOCK_TOKENS, kv_heads, HEAD_WIDTH)
    value_blocks = whole_values.reshape(all_blocks, BLOCK_TOKENS, kv_heads, HEAD_WIDTH)
    selected_blocks = [
        lax.dynamic_slice_in_dim(block_order, rollout_prompt[0] * prompt_stride, prompt_stride)
    ]
    prefix_key_piece = [
        key_blocks[picked].reshape(prompt_stride * BLOCK_TOKENS, kv_heads, HEAD_WIDTH)
        for picked in selected_blocks
    ]
    prefix_value_piece = [
        value_blocks[picked].reshape(prompt_stride * BLOCK_TOKENS, kv_heads, HEAD_WIDTH)
        for picked in selected_blocks
    ]
    group_member = 0
    pre_logits = scores_of(
        query_head_rows[group_member], prefix_key_piece[group_member], score_scale
    )
    peak = jnp.maximum(jnp.max(pre_logits, -1), jnp.max(suffix_logits[group_member], -1))
    w_pre = jnp.exp(pre_logits - peak[..., None])
    w_suf = jnp.exp(suffix_logits[group_member] - peak[..., None])
    weight_sum = jnp.sum(w_pre, -1) + jnp.sum(w_suf, -1)
    accum = jnp.einsum(
        "sgek,kgd->sged",
        w_pre.astype(jnp.bfloat16),
        prefix_value_piece[group_member],
        preferred_element_type=jnp.float32,
    )
    accum = accum + jnp.einsum(
        "sgek,kgd->sged",
        w_suf.astype(jnp.bfloat16),
        value_suffix[group_member],
        preferred_element_type=jnp.float32,
    )
    outputs = [accum / weight_sum[..., None]]
    log_totals = [peak + jnp.log(weight_sum)]
    attended = (jnp.stack(outputs) * live_rows[:, :, None, None, None]).astype(jnp.bfloat16)
    log_total = jnp.stack(log_totals)
    row_count = queries.shape[0]
    head_terms = jnp.dot(
        attended.reshape(row_count, queries.shape[1]),
        out_weight,
        preferred_element_type=jnp.float32,
    )
    projected = lax.psum_scatter(head_terms, "tensor", scatter_dimension=1, tiled=True).astype(
        jnp.bfloat16
    )
    full_grad = lax.all_gather(out_grad, "tensor", axis=1, tiled=True)
    attended_gradient = lax.dot_general(
        full_grad, out_weight, (((1,), (1,)), ((), ())), preferred_element_type=jnp.float32
    )
    attended_gradient = (attended_gradient * live_rows.reshape(row_count)[:, None]).astype(
        jnp.bfloat16
    )
    attended_gradient = attended_gradient.reshape(
        own_rollouts, suffix_rows, kv_heads, group_stride, HEAD_WIDTH
    )
    row_dots = jnp.sum(attended_gradient.astype(jnp.float32) * attended.astype(jnp.float32), -1)
    group_member = 0
    dq_add, dk_add, dv_add = grad_block(
        query_head_rows[group_member],
        attended_gradient[group_member],
        log_total[group_member],
        row_dots[group_member],
        key_suffix[group_member],
        value_suffix[group_member],
        score_scale,
        visible[group_member][:, None, None, :],
    )
    dq_list = [dq_add]
    dk_suffix = [dk_add]
    dv_suffix = [dv_add]
    dk_blocks = jnp.zeros((all_blocks, BLOCK_TOKENS, kv_heads, HEAD_WIDTH), jnp.float32)
    dv_blocks = jnp.zeros((all_blocks, BLOCK_TOKENS, kv_heads, HEAD_WIDTH), jnp.float32)
    group_member = 0
    dq_add, dk_add, dv_add = grad_block(
        query_head_rows[group_member],
        attended_gradient[group_member],
        log_total[group_member],
        row_dots[group_member],
        prefix_key_piece[group_member],
        prefix_value_piece[group_member],
        score_scale,
        None,
    )
    dq_list[group_member] = dq_list[group_member] + dq_add
    dk_blocks = dk_blocks.at[selected_blocks[group_member]].add(
        dk_add.reshape(prompt_stride, BLOCK_TOKENS, kv_heads, HEAD_WIDTH)
    )
    dv_blocks = dv_blocks.at[selected_blocks[group_member]].add(
        dv_add.reshape(prompt_stride, BLOCK_TOKENS, kv_heads, HEAD_WIDTH)
    )
    dk_term = dk_blocks.reshape(prefix_rows, kv_heads * HEAD_WIDTH)
    dv_term = dv_blocks.reshape(prefix_rows, kv_heads * HEAD_WIDTH)
    dk_prefix, dv_prefix = (
        lax.psum_scatter(dk_term, "seq", scatter_dimension=0, tiled=True),
        lax.psum_scatter(dv_term, "seq", scatter_dimension=0, tiled=True),
    )
    d_queries = jnp.stack(dq_list).reshape(row_count, queries.shape[1]).astype(jnp.bfloat16)
    d_suffix_keys = (
        jnp.stack(dk_suffix).reshape(row_count, kv_heads * HEAD_WIDTH).astype(jnp.bfloat16)
    )
    d_suffix_values = (
        jnp.stack(dv_suffix).reshape(row_count, kv_heads * HEAD_WIDTH).astype(jnp.bfloat16)
    )
    return (
        projected,
        d_queries,
        d_suffix_keys,
        d_suffix_values,
        dk_prefix.astype(jnp.bfloat16),
        dv_prefix.astype(jnp.bfloat16),
    )


def solution(mesh):
    in_specs = (
        P("seq", "tensor"),
        P("seq", "tensor"),
        P("seq", "tensor"),
        P("seq", "tensor"),
        P("seq", "tensor"),
        P("seq"),
        P("seq"),
        P("seq"),
        P("tensor", None),
        P("seq", "tensor"),
    )
    out_specs = (
        P("seq", "tensor"),
        P("seq", "tensor"),
        P("seq", "tensor"),
        P("seq", "tensor"),
        P("seq", "tensor"),
        P("seq", "tensor"),
    )
    return jax.shard_map(shards, mesh=mesh, in_specs=in_specs, out_specs=out_specs, check_vma=False)
```

profile of v0, /device:TPU:1, one launch (start us, length us, event | category | flops | bytes accessed | tf_op | source)
XLA Modules:
  0.0 502.2 jit_solution(15473863120849383819)
XLA Ops:
  7.2 0.7 all-gather.5.cloned.1.call-update
  8.0 0.7 all-gather.3.cloned.1.call-update
  9.4 13.2 %all_gather.15 = bf16[128,2560]{1,0:T(8,128)(2,1)S(1)} all-gather(bf16[128,640]{1,0:T(8,128)(2,1)} %param.19), channel_id=1, replica_groups=mesh['seq'=64,'tensor'=4] {'tensor'}, dimensions={1}, use_global_device_ids=true | all-gather | bytes 819200 | tf_op jit(solution)/shard_map/all_gather | solution.py:123
  22.6 4.3 fusion.39
  26.9 0.1 copy.51
  28.4 0.6 dynamic-slice
  29.0 0.8 dynamic-update-slice
  29.7 21.4 %all-reduce = s32[64]{0:T(128)S(1)} all-reduce(s32[64]{0:T(128)S(1)} %dynamic-update-slice), channel_id=1, replica_groups=mesh['seq'=64,'tensor'=4] {'seq'}, use_global_device_ids=true, to_apply=%add | all-reduce | flops 64 | bytes 512
  51.1 2.0 sort.17
  53.3 0.2 fusion.77
  53.6 38.8 %all-gather.5.cloned.1.call-done = bf16[8192,128]{1,0:T(8,128)(2,1)} async-done(((bf16[128,128]{1,0:T(8,128)(2,1)}), bf16[8192,128]{1,0:T(8,128)(2,1)}) %all-gather.5.cloned.1.call-update) | async-done | bytes 2097168 | tf_op jit(solution)/shard_map/all_gather | solution.py:71
  92.4 2.2 gather_fusion.1
  94.6 0.7 bitcast_reduce_fusion
  95.3 0.1 fusion.48
  95.4 1.8 copy-done.1
  97.2 0.7 fusion.4
  97.9 72.2 %all-gather.3.cloned.1.call-done = bf16[8192,128]{1,0:T(8,128)(2,1)} async-done(((bf16[128,128]{1,0:T(8,128)(2,1)}), bf16[8192,128]{1,0:T(8,128)(2,1)}) %all-gather.3.cloned.1.call-update) | async-done | bytes 2097168 | tf_op jit(solution)/shard_map/all_gather | solution.py:72
  170.1 2.2 gather_fusion
  172.3 3.2 fusion.7
  175.5 0.3 multiply_reduce_fusion
  175.9 0.2 copy.48
  176.1 4.5 fusion.54
  180.6 3.4 fusion
  184.0 1.6 fusion.32
  185.6 2.5 broadcast.111.clone
  188.0 3.1 scatter_fusion
  191.2 0.2 reduce-scatter.8.cloned.1.call-start
  191.4 0.7 copy.87
  192.2 4.3 fusion.9
  196.5 4.2 copy.77
  200.7 3.1 convolution_bitcast_fusion
  203.8 2.1 copy.84
  205.9 2.4 broadcast.111.clone.1
  208.3 2.9 scatter_fusion.1
  211.3 0.2 fusion.41
  211.5 0.7 copy-done.3
  212.2 0.3 fusion.19
  212.5 0.5 fusion.36
  213.0 0.9 copy.63
  213.9 0.2 copy.75
  214.1 1.2 fusion.45
  215.3 0.7 copy.64
  216.1 0.8 fusion.43
  216.9 1.7 convert_element_type.119
  218.6 128.9 %reduce-scatter.6.cloned.1.call-done = f32[128,128]{1,0:T(8,128)} async-done(((f32[8192,128]{1,0:T(8,128)}), f32[128,128]{1,0:T(8,128)}) %reduce-scatter.6.cloned.1.call-update) | async-done | bytes 65552 | tf_op jit(solution)/shard_map/reduce_scatter | solution.py:171
  347.5 1.5 convert_element_type.137
  348.9 145.2 %reduce-scatter.8.cloned.1.call-done = f32[128,128]{1,0:T(8,128)} async-done(((f32[8192,128]{1,0:T(8,128)}), f32[128,128]{1,0:T(8,128)}) %reduce-scatter.8.cloned.1.call-update) | async-done | bytes 65552 | tf_op jit(solution)/shard_map/reduce_scatter | solution.py:172
  494.2 1.5 convert_element_type.139
  (31 shorter events, 0.5 us)
Async XLA Ops:
  7.2 46.1 %copy-start = (bf16[128,1024]{1,0:T(8,128)(2,1)S(1)}, bf16[128,1024]{1,0:T(8,128)(2,1)}, u32[]{:S(2)}) copy-start(bf16[128,1024]{1,0:T(8,128)(2,1)} %param.10) | copy-start | bytes 786436
  7.2 21.2 %copy-start.7 = (u32[256]{0:T(256)S(1)}, u32[256]{0:T(256)}, u32[]{:S(2)}) copy-start(u32[256]{0:T(256)} %constant.24) | copy-start | bytes 3076
  7.2 46.1 %copy-start.5 = (bf16[128,128]{1,0:T(8,128)(2,1)S(1)}, bf16[128,128]{1,0:T(8,128)(2,1)}, u32[]{:S(2)}) copy-start(bf16[128,128]{1,0:T(8,128)(2,1)} %param.11) | copy-start | bytes 98308
  7.2 85.2 %all-gather.5.cloned.1.call-start = ((), (), s32[]{:S(2)}) async-start(), calls=%async_computation.4 | async-start | bytes 2129920 | tf_op jit(solution)/shard_map/all_gather | solution.py:71
  7.9 162.2 %all-gather.3.cloned.1.call-start = ((), (), s32[]{:S(2)}) async-start(), calls=%async_computation.3 | async-start | bytes 2129920 | tf_op jit(solution)/shard_map/all_gather | solution.py:72
  8.7 208.2 %reduce-scatter.4.cloned.1.call-start = ((), (), s32[]{:S(2)}) async-start(), calls=%async_computation.5 | async-start | bytes 1638400 | tf_op jit(solution)/shard_map/reduce_scatter | solution.py:120
  95.3 1.9 copy-start.1
  97.2 78.3 %copy-start.6 = (bf16[128,128]{1,0:T(8,128)(2,1)S(1)}, bf16[128,128]{1,0:T(8,128)(2,1)}, u32[]{:S(2)}) copy-start(bf16[128,128]{1,0:T(8,128)(2,1)} %param.12) | copy-start | bytes 98308
  172.3 3.8 copy-start.2
  180.6 166.9 %reduce-scatter.6.cloned.1.call-start = ((), (), s32[]{:S(2)}) async-start(), calls=%async_computation.6 | async-start | bytes 4259840 | tf_op jit(solution)/shard_map/reduce_scatter | solution.py:171
  191.2 303.0 %reduce-scatter.8.cloned.1.call-start = ((), (), s32[]{:S(2)}) async-start(), calls=%async_computation.7 | async-start | bytes 4259840 | tf_op jit(solution)/shard_map/reduce_scatter | solution.py:172
  211.5 0.7 copy-start.3
  213.0 3.1 copy-start.4
Sparse Core Ops, SparseCore 0:
  10.8 81.5 all-gather.4
  95.1 74.9 all-gather.2
  180.7 23.0 reduce-scatter.3
  207.7 139.7 reduce-scatter.5
  352.0 142.1 reduce-scatter.7
where the time goes:
time: 507 us; the launch traced here: 502 us
  waiting for transfers between devices  387 us (76%)
  blocking collectives  34.6 us (7%)
  matrix products  24.3 us (5%)
  local copies, waits for them, and re-layouts  22.3 us (4%)
  other arithmetic  18 us (4%)
  between operations  16 us (3%)
    reduce_scatter x1, waiting for transfers between devices, shards(): lax.psum_scatter(dv_term, 'seq', scatter_dimension=0, tiled=True)  145 us
    reduce_scatter x1, waiting for transfers between devices, shards(): lax.psum_scatter(dk_term, 'seq', scatter_dimension=0, tiled=True)  129 us
    all_gather x1, waiting for transfers between devices, shards(): lax.all_gather(blockwise_prefix_values, 'seq', axis=0, tiled=True)  72.2 us
    all_gather x1, waiting for transfers between devices, shards(): lax.all_gather(blockwise_prefix_keys, 'seq', axis=0, tiled=True)  38.8 us
    unnamed x1, blocking collectives  21.4 us
    all_gather x1, blocking collectives, shards(): full_grad = lax.all_gather(out_grad, 'tensor', axis=1, tiled=True)  13.2 us
  transfers between devices with their start and end apart: 5, of which 4 were waited for; matrix products, arithmetic and copies ran while one was open for 10% of the time, Pallas kernels for 0%

commit v1 on v0

v1 whole, which is shorter than its diff:
```python
import functools

import jax
import jax.numpy as jnp
from jax import lax
from jax.experimental import pallas as pl
from jax.experimental.pallas import tpu as pltpu
from jax.sharding import PartitionSpec as P

HEAD_WIDTH = 128
PROMPTS = 8
F32 = jnp.float32
BF16 = jnp.bfloat16
NT = (((1,), (1,)), ((), ()))
VMEM_LIMIT = 56 * 1024 * 1024


def dot(a, b):
    return jnp.dot(a, b, preferred_element_type=F32)


def dot_nt(a, b):
    return lax.dot_general(a, b, NT, preferred_element_type=F32)


def iota(shape, dim):
    return lax.broadcasted_iota(jnp.int32, shape, dim)


def select_kernel(pieces_ref, picked_ref, map_ref, *, blocks, per_prompt, width):
    meta = pieces_ref[:, width : width + 128].astype(F32)
    block_prompt, rollout_prompt = meta[:, 0:1], meta[:, 1:2]
    lanes = iota((blocks, 128), 1).astype(F32)
    one_hot = (block_prompt == lanes).astype(BF16)
    same = dot_nt(one_hot, one_hot)
    row, col = iota((blocks, blocks), 0), iota((blocks, blocks), 1)
    rank = jnp.sum(jnp.where(col < row, same, 0.0), axis=1, keepdims=True)
    code_col = block_prompt * per_prompt + rank
    code_row = jnp.sum(jnp.where(row == col, code_col, 0.0), axis=0, keepdims=True)
    wants = blocks * per_prompt
    expand = (iota((wants, blocks), 0) // per_prompt == iota((wants, blocks), 1)).astype(F32)
    rollout_row = jnp.sum(jnp.where(row == col, rollout_prompt, 0.0), axis=0, keepdims=True)
    want_col = jnp.sum(expand * rollout_row, axis=1, keepdims=True) * per_prompt
    want_col = want_col + (iota((wants, 1), 0) % per_prompt).astype(F32)
    expand_t = (iota((blocks, wants), 1) // per_prompt == iota((blocks, wants), 0)).astype(F32)
    want_row = jnp.sum(expand_t * rollout_prompt, axis=0, keepdims=True) * per_prompt
    want_row = want_row + (iota((1, wants), 1) % per_prompt).astype(F32)
    choose = (want_col == code_row).astype(BF16)
    map_ref[...] = (code_col == want_row).astype(BF16)
    picked_ref[...] = dot(choose, pieces_ref[:, :width]).astype(BF16)


def combine_kernel(map_ref, terms_ref, out_ref):
    out_ref[...] = dot(map_ref[...], terms_ref[...]).astype(BF16)


def grad_rows_kernel(at_ref, len_ref, g0, g1, g2, g3, w_ref, rows_ref, cols_ref, acc):
    step = pl.program_id(0)
    for d, g in enumerate((g0, g1, g2, g3)):

        @pl.when(step == d)
        def _():
            term = dot_nt(w_ref[...], g[...])
            acc[...] = term if d == 0 else acc[...] + term

    @pl.when(step == 3)
    def _():
        total = acc[...]
        live = iota(total.shape, 1) < len_ref[0]
        total = jnp.where(live, total, 0.0)
        cols_ref[...] = total.astype(BF16)
        for h in range(total.shape[0] // HEAD_WIDTH):
            part = slice(h * HEAD_WIDTH, (h + 1) * HEAD_WIDTH)
            rows_ref[:, part] = total[part].T.astype(BF16)


def project_kernel(at_ref, a_ref, w_ref, o0, o1, o2, o3):
    step = pl.program_id(0)
    for d, o in enumerate((o0, o1, o2, o3)):

        @pl.when(step == d)
        def _():
            o[...] = dot(a_ref[...], w_ref[...]).astype(o.dtype)


def attention_kernel(
    len_ref,
    q_ref,
    ks_ref,
    vs_ref,
    g_ref,
    da_ref,
    dat_ref,
    att_ref,
    dq_ref,
    dks_ref,
    dvs_ref,
    dg_ref,
    k_all,
    v_all,
    dk_acc,
    dv_acc,
    *,
    scale,
):
    n = len_ref[0]
    pieces, width = g_ref.shape
    parts = width // 256
    suffix = ks_ref.shape[0]
    prefix = pieces * parts
    for t in range(parts):
        rows = slice(t * pieces, (t + 1) * pieces)
        k_all[rows, :] = g_ref[:, t * 128 : (t + 1) * 128]
        v_all[rows, :] = g_ref[:, (parts + t) * 128 : (parts + t + 1) * 128]
    k_all[prefix:, :] = ks_ref[...]
    v_all[prefix:, :] = vs_ref[...]
    k_t = k_all[...].T
    v_t = v_all[...].T
    heads = q_ref.shape[1] // 128
    key_at = iota((suffix, 2 * suffix), 0)
    slot_at = iota((suffix, 2 * suffix), 1) % suffix
    hidden = jnp.logical_or(key_at > slot_at, key_at >= n)
    live = iota((1, 2 * suffix), 1) % suffix < n
    to_log2 = scale * 1.4426950408889634
    for pair in range(heads // 2):
        one = slice(pair * 256, pair * 256 + 128)
        two = slice(pair * 256 + 128, pair * 256 + 256)
        q2 = jnp.concatenate([q_ref[:, one], q_ref[:, two]], axis=0)
        da2 = jnp.concatenate([da_ref[:, one], da_ref[:, two]], axis=0)
        dat2 = jnp.concatenate([dat_ref[one, :], dat_ref[two, :]], axis=1)
        s_pre = dot_nt(k_all[:prefix], q2)
        s_suf = jnp.where(hidden, -jnp.inf, dot_nt(k_all[prefix:], q2))
        peak = jnp.maximum(
            jnp.max(s_pre, axis=0, keepdims=True), jnp.max(s_suf, axis=0, keepdims=True)
        )
        w = jnp.concatenate(
            [jnp.exp2((s_pre - peak) * to_log2), jnp.exp2((s_suf - peak) * to_log2)], axis=0
        )
        inverse = 1.0 / jnp.sum(w, axis=0, keepdims=True)
        out_t = dot(v_t, w.astype(BF16)) * inverse
        out_t = jnp.where(live, out_t, 0.0).astype(BF16).astype(F32)
        att_ref[:, one] = out_t[:, :128].T.astype(BF16)
        att_ref[:, two] = out_t[:, 128:].T.astype(BF16)
        dots = jnp.sum(out_t * dat2.astype(F32), axis=0, keepdims=True)
        probs = w * inverse
        ds = (probs * (dot(v_all[...], dat2) - dots)).astype(BF16)
        dq_t = dot(k_t, ds) * scale
        dq_ref[:, one] = dq_t[:, :128].T.astype(BF16)
        dq_ref[:, two] = dq_t[:, 128:].T.astype(BF16)
        dk = dot(ds, q2)
        dv = dot(probs.astype(BF16), da2)
        if pair == 0:
            dk_acc[...] = dk
            dv_acc[...] = dv
        else:
            dk_acc[...] += dk
            dv_acc[...] += dv
    for t in range(parts):
        rows = slice(t * pieces, (t + 1) * pieces)
        dg_ref[:, t * 128 : (t + 1) * 128] = (dk_acc[rows] * scale).astype(BF16)
        dg_ref[:, (parts + t) * 128 : (parts + t + 1) * 128] = dv_acc[rows].astype(BF16)
    dks_ref[...] = (dk_acc[prefix:] * scale).astype(BF16)
    dvs_ref[...] = dv_acc[prefix:].astype(BF16)


def whole(memory=pltpu.VMEM):
    return pl.BlockSpec(memory_space=memory)


def params():
    return pltpu.CompilerParams(vmem_limit_bytes=VMEM_LIMIT)


def shape(*dims, dtype=BF16):
    return jax.ShapeDtypeStruct(dims, dtype)


def shards(
    queries,
    suffix_keys,
    suffix_values,
    prefix_keys,
    prefix_values,
    block_prompt,
    rollout_prompt,
    suffix_length,
    out_weight,
    out_grad,
):
    homes = lax.axis_size("seq")
    cuts = lax.axis_size("tensor")
    rows, width = queries.shape
    features = out_grad.shape[1]
    per_prompt = homes // PROMPTS
    tokens = prefix_keys.shape[0] // homes
    piece = 2 * tokens * HEAD_WIDTH
    at = lax.axis_index("tensor").astype(jnp.int32).reshape(1)

    parts = [p[t * homes : (t + 1) * homes] for p in (prefix_keys, prefix_values) for t in range(tokens)]
    lane = iota((homes, 128), 1)
    meta = jnp.where(lane == 0, block_prompt[0], jnp.where(lane == 1, rollout_prompt[0], 0))
    sent = jnp.concatenate(parts + [meta.astype(BF16)], axis=1)
    pieces = lax.all_to_all(sent, "seq", 0, 0, tiled=True)
    picked, home_map = pl.pallas_call(
        functools.partial(select_kernel, blocks=homes, per_prompt=per_prompt, width=piece),
        out_shape=(shape(homes * per_prompt, piece), shape(homes, homes * per_prompt)),
        in_specs=[whole()],
        out_specs=(whole(), whole()),
        compiler_params=params(),
        name="select",
    )(pieces)
    gathered = lax.all_to_all(
        picked.reshape(homes, per_prompt, piece), "seq", 0, 0, tiled=True
    ).reshape(homes * per_prompt, piece)

    turn = lambda x, d: lax.ppermute(x, "tensor", [(i, (i + d) % cuts) for i in range(cuts)])
    grads = [out_grad] + [turn(out_grad, cuts - d) for d in range(1, cuts)]
    weight_spec = pl.BlockSpec(
        (width, features), lambda d, at_ref, *_: (0, lax.rem(at_ref[0] + d, cuts))
    )
    d_rows, d_cols = pl.pallas_call(
        grad_rows_kernel,
        out_shape=(shape(rows, width), shape(width, rows)),
        grid_spec=pltpu.PrefetchScalarGridSpec(
            num_scalar_prefetch=2,
            grid=(cuts,),
            in_specs=[whole()] * cuts + [weight_spec],
            out_specs=(whole(), whole()),
            scratch_shapes=[pltpu.VMEM((width, rows), F32)],
        ),
        compiler_params=params(),
        name="grad_rows",
    )(at, suffix_length, *grads, out_weight)

    keys = prefix_keys.shape[0] * per_prompt + rows
    attended, d_queries, d_suffix_keys, d_suffix_values, d_gathered = pl.pallas_call(
        functools.partial(attention_kernel, scale=HEAD_WIDTH**-0.5),
        out_shape=(
            shape(rows, width),
            shape(rows, width),
            shape(rows, HEAD_WIDTH),
            shape(rows, HEAD_WIDTH),
            shape(homes * per_prompt, piece),
        ),
        in_specs=[whole(pltpu.SMEM)] + [whole()] * 6,
        out_specs=(whole(),) * 5,
        scratch_shapes=[
            pltpu.VMEM((keys, HEAD_WIDTH), BF16),
            pltpu.VMEM((keys, HEAD_WIDTH), BF16),
            pltpu.VMEM((keys, HEAD_WIDTH), F32),
            pltpu.VMEM((keys, HEAD_WIDTH), F32),
        ],
        compiler_params=params(),
        name="attention",
    )(suffix_length, queries, suffix_keys, suffix_values, gathered, d_rows, d_cols)

    head_terms = pl.pallas_call(
        project_kernel,
        out_shape=(shape(rows, features, dtype=F32),) + (shape(rows, features),) * (cuts - 1),
        grid_spec=pltpu.PrefetchScalarGridSpec(
            num_scalar_prefetch=1,
            grid=(cuts,),
            in_specs=[whole(), weight_spec],
            out_specs=(whole(),) * cuts,
        ),
        compiler_params=params(),
        name="project",
    )(at, attended, out_weight)
    projected = head_terms[0]
    for d in range(1, cuts):
        projected = projected + turn(head_terms[d], d).astype(F32)

    terms = lax.all_to_all(
        d_gathered.reshape(homes, per_prompt, piece), "seq", 0, 0, tiled=True
    ).reshape(homes * per_prompt, piece)
    sums = pl.pallas_call(
        combine_kernel,
        out_shape=shape(homes, piece),
        in_specs=[whole(), whole()],
        out_specs=whole(),
        compiler_params=params(),
        name="combine",
    )(home_map, terms)
    back = lax.all_to_all(sums, "seq", 0, 0, tiled=True)
    back = [back[:, t * HEAD_WIDTH : (t + 1) * HEAD_WIDTH] for t in range(2 * tokens)]
    d_prefix_keys = jnp.concatenate(back[:tokens], axis=0)
    d_prefix_values = jnp.concatenate(back[tokens:], axis=0)
    return (
        projected.astype(BF16),
        d_queries,
        d_suffix_keys,
        d_suffix_values,
        d_prefix_keys,
        d_prefix_values,
    )


def solution(mesh):
    split = P("seq", "tensor")
    in_specs = (split,) * 5 + (P("seq"),) * 3 + (P("tensor", None), split)
    return jax.shard_map(
        shards, mesh=mesh, in_specs=in_specs, out_specs=(split,) * 6, check_vma=False
    )
```

time: 507 us -> 115 us (0.23)
  waiting for transfers between devices: 387 us -> 23.5 us
  starting transfers between devices: 0.38 us -> 29.7 us
  matrix products: 24.3 us -> 0 us
  Pallas kernels: 0 us -> 22.9 us
  local copies, waits for them, and re-layouts: 22.3 us -> 7.32 us
  other arithmetic: 18 us -> 4.53 us
  between operations: 16 us -> 2.7 us
  blocking collectives: 34.6 us -> 23.5 us
    reduce_scatter x3 -> x0, waiting for transfers between devices: 274 us -> none  [the longest x1 145 us: shards(): lax.psum_scatter(dv_term, 'seq', scatter_dimension=0, tiled=True)]
    all_gather x2 -> x0, waiting for transfers between devices: 111 us -> none  [the longest x1 72.2 us: shards(): lax.all_gather(blockwise_prefix_values, 'seq', axis=0, tiled=True)]
    dot_general x14 -> x0, matrix products: 24.3 us -> none  [the longest x1 4.46 us: shards(): jnp.dot(attended.reshape(row_count, queries.shape[1]), out_weight, prefer...]
    all_to_all x0 -> x1, blocking collectives: none -> 23.5 us  [shards(): pieces = lax.all_to_all(sent, 'seq', 0, 0, tiled=True)]
    pallas_call x0 -> x5, Pallas kernels: none -> 22.9 us  [the longest x1 8.35 us: shards(): pl.pallas_call(functools.partial(attention_kernel, scale=HEAD_WIDTH ** (-...]
    unnamed x1 -> x0, blocking collectives: 21.4 us -> none
    all_to_all x0 -> x3, starting transfers between devices: none -> 20.9 us  [the longest x1 10.7 us: shards(): lax.all_to_all(d_gathered.reshape(homes, per_prompt, piece), 'seq', 0, 0,...]
    all_to_all x0 -> x3, waiting for transfers between devices: none -> 17.5 us  [the longest x1 8.34 us: shards(): back = lax.all_to_all(sums, 'seq', 0, 0, tiled=True)]
  transfers between devices with their start and end apart: 5 -> 9, of which waited for: 4 -> 6; matrix products, arithmetic and copies ran while one was open for 10% -> 3% of each run, Pallas kernels for 0% -> 11%
where the time goes in v1:
time: 115 us; the launch traced here: 114 us
  starting transfers between devices  29.7 us (26%)
  blocking collectives  23.5 us (20%)
  waiting for transfers between devices  23.5 us (20%)
  Pallas kernels  22.9 us (20%)
  local copies, waits for them, and re-layouts  7.32 us (6%)
  other arithmetic  4.53 us (4%)
  between operations  2.7 us (2%)
    all_to_all x1, blocking collectives, shards(): pieces = lax.all_to_all(sent, 'seq', 0, 0, tiled=True)  23.5 us
    all_to_all x1, starting transfers between devices, shards(): lax.all_to_all(d_gathered.reshape(homes, per_prompt, piece), 'seq', 0, 0,...  10.7 us
    ppermute x6, starting transfers between devices, shards(): lax.ppermute(x, 'tensor', [(i, (i + d) % cuts) for i in range(cuts)])  8.81 us
    pallas_call x1, Pallas kernels, shards(): pl.pallas_call(functools.partial(attention_kernel, scale=HEAD_WIDTH ** (-...  8.35 us
    all_to_all x1, waiting for transfers between devices, shards(): back = lax.all_to_all(sums, 'seq', 0, 0, tiled=True)  8.34 us
    all_to_all x1, waiting for transfers between devices, shards(): lax.all_to_all(d_gathered.reshape(homes, per_prompt, piece), 'seq', 0, 0,...  8.29 us
    unnamed x20, local copies, waits for them, and re-layouts  6.79 us
    ppermute x6, waiting for transfers between devices, shards(): lax.ppermute(x, 'tensor', [(i, (i + d) % cuts) for i in range(cuts)])  5.96 us
  transfers between devices with their start and end apart: 9, of which 6 were waited for; matrix products, arithmetic and copies ran while one was open for 3% of the time, Pallas kernels for 11%

profile of v1, /device:TPU:1, one launch (start us, length us, event | category | flops | bytes accessed | tf_op | source)
XLA Modules:
  0.0 114.1 jit_solution(13518407901175477469)
XLA Ops:
  1.9 0.7 slice_dynamic-update-slice_fusion.3
  2.7 0.7 slice_dynamic-update-slice_fusion.2
  3.4 0.7 slice_dynamic-update-slice_fusion.1
  4.1 0.7 slice_dynamic-update-slice_fusion
  4.9 0.5 broadcast.7
  5.4 0.7 reduce
  6.0 0.1 reshape.36
  6.2 23.5 %all_to_all.33 = bf16[64,2,320]{2,1,0:T(2,128)(2,1)S(1)} all-to-all(bf16[64,2,320]{2,1,0:T(2,128)(2,1)S(1)} %reshape.36), channel_id=1, replica_groups=mesh['seq'=64,'tensor'=4] {'seq'}, dimensions={0} | all-to-all | bytes 163840 | tf_op jit(solution)/shard_map/all_to_all | solution.py:203
  29.7 0.2 reshape.37
  29.9 0.6 copy.23
  30.5 2.4 %select.1 = (bf16[512,512]{1,0:T(8,128)(2,1)}, bf16[64,512]{1,0:T(8,128)(2,1)}) custom-call(bf16[64,640]{1,0:T(8,128)(2,1)} %bitcast.21), custom_call_target="tpu_custom_call" | custom-call | tf_op jit(solution)/shard_map/select/pallas_call | solution.py:204
  32.9 4.5 %all-to-all-start.1 = ((bf16[64,8,512]{2,1,0:T(8,128)(2,1)}), bf16[64,8,512]{2,1,0:T(8,128)(2,1)S(1)}, u32[]{:S(2)}, u32[]{:S(2)}) async-start(bf16[64,8,512]{2,1,0:T(8,128)(2,1)} %bitcast.19), calls=%async_computation.1 | async-start | bytes 1048576 | tf_op jit(solution)/shard_map/all_to_all | solution.py:212
  37.3 2.8 %collective-permute-start.1 = (bf16[128,640]{1,0:T(8,128)(2,1)}, bf16[128,640]{1,0:T(8,128)(2,1)S(1)}, u32[]{:S(2)}, u32[]{:S(2)}) collective-permute-start(bf16[128,640]{1,0:T(8,128)(2,1)} %g0.1), channel_id=1, source_target_pairs={{0,2},{1,3},{2,0},{3,1},{4,6},{5,7},{6,4},{7,5},{8,10},{9,11},{10,... | collective-permute-start | bytes 491528 | tf_op jit(solution)/shard_map/ppermute | solution.py:216
  40.2 0.9 collective-permute-start
  41.0 0.6 collective-permute-start.2
  42.3 2.0 %collective-permute-done.1.g2 = bf16[128,640]{1,0:T(8,128)(2,1)S(1)} collective-permute-done((bf16[128,640]{1,0:T(8,128)(2,1)}, bf16[128,640]{1,0:T(8,128)(2,1)S(1)}, u32[]{:S(2)}, u32[]{:S(2)}) %collective-permute-start.1) | collective-permute-done | bytes 163872 | tf_op jit(solution)/shard_map/ppermute | solution.py:216
  44.3 0.0 copy-start.2
  44.3 3.6 %collective-permute-done.g1 = bf16[128,640]{1,0:T(8,128)(2,1)S(1)} collective-permute-done((bf16[128,640]{1,0:T(8,128)(2,1)}, bf16[128,640]{1,0:T(8,128)(2,1)S(1)}, u32[]{:S(2)}, u32[]{:S(2)}) %collective-permute-start) | collective-permute-done | bytes 163872 | tf_op jit(solution)/shard_map/ppermute | solution.py:216
  47.9 0.0 copy-start.3
  47.9 0.3 collective-permute-done.2.g3
  48.2 0.0 copy-start.4
  48.2 0.0 copy-done.2
  48.2 0.4 copy-done.3
  48.6 0.3 copy-done.4
  48.9 5.4 %grad_rows.1 = (bf16[128,1024]{1,0:T(8,128)(2,1)}, bf16[1024,128]{1,0:T(8,128)(2,1)}) custom-call(s32[1]{0:T(128)} %bitcast.at_ref, s32[1]{0:T(128)S(6)} %copy.33.len_ref, bf16[128,640]{1,0:T(8,128)(2,1)} %g0.1, bf16[128,640]{1,0:T(8,128)(2,1)} %copy-done.3, bf16[128,640]{1,0:T(8,128)(2,1)} %copy-done.2, bf16[128,640]{1,0:T(8,128)(2,1)} %copy-done.4, ...), custom_call_target="tpu_custom_call" | custom-call | tf_op jit(solution)/shard_map/grad_rows/pallas_call | solution.py:221
  54.3 0.9 all-to-all-done.1
  55.2 0.0 copy-start
  55.2 0.8 copy-done
  56.0 8.4 %attention.1 = (bf16[128,1024]{1,0:T(8,128)(2,1)}, bf16[128,1024]{1,0:T(8,128)(2,1)}, bf16[128,128]{1,0:T(8,128)(2,1)}, bf16[128,128]{1,0:T(8,128)(2,1)}, bf16[512,512]{1,0:T(8,128)(2,1)}) custom-call(s32[1]{0:T(128)S(6)} %copy.33.len_ref, bf16[128,1024]{1,0:T(8,128)(2,1)} %q_ref.1, bf16[128,128]{1,0:T(8,128)(2,1)} %ks_ref.1, bf16[128,128]{1,0:T(8,128)(2,1)} %vs_ref.1, ...), custom_call_target="tpu_custom_call" | custom-call | tf_op jit(solution)/shard_map/attention/pallas_call | solution.py:236
  64.3 10.7 %all-to-all-start.2 = ((bf16[64,8,512]{2,1,0:T(8,128)(2,1)}), bf16[64,8,512]{2,1,0:T(8,128)(2,1)S(1)}, u32[]{:S(2)}, u32[]{:S(2)}) async-start(bf16[64,8,512]{2,1,0:T(8,128)(2,1)} %bitcast.20), calls=%async_computation.2 | async-start | bytes 1048576 | tf_op jit(solution)/shard_map/all_to_all | solution.py:273
  75.0 4.9 %project.1 = (f32[128,640]{1,0:T(8,128)}, bf16[128,640]{1,0:T(8,128)(2,1)}, bf16[128,640]{1,0:T(8,128)(2,1)}, bf16[128,640]{1,0:T(8,128)(2,1)}) custom-call(s32[1]{0:T(128)} %bitcast.at_ref, bf16[128,1024]{1,0:T(8,128)(2,1)} %get-tuple-element.22.a_ref, bf16[1024,2560]{1,0:T(8,128)(2,1)} %w_ref.3), custom_call_target="tpu_custom_call" | custom-call | tf_op jit(solution)/shard_map/project/pallas_call | solution.py:257
  79.9 1.0 collective-permute-start.3
  80.9 2.5 %collective-permute-start.4 = (bf16[128,640]{1,0:T(8,128)(2,1)}, bf16[128,640]{1,0:T(8,128)(2,1)S(1)}, u32[]{:S(2)}, u32[]{:S(2)}) collective-permute-start(bf16[128,640]{1,0:T(8,128)(2,1)} %get-tuple-element.25), channel_id=1, source_target_pairs={{0,2},{1,3},{2,0},{3,1},{4,6},{5,7},{6,4},{7,5},{8,10},{9,11},{10,... | collective-permute-start | bytes 491528 | tf_op jit(solution)/shard_map/ppermute | solution.py:216
  83.3 1.1 collective-permute-start.5
  84.4 8.3 %all-to-all-done.2 = bf16[64,8,512]{2,1,0:T(8,128)(2,1)S(1)} async-done(((bf16[64,8,512]{2,1,0:T(8,128)(2,1)}), bf16[64,8,512]{2,1,0:T(8,128)(2,1)S(1)}, u32[]{:S(2)}, u32[]{:S(2)}) %all-to-all-start.2) | async-done | bytes 524320 | tf_op jit(solution)/shard_map/all_to_all | solution.py:273
  92.7 0.0 copy-start.1
  92.7 0.8 copy-done.1
  93.5 1.9 %combine.1 = bf16[64,512]{1,0:T(8,128)(2,1)} custom-call(bf16[64,512]{1,0:T(8,128)(2,1)} %get-tuple-element.30.map_ref, bf16[512,512]{1,0:T(8,128)(2,1)} %bitcast.18), custom_call_target="tpu_custom_call" | custom-call | tf_op jit(solution)/shard_map/combine/pallas_call | solution.py:276
  95.4 1.5 %reduce.1 = bf16[64,512]{1,0:T(8,128)(2,1)S(1)} reduce(bf16[64,1,512]{2,0,1:T(8,128)(2,1)} %bitcast.23, bf16[]{:T(256)} %broadcast.7), dimensions={1}, to_apply=%copy.18.reduce_sub_computation | reduce | bytes 131074 | tf_op jit(solution)/shard_map/all_to_all | solution.py:284
  96.9 0.6 reshape.38
  97.5 5.7 %all-to-all-start.3 = ((bf16[64,2,256]{2,1,0:T(2,128)(2,1)}), bf16[64,2,256]{2,1,0:T(2,128)(2,1)S(1)}, u32[]{:S(2)}, u32[]{:S(2)}) async-start(bf16[64,2,256]{2,1,0:T(2,128)(2,1)} %reshape.38), calls=%async_computation.3 | async-start | bytes 131072 | tf_op jit(solution)/shard_map/all_to_all | solution.py:284
  103.3 0.0 collective-permute-done.3
  103.3 0.0 collective-permute-done.4
  103.3 0.0 collective-permute-done.5
  103.3 1.7 %add_convert_fusion = bf16[128,640]{1,0:T(8,128)(2,1)} fusion(bf16[128,640]{1,0:T(8,128)(2,1)S(1)} %collective-permute-done.5, bf16[128,640]{1,0:T(8,128)(2,1)S(1)} %collective-permute-done.4, f32[128,640]{1,0:T(8,128)} %get-tuple-element.23, bf16[128,640]{1,0:T(8,128)(2,1)S(1)} %collective-permute-done.3), kind=kLoop, calls=%fused_computation | loop fusion | flops 573440 | bytes 983040 | tf_op jit(solution)/shard_map/convert_element_type | solution.py:289
  105.0 8.3 %all-to-all-done.3 = bf16[64,2,256]{2,1,0:T(2,128)(2,1)S(1)} async-done(((bf16[64,2,256]{2,1,0:T(2,128)(2,1)}), bf16[64,2,256]{2,1,0:T(2,128)(2,1)S(1)}, u32[]{:S(2)}, u32[]{:S(2)}) %all-to-all-start.3) | async-done | bytes 65568 | tf_op jit(solution)/shard_map/all_to_all | solution.py:284
  113.4 0.1 reshape.39
  113.5 0.6 pad_maximum_fusion
  (5 shorter events, 0.0 us)
Async XLA Ops:
  32.9 22.3 %all-to-all-start.1 = ((bf16[64,8,512]{2,1,0:T(8,128)(2,1)}), bf16[64,8,512]{2,1,0:T(8,128)(2,1)S(1)}, u32[]{:S(2)}, u32[]{:S(2)}) async-start(bf16[64,8,512]{2,1,0:T(8,128)(2,1)} %bitcast.19), calls=%async_computation.1 | async-start | bytes 1048576 | tf_op jit(solution)/shard_map/all_to_all | solution.py:212
  37.3 7.0 %collective-permute-start.1 = (bf16[128,640]{1,0:T(8,128)(2,1)}, bf16[128,640]{1,0:T(8,128)(2,1)S(1)}, u32[]{:S(2)}, u32[]{:S(2)}) collective-permute-start(bf16[128,640]{1,0:T(8,128)(2,1)} %g0.1), channel_id=1, source_target_pairs={{0,2},{1,3},{2,0},{3,1},{4,6},{5,7},{6,4},{7,5},{8,10},{9,11},{10,... | collective-permute-start | bytes 491528 | tf_op jit(solution)/shard_map/ppermute | solution.py:216
  40.2 7.8 %collective-permute-start = (bf16[128,640]{1,0:T(8,128)(2,1)}, bf16[128,640]{1,0:T(8,128)(2,1)S(1)}, u32[]{:S(2)}, u32[]{:S(2)}) collective-permute-start(bf16[128,640]{1,0:T(8,128)(2,1)} %g0.1), channel_id=1, source_target_pairs={{0,3},{1,0},{2,1},{3,2},{4,7},{5,4},{6,5},{7,6},{8,11},{9,8},{10,9... | collective-permute-start | bytes 491528 | tf_op jit(solution)/shard_map/ppermute | solution.py:216
  41.0 7.2 %collective-permute-start.2 = (bf16[128,640]{1,0:T(8,128)(2,1)}, bf16[128,640]{1,0:T(8,128)(2,1)S(1)}, u32[]{:S(2)}, u32[]{:S(2)}) collective-permute-start(bf16[128,640]{1,0:T(8,128)(2,1)} %g0.1), channel_id=1, source_target_pairs={{0,1},{1,2},{2,3},{3,0},{4,5},{5,6},{6,7},{7,4},{8,9},{9,10},{10,1... | collective-permute-start | bytes 491528 | tf_op jit(solution)/shard_map/ppermute | solution.py:216
  44.3 3.9 %copy-start.2 = (bf16[128,640]{1,0:T(8,128)(2,1)}, bf16[128,640]{1,0:T(8,128)(2,1)S(1)}, u32[]{:S(2)}) copy-start(bf16[128,640]{1,0:T(8,128)(2,1)S(1)} %collective-permute-done.1.g2) | copy-start | bytes 491524
  47.9 0.7 copy-start.3
  48.2 0.7 copy-start.4
  55.2 0.8 copy-start
  64.3 28.4 %all-to-all-start.2 = ((bf16[64,8,512]{2,1,0:T(8,128)(2,1)}), bf16[64,8,512]{2,1,0:T(8,128)(2,1)S(1)}, u32[]{:S(2)}, u32[]{:S(2)}) async-start(bf16[64,8,512]{2,1,0:T(8,128)(2,1)} %bitcast.20), calls=%async_computation.2 | async-start | bytes 1048576 | tf_op jit(solution)/shard_map/all_to_all | solution.py:273
  79.9 23.4 %collective-permute-start.3 = (bf16[128,640]{1,0:T(8,128)(2,1)}, bf16[128,640]{1,0:T(8,128)(2,1)S(1)}, u32[]{:S(2)}, u32[]{:S(2)}) collective-permute-start(bf16[128,640]{1,0:T(8,128)(2,1)} %get-tuple-element.24), channel_id=1, source_target_pairs={{0,1},{1,2},{2,3},{3,0},{4,5},{5,6},{6,7},{7,4},{8,9},{9,10},{10,1... | collective-permute-start | bytes 491528 | tf_op jit(solution)/shard_map/ppermute | solution.py:216
  80.9 22.4 %collective-permute-start.4 = (bf16[128,640]{1,0:T(8,128)(2,1)}, bf16[128,640]{1,0:T(8,128)(2,1)S(1)}, u32[]{:S(2)}, u32[]{:S(2)}) collective-permute-start(bf16[128,640]{1,0:T(8,128)(2,1)} %get-tuple-element.25), channel_id=1, source_target_pairs={{0,2},{1,3},{2,0},{3,1},{4,6},{5,7},{6,4},{7,5},{8,10},{9,11},{10,... | collective-permute-start | bytes 491528 | tf_op jit(solution)/shard_map/ppermute | solution.py:216
  83.3 20.0 %collective-permute-start.5 = (bf16[128,640]{1,0:T(8,128)(2,1)}, bf16[128,640]{1,0:T(8,128)(2,1)S(1)}, u32[]{:S(2)}, u32[]{:S(2)}) collective-permute-start(bf16[128,640]{1,0:T(8,128)(2,1)} %get-tuple-element.26), channel_id=1, source_target_pairs={{0,3},{1,0},{2,1},{3,2},{4,7},{5,4},{6,5},{7,6},{8,11},{9,8},{10,9... | collective-permute-start | bytes 491528 | tf_op jit(solution)/shard_map/ppermute | solution.py:216
  92.7 0.8 copy-start.1
  97.5 15.8 %all-to-all-start.3 = ((bf16[64,2,256]{2,1,0:T(2,128)(2,1)}), bf16[64,2,256]{2,1,0:T(2,128)(2,1)S(1)}, u32[]{:S(2)}, u32[]{:S(2)}) async-start(bf16[64,2,256]{2,1,0:T(2,128)(2,1)} %reshape.38), calls=%async_computation.3 | async-start | bytes 131072 | tf_op jit(solution)/shard_map/all_to_all | solution.py:284

commit v2 on v1

v2 whole, which is shorter than its diff:
```python
import functools

import jax
import jax.numpy as jnp
from jax import lax
from jax.experimental import pallas as pl
from jax.experimental.pallas import tpu as pltpu
from jax.sharding import PartitionSpec as P

HEAD_WIDTH = 128
PROMPTS = 8
F32 = jnp.float32
BF16 = jnp.bfloat16
NT = (((1,), (1,)), ((), ()))


def dot(a, b):
    return jnp.dot(a, b, preferred_element_type=F32)


def dot_nt(a, b):
    return lax.dot_general(a, b, NT, preferred_element_type=F32)


def iota(shape, dim):
    return lax.broadcasted_iota(jnp.int32, shape, dim)


def one_hot(left, right):
    return (left == right).astype(BF16)


def fiota(shape, dim):
    return iota(shape, dim).astype(F32)


def pack_kernel(block_ref, rollout_ref, keys_ref, values_ref, sent_ref, *, rows):
    total, tall = keys_ref.shape[0], sent_ref.shape[0]
    group = rows + 2
    row, col = iota((tall, total), 0), iota((tall, total), 1)
    place = row % group
    source = jnp.where(place < rows, (row // group) * rows + place, -1)
    packed = dot(one_hot(source, col), keys_ref[...])
    packed = packed + dot(one_hot(source - total, col), values_ref[...])
    row, lane = iota(packed.shape, 0), iota(packed.shape, 1)
    names = jnp.where(lane == 0, block_ref[0], jnp.where(lane == 1, rollout_ref[0], 0))
    packed = jnp.where(row % group == rows, names.astype(F32), packed)
    sent_ref[...] = packed.astype(BF16)


def block_codes(pieces, *, blocks, per_prompt, group):
    tall = pieces.shape[0]
    take = one_hot(iota((blocks, tall), 0) * group + group - 2, iota((blocks, tall), 1))
    meta = dot(take, pieces)
    block_prompt, rollout_prompt = meta[:, 0:1], meta[:, 1:2]
    named = one_hot(block_prompt, fiota((blocks, 128), 1))
    same = dot_nt(named, named)
    row, col = iota((blocks, blocks), 0), iota((blocks, blocks), 1)
    rank = jnp.sum(jnp.where(col < row, same, 0.0), axis=1, keepdims=True)
    return block_prompt * per_prompt + rank, rollout_prompt, meta


def select_kernel(pieces_ref, picked_ref, *, blocks, per_prompt, rows):
    group = rows + 2
    pieces = pieces_ref[...]
    code, _, meta = block_codes(pieces, blocks=blocks, per_prompt=per_prompt, group=group)
    tall, wants = pieces.shape[0], picked_ref.shape[0]
    span = per_prompt * rows
    spread = iota((blocks, tall), 1) // group == iota((blocks, tall), 0)
    have = jnp.sum(jnp.where(spread, code, 0.0), axis=0, keepdims=True) * rows
    place = iota((1, tall), 1) % group
    have = jnp.where(place < rows, have + place.astype(F32), -1.0)
    expand = one_hot(iota((wants, blocks), 0) // span, iota((wants, blocks), 1))
    want = dot(expand, meta.astype(BF16))[:, 1:2] * span
    want = want + (iota((wants, 1), 0) % span).astype(F32)
    picked_ref[...] = dot(one_hot(want, have), pieces).astype(BF16)


def map_kernel(pieces_ref, map_ref, *, blocks, per_prompt, rows):
    code, rollout, _ = block_codes(
        pieces_ref[...], blocks=blocks, per_prompt=per_prompt, group=rows + 2
    )
    tall, wants = map_ref.shape
    span = per_prompt * rows
    row, col = iota((tall, blocks), 0), iota((tall, blocks), 1)
    eye = iota((blocks, blocks), 0) == iota((blocks, blocks), 1)
    code_row = jnp.sum(jnp.where(eye, code, 0.0), axis=0, keepdims=True)
    have = jnp.sum(jnp.where(row // rows == col, code_row, 0.0), axis=1, keepdims=True) * rows
    have = have + (iota((tall, 1), 0) % rows).astype(F32)
    spread = iota((blocks, wants), 1) // span == iota((blocks, wants), 0)
    want = jnp.sum(jnp.where(spread, rollout, 0.0), axis=0, keepdims=True) * span
    want = want + (iota((1, wants), 1) % span).astype(F32)
    map_ref[...] = one_hot(have, want)


def combine_kernel(map_ref, terms_ref, out_ref):
    out_ref[...] = dot(map_ref[...], terms_ref[...]).astype(BF16)


def turned(at_ref, d, cuts, width):
    return pl.ds(pl.multiple_of(lax.rem(at_ref[0] + d, cuts) * width, width), width)


def grad_rows_kernel(at_ref, len_ref, *refs):
    *g_refs, w_ref, rows_ref, cols_ref = refs
    cuts, width = len(g_refs), g_refs[0].shape[1]
    total = None
    for d, g in enumerate(g_refs):
        term = dot_nt(w_ref[:, turned(at_ref, d, cuts, width)], g[...])
        total = term if total is None else total + term
    live = iota(total.shape, 1) < len_ref[0]
    total = jnp.where(live, total, 0.0)
    cols_ref[...] = total.astype(BF16)
    for h in range(total.shape[0] // HEAD_WIDTH):
        part = slice(h * HEAD_WIDTH, (h + 1) * HEAD_WIDTH)
        rows_ref[:, part] = total[part].T.astype(BF16)


def project_kernel(at_ref, a_ref, w_ref, *out_refs):
    cuts, width = len(out_refs), out_refs[0].shape[1]
    for d, o in enumerate(out_refs):
        o[...] = dot(a_ref[...], w_ref[:, turned(at_ref, d, cuts, width)]).astype(o.dtype)


def attention_kernel(
    len_ref,
    q_ref,
    ks_ref,
    vs_ref,
    g_ref,
    da_ref,
    dat_ref,
    att_ref,
    dq_ref,
    dks_ref,
    dvs_ref,
    dg_ref,
    k_all,
    v_all,
    dk_acc,
    dv_acc,
    *,
    scale,
):
    n = len_ref[0]
    half = g_ref.shape[0] // 2
    prefix = half * g_ref.shape[1]
    suffix = ks_ref.shape[0]
    k_all[:prefix, :] = g_ref[:half].reshape(prefix, HEAD_WIDTH)
    v_all[:prefix, :] = g_ref[half:].reshape(prefix, HEAD_WIDTH)
    k_all[prefix:, :] = ks_ref[...]
    v_all[prefix:, :] = vs_ref[...]
    k_t = k_all[...].T
    v_t = v_all[...].T
    heads = q_ref.shape[1] // 128
    key_at = iota((suffix, 2 * suffix), 0)
    slot_at = iota((suffix, 2 * suffix), 1) % suffix
    hidden = jnp.logical_or(key_at > slot_at, key_at >= n)
    live = iota((1, 2 * suffix), 1) % suffix < n
    to_log2 = scale * 1.4426950408889634
    for pair in range(heads // 2):
        one = slice(pair * 256, pair * 256 + 128)
        two = slice(pair * 256 + 128, pair * 256 + 256)
        q2 = jnp.concatenate([q_ref[:, one], q_ref[:, two]], axis=0)
        da2 = jnp.concatenate([da_ref[:, one], da_ref[:, two]], axis=0)
        dat2 = jnp.concatenate([dat_ref[one, :], dat_ref[two, :]], axis=1)
        s_pre = dot_nt(k_all[:prefix], q2)
        s_suf = jnp.where(hidden, -jnp.inf, dot_nt(k_all[prefix:], q2))
        peak = jnp.maximum(
            jnp.max(s_pre, axis=0, keepdims=True), jnp.max(s_suf, axis=0, keepdims=True)
        )
        w = jnp.concatenate(
            [jnp.exp2((s_pre - peak) * to_log2), jnp.exp2((s_suf - peak) * to_log2)], axis=0
        )
        inverse = 1.0 / jnp.sum(w, axis=0, keepdims=True)
        out_t = dot(v_t, w.astype(BF16)) * inverse
        out_t = jnp.where(live, out_t, 0.0).astype(BF16).astype(F32)
        att_ref[:, one] = out_t[:, :128].T.astype(BF16)
        att_ref[:, two] = out_t[:, 128:].T.astype(BF16)
        dots = jnp.sum(out_t * dat2.astype(F32), axis=0, keepdims=True)
        probs = w * inverse
        ds = (probs * (dot(v_all[...], dat2) - dots)).astype(BF16)
        dq_t = dot(k_t, ds) * scale
        dq_ref[:, one] = dq_t[:, :128].T.astype(BF16)
        dq_ref[:, two] = dq_t[:, 128:].T.astype(BF16)
        dk = dot(ds, q2)
        dv = dot(probs.astype(BF16), da2)
        if pair == 0:
            dk_acc[...] = dk
            dv_acc[...] = dv
        else:
            dk_acc[...] += dk
            dv_acc[...] += dv
    dg_ref[:half] = (dk_acc[:prefix] * scale).astype(BF16).reshape(half, -1, HEAD_WIDTH)
    dg_ref[half:] = dv_acc[:prefix].astype(BF16).reshape(half, -1, HEAD_WIDTH)
    dks_ref[...] = (dk_acc[prefix:] * scale).astype(BF16)
    dvs_ref[...] = dv_acc[prefix:].astype(BF16)


def whole(memory=pltpu.VMEM):
    return pl.BlockSpec(memory_space=memory)


def params(mib=24):
    return pltpu.CompilerParams(vmem_limit_bytes=mib * 1024 * 1024)


def shape(*dims, dtype=BF16):
    return jax.ShapeDtypeStruct(dims, dtype)


def shards(
    queries,
    suffix_keys,
    suffix_values,
    prefix_keys,
    prefix_values,
    block_prompt,
    rollout_prompt,
    suffix_length,
    out_weight,
    out_grad,
):
    homes = lax.axis_size("seq")
    cuts = lax.axis_size("tensor")
    rows, width = queries.shape
    features = out_grad.shape[1]
    per_prompt = homes // PROMPTS
    prefix_rows = prefix_keys.shape[0]
    served = 2 * prefix_rows // homes
    group = served + 2
    span = per_prompt * served
    at = lax.axis_index("tensor").astype(jnp.int32).reshape(1)

    sent = pl.pallas_call(
        functools.partial(pack_kernel, rows=served),
        out_shape=shape(homes * group, HEAD_WIDTH),
        in_specs=[whole(pltpu.SMEM)] * 2 + [whole()] * 2,
        out_specs=whole(),
        compiler_params=params(),
        name="pack",
    )(block_prompt, rollout_prompt, prefix_keys, prefix_values)
    pieces = lax.all_to_all(
        sent.reshape(homes, group // 2, 2, HEAD_WIDTH), "seq", 0, 0, tiled=True
    ).reshape(homes * group, HEAD_WIDTH)
    sizes = dict(blocks=homes, per_prompt=per_prompt, rows=served)
    picked = pl.pallas_call(
        functools.partial(select_kernel, **sizes),
        out_shape=shape(homes * span, HEAD_WIDTH),
        in_specs=[whole()],
        out_specs=whole(),
        compiler_params=params(),
        name="select",
    )(pieces)
    gathered = lax.all_to_all(
        picked.reshape(homes, span, HEAD_WIDTH), "seq", 0, 0, tiled=True
    )
    home_map = pl.pallas_call(
        functools.partial(map_kernel, **sizes),
        out_shape=shape(homes * served, homes * span),
        in_specs=[whole()],
        out_specs=whole(),
        compiler_params=params(),
        name="home_map",
    )(pieces)

    turn = lambda x, d: lax.ppermute(x, "tensor", [(i, (i + d) % cuts) for i in range(cuts)])
    grads = [out_grad] + [turn(out_grad, cuts - d) for d in range(1, cuts)]
    d_rows, d_cols = pl.pallas_call(
        grad_rows_kernel,
        out_shape=(shape(rows, width), shape(width, rows)),
        in_specs=[whole(pltpu.SMEM)] * 2 + [whole()] * (cuts + 1),
        out_specs=(whole(), whole()),
        compiler_params=params(),
        name="grad_rows",
    )(at, suffix_length, *grads, out_weight)

    keys = prefix_keys.shape[0] * per_prompt + rows
    attended, d_queries, d_suffix_keys, d_suffix_values, d_gathered = pl.pallas_call(
        functools.partial(attention_kernel, scale=HEAD_WIDTH**-0.5),
        out_shape=(
            shape(rows, width),
            shape(rows, width),
            shape(rows, HEAD_WIDTH),
            shape(rows, HEAD_WIDTH),
            shape(homes, span, HEAD_WIDTH),
        ),
        in_specs=[whole(pltpu.SMEM)] + [whole()] * 6,
        out_specs=(whole(),) * 5,
        scratch_shapes=[
            pltpu.VMEM((keys, HEAD_WIDTH), BF16),
            pltpu.VMEM((keys, HEAD_WIDTH), BF16),
            pltpu.VMEM((keys, HEAD_WIDTH), F32),
            pltpu.VMEM((keys, HEAD_WIDTH), F32),
        ],
        compiler_params=params(),
        name="attention",
    )(suffix_length, queries, suffix_keys, suffix_values, gathered, d_rows, d_cols)

    head_terms = pl.pallas_call(
        project_kernel,
        out_shape=(shape(rows, features, dtype=F32),) + (shape(rows, features),) * (cuts - 1),
        in_specs=[whole(pltpu.SMEM), whole(), whole()],
        out_specs=(whole(),) * cuts,
        compiler_params=params(),
        name="project",
    )(at, attended, out_weight)
    projected = head_terms[0]
    for d in range(1, cuts):
        projected = projected + turn(head_terms[d], d).astype(F32)

    terms = lax.all_to_all(d_gathered, "seq", 0, 0, tiled=True)
    sums = pl.pallas_call(
        combine_kernel,
        out_shape=shape(homes * served, HEAD_WIDTH),
        in_specs=[whole(), whole()],
        out_specs=whole(),
        compiler_params=params(),
        name="combine",
    )(home_map, terms.reshape(homes * span, HEAD_WIDTH))
    back = lax.all_to_all(
        sums.reshape(homes, served, HEAD_WIDTH), "seq", 0, 0, tiled=True
    ).reshape(homes * served, HEAD_WIDTH)
    d_prefix_keys, d_prefix_values = back[:prefix_rows], back[prefix_rows:]
    return (
        projected.astype(BF16),
        d_queries,
        d_suffix_keys,
        d_suffix_values,
        d_prefix_keys,
        d_prefix_values,
    )


def solution(mesh):
    split = P("seq", "tensor")
    in_specs = (split,) * 5 + (P("seq"),) * 3 + (P("tensor", None), split)
    return jax.shard_map(
        shards, mesh=mesh, in_specs=in_specs, out_specs=(split,) * 6, check_vma=False
    )
```

time: 115 us -> 104 us (0.904)
  Pallas kernels: 22.9 us -> 13.6 us
  other arithmetic: 4.53 us -> 0.74 us
  waiting for transfers between devices: 23.5 us -> 26 us
    pallas_call x1, Pallas kernels: 4.91 us -> 1.02 us  [shards(): pl.pallas_call(project_kernel, out_shape=(shape(rows, features, dtype=F32...]
    pallas_call x1, Pallas kernels: 5.38 us -> 1.64 us  [shards(): pl.pallas_call(grad_rows_kernel, out_shape=(shape(rows, width), shape(wid...]
    all_to_all x3, waiting for transfers between devices: 17.5 us -> 20 us  [the longest x1 9.31 us: shards(): lax.all_to_all(sums.reshape(homes, served, HEAD_WIDTH), 'seq', 0, 0, tile...]
    all_to_all x2 -> x0, other arithmetic: 2.16 us -> none  [the longest x1 1.5 us: shards(): back = lax.all_to_all(sums, 'seq', 0, 0, tiled=True)]
    pallas_call x1, Pallas kernels: 8.35 us -> 6.93 us  [shards(): pl.pallas_call(functools.partial(attention_kernel, scale=HEAD_WIDTH ** (-...]
    all_to_all x3, starting transfers between devices: 20.9 us -> 19.7 us  [the longest x1 9.52 us: shards(): terms = lax.all_to_all(d_gathered, 'seq', 0, 0, tiled=True)]
    unnamed x20 -> x16, local copies, waits for them, and re-layouts: 6.79 us -> 7.4 us
    pallas_call x2 -> x4, Pallas kernels: 4.26 us -> 4.02 us  [the longest x1 1.97 us: shards(): pl.pallas_call(functools.partial(select_kernel, **sizes), out_shape=shape...]
  transfers between devices with their start and end apart: 9 -> 9, of which waited for: 6 -> 6; matrix products, arithmetic and copies ran while one was open for 3% -> 1% of each run, Pallas kernels for 11% -> 4%
where the time goes in v2:
time: 104 us; the launch traced here: 103 us
  starting transfers between devices  28.6 us (28%)
  waiting for transfers between devices  26 us (25%)
  blocking collectives  23.5 us (23%)
  Pallas kernels  13.6 us (13%)
  local copies, waits for them, and re-layouts  8.05 us (8%)
  between operations  2.73 us (3%)
    all_to_all x1, blocking collectives, shards(): lax.all_to_all(sent.reshape(homes, group // 2, 2, HEAD_WIDTH), 'seq', 0,...  23.5 us
    all_to_all x1, starting transfers between devices, shards(): terms = lax.all_to_all(d_gathered, 'seq', 0, 0, tiled=True)  9.52 us
    all_to_all x1, waiting for transfers between devices, shards(): lax.all_to_all(sums.reshape(homes, served, HEAD_WIDTH), 'seq', 0, 0, tile...  9.31 us
    ppermute x6, starting transfers between devices, shards(): lax.ppermute(x, 'tensor', [(i, (i + d) % cuts) for i in range(cuts)])  8.89 us
    all_to_all x1, waiting for transfers between devices, shards(): terms = lax.all_to_all(d_gathered, 'seq', 0, 0, tiled=True)  8.83 us
    unnamed x16, local copies, waits for them, and re-layouts  7.4 us
    pallas_call x1, Pallas kernels, shards(): pl.pallas_call(functools.partial(attention_kernel, scale=HEAD_WIDTH ** (-...  6.93 us
    ppermute x6, waiting for transfers between devices, shards(): lax.ppermute(x, 'tensor', [(i, (i + d) % cuts) for i in range(cuts)])  5.96 us
  transfers between devices with their start and end apart: 9, of which 6 were waited for; matrix products, arithmetic and copies ran while one was open for 1% of the time, Pallas kernels for 4%

profile of v2, /device:TPU:1, one launch (start us, length us, event | category | flops | bytes accessed | tf_op | source)
XLA Modules:
  0.0 103.2 jit_solution(9702767591737658743)
XLA Ops:
  0.6 0.0 copy-start.2
  2.0 0.0 copy-start.4
  2.0 0.7 copy-done.4
  2.7 0.0 copy-start.5
  2.7 0.8 copy-done.5
  3.5 0.0 copy-start.6
  3.5 0.0 copy-start.7
  3.5 0.2 pack.1
  3.7 23.5 %all_to_all.20 = bf16[64,3,2,128]{3,2,1,0:T(2,128)(2,1)S(1)} all-to-all(bf16[64,3,2,128]{3,2,1,0:T(2,128)(2,1)S(1)} %bitcast.11), channel_id=1, replica_groups=mesh['seq'=64,'tensor'=4] {'seq'}, dimensions={0} | all-to-all | bytes 196608 | tf_op jit(solution)/shard_map/all_to_all | solution.py:243
  27.3 2.0 %select.1 = bf16[2048,128]{1,0:T(8,128)(2,1)} custom-call(bf16[384,128]{1,0:T(8,128)(2,1)S(1)} %bitcast.9), custom_call_target="tpu_custom_call" | custom-call | tf_op jit(solution)/shard_map/select/pallas_call | solution.py:247
  29.2 4.5 %all-to-all-start.1 = ((bf16[64,32,128]{2,1,0:T(8,128)(2,1)}), bf16[64,32,128]{2,1,0:T(8,128)(2,1)S(1)}, u32[]{:S(2)}, u32[]{:S(2)}) async-start(bf16[64,32,128]{2,1,0:T(8,128)(2,1)} %bitcast.3), calls=%async_computation.1 | async-start | bytes 1048576 | tf_op jit(solution)/shard_map/all_to_all | solution.py:255
  33.7 2.8 %collective-permute-start.1 = (bf16[128,640]{1,0:T(8,128)(2,1)}, bf16[128,640]{1,0:T(8,128)(2,1)S(1)}, u32[]{:S(2)}, u32[]{:S(2)}) collective-permute-start(bf16[128,640]{1,0:T(8,128)(2,1)} %refs_0_.1), channel_id=1, source_target_pairs={{0,2},{1,3},{2,0},{3,1},{4,6},{5,7},{6,4},{7,5},{8,10},{9,11},{10,... | collective-permute-start | bytes 491528 | tf_op jit(solution)/shard_map/ppermute | solution.py:267
  36.5 0.9 collective-permute-start
  37.4 0.6 collective-permute-start.2
  38.6 2.0 %collective-permute-done.1.refs_2_ = bf16[128,640]{1,0:T(8,128)(2,1)S(1)} collective-permute-done((bf16[128,640]{1,0:T(8,128)(2,1)}, bf16[128,640]{1,0:T(8,128)(2,1)S(1)}, u32[]{:S(2)}, u32[]{:S(2)}) %collective-permute-start.1) | collective-permute-done | bytes 163872 | tf_op jit(solution)/shard_map/ppermute | solution.py:267
  40.7 3.6 %collective-permute-done.refs_1_ = bf16[128,640]{1,0:T(8,128)(2,1)S(1)} collective-permute-done((bf16[128,640]{1,0:T(8,128)(2,1)}, bf16[128,640]{1,0:T(8,128)(2,1)S(1)}, u32[]{:S(2)}, u32[]{:S(2)}) %collective-permute-start) | collective-permute-done | bytes 163872 | tf_op jit(solution)/shard_map/ppermute | solution.py:267
  44.3 0.3 collective-permute-done.2.refs_3_
  44.6 0.0 copy-start
  44.6 2.5 %copy-done = bf16[1024,2560]{1,0:T(8,128)(2,1)S(1)} copy-done((bf16[1024,2560]{1,0:T(8,128)(2,1)S(1)}, bf16[1024,2560]{1,0:T(8,128)(2,1)}, u32[]{:S(2)}) %copy-start) | copy-done | bytes 5242904
  47.1 0.0 copy-start.3
  47.1 0.9 copy-done.3
  48.0 1.6 %grad_rows.1 = (bf16[128,1024]{1,0:T(8,128)(2,1)S(1)}, bf16[1024,128]{1,0:T(8,128)(2,1)S(1)}) custom-call(s32[1]{0:T(128)} %bitcast.at_ref, s32[1]{0:T(128)S(6)} %copy.18.len_ref, bf16[128,640]{1,0:T(8,128)(2,1)S(1)} %copy-done.3, bf16[128,640]{1,0:T(8,128)(2,1)S(1)} %collective-permute-done.refs_1_, bf16[128,640]{1,0:T(8,128)(2,1)S(1)} %collective-permute-done.1.refs_2_, ...), custom_call_target="tpu_custom_call" | custom-call | tf_op jit(solution)/shard_map/grad_rows/pallas_call | solution.py:269
  49.6 1.9 %all-to-all-done.1.g_ref = bf16[64,32,128]{2,1,0:T(8,128)(2,1)S(1)} async-done(((bf16[64,32,128]{2,1,0:T(8,128)(2,1)}), bf16[64,32,128]{2,1,0:T(8,128)(2,1)S(1)}, u32[]{:S(2)}, u32[]{:S(2)}) %all-to-all-start.1) | async-done | bytes 524320 | tf_op jit(solution)/shard_map/all_to_all | solution.py:255
  51.5 0.0 copy-done.2
  51.5 0.0 copy-done.6
  51.5 0.0 copy-done.7
  51.5 6.9 %attention.1 = (bf16[128,1024]{1,0:T(8,128)(2,1)S(1)}, bf16[128,1024]{1,0:T(8,128)(2,1)}, bf16[128,128]{1,0:T(8,128)(2,1)}, bf16[128,128]{1,0:T(8,128)(2,1)}, bf16[64,32,128]{2,1,0:T(8,128)(2,1)}) custom-call(s32[1]{0:T(128)S(6)} %copy.18.len_ref, bf16[128,1024]{1,0:T(8,128)(2,1)S(1)} %copy-done.2, bf16[128,128]{1,0:T(8,128)(2,1)S(1)} %copy-done.6, ...), custom_call_target="tpu_custom_call" | custom-call | tf_op jit(solution)/shard_map/attention/pallas_call | solution.py:279
  58.5 9.5 %all-to-all-start.2 = ((bf16[64,32,128]{2,1,0:T(8,128)(2,1)}), bf16[64,32,128]{2,1,0:T(8,128)(2,1)S(1)}, u32[]{:S(2)}, u32[]{:S(2)}) async-start(bf16[64,32,128]{2,1,0:T(8,128)(2,1)} %get-tuple-element.27), calls=%async_computation.2 | async-start | bytes 1048576 | tf_op jit(solution)/shard_map/all_to_all | solution.py:312
  68.0 0.0 copy-start.1
  68.0 2.5 %copy-done.1 = bf16[1024,2560]{1,0:T(8,128)(2,1)S(1)} copy-done((bf16[1024,2560]{1,0:T(8,128)(2,1)S(1)}, bf16[1024,2560]{1,0:T(8,128)(2,1)}, u32[]{:S(2)}) %copy-start.1) | copy-done | bytes 5242904
  70.5 1.0 project.1
  71.5 1.1 %collective-permute-start.3 = (bf16[128,640]{1,0:T(8,128)(2,1)S(1)}, bf16[128,640]{1,0:T(8,128)(2,1)S(1)}, u32[]{:S(2)}, u32[]{:S(2)}) collective-permute-start(bf16[128,640]{1,0:T(8,128)(2,1)S(1)} %get-tuple-element.21), channel_id=1, source_target_pairs={{0,1},{1,2},{2,3},{3,0},{4,5},{5,6},{6,7},{7,4},{8,9},{9,10},{10,1... | collective-permute-start | bytes 491528 | tf_op jit(solution)/shard_map/ppermute | solution.py:267
  72.6 2.4 %collective-permute-start.4 = (bf16[128,640]{1,0:T(8,128)(2,1)S(1)}, bf16[128,640]{1,0:T(8,128)(2,1)S(1)}, u32[]{:S(2)}, u32[]{:S(2)}) collective-permute-start(bf16[128,640]{1,0:T(8,128)(2,1)S(1)} %get-tuple-element.22), channel_id=1, source_target_pairs={{0,2},{1,3},{2,0},{3,1},{4,6},{5,7},{6,4},{7,5},{8,10},{9,11},{10,... | collective-permute-start | bytes 491528 | tf_op jit(solution)/shard_map/ppermute | solution.py:267
  75.0 1.1 %collective-permute-start.5 = (bf16[128,640]{1,0:T(8,128)(2,1)S(1)}, bf16[128,640]{1,0:T(8,128)(2,1)S(1)}, u32[]{:S(2)}, u32[]{:S(2)}) collective-permute-start(bf16[128,640]{1,0:T(8,128)(2,1)S(1)} %get-tuple-element.23), channel_id=1, source_target_pairs={{0,3},{1,0},{2,1},{3,2},{4,7},{5,4},{6,5},{7,6},{8,11},{9,8},{10,9... | collective-permute-start | bytes 491528 | tf_op jit(solution)/shard_map/ppermute | solution.py:267
  76.1 0.8 home_map.1.map_ref
  76.9 8.8 %all-to-all-done.2 = bf16[64,32,128]{2,1,0:T(8,128)(2,1)S(1)} async-done(((bf16[64,32,128]{2,1,0:T(8,128)(2,1)}), bf16[64,32,128]{2,1,0:T(8,128)(2,1)S(1)}, u32[]{:S(2)}, u32[]{:S(2)}) %all-to-all-start.2) | async-done | bytes 524320 | tf_op jit(solution)/shard_map/all_to_all | solution.py:312
  85.7 1.0 %combine.1 = bf16[256,128]{1,0:T(8,128)(2,1)} custom-call(bf16[256,2048]{1,0:T(8,128)(2,1)S(1)} %home_map.1.map_ref, bf16[2048,128]{1,0:T(8,128)(2,1)S(1)} %bitcast.8), custom_call_target="tpu_custom_call" | custom-call | tf_op jit(solution)/shard_map/combine/pallas_call | solution.py:313
  86.8 5.7 %all-to-all-start.3 = ((bf16[64,4,128]{2,1,0:T(4,128)(2,1)}), bf16[64,4,128]{2,1,0:T(4,128)(2,1)S(1)}, u32[]{:S(2)}, u32[]{:S(2)}) async-start(bf16[64,4,128]{2,1,0:T(4,128)(2,1)} %bitcast.5), calls=%async_computation.3 | async-start | bytes 131072 | tf_op jit(solution)/shard_map/all_to_all | solution.py:321
  92.5 0.0 collective-permute-done.3
  92.5 0.0 collective-permute-done.4
  92.5 0.0 collective-permute-done.5
  92.5 0.7 add_convert_fusion
  93.3 9.3 %all-to-all-done.3 = bf16[64,4,128]{2,1,0:T(4,128)(2,1)S(1)} async-done(((bf16[64,4,128]{2,1,0:T(4,128)(2,1)}), bf16[64,4,128]{2,1,0:T(4,128)(2,1)S(1)}, u32[]{:S(2)}, u32[]{:S(2)}) %all-to-all-start.3) | async-done | bytes 65568 | tf_op jit(solution)/shard_map/all_to_all | solution.py:321
  102.6 0.6 fusion
Async XLA Ops:
  0.6 50.9 %copy-start.2 = (bf16[128,1024]{1,0:T(8,128)(2,1)S(1)}, bf16[128,1024]{1,0:T(8,128)(2,1)}, u32[]{:S(2)}) copy-start(bf16[128,1024]{1,0:T(8,128)(2,1)} %q_ref.1) | copy-start | bytes 786436
  2.0 0.8 copy-start.4
  2.7 0.8 copy-start.5
  3.5 48.0 %copy-start.6 = (bf16[128,128]{1,0:T(8,128)(2,1)S(1)}, bf16[128,128]{1,0:T(8,128)(2,1)}, u32[]{:S(2)}) copy-start(bf16[128,128]{1,0:T(8,128)(2,1)} %ks_ref.1) | copy-start | bytes 98308
  3.5 48.0 %copy-start.7 = (bf16[128,128]{1,0:T(8,128)(2,1)S(1)}, bf16[128,128]{1,0:T(8,128)(2,1)}, u32[]{:S(2)}) copy-start(bf16[128,128]{1,0:T(8,128)(2,1)} %vs_ref.1) | copy-start | bytes 98308
  29.2 22.3 %all-to-all-start.1 = ((bf16[64,32,128]{2,1,0:T(8,128)(2,1)}), bf16[64,32,128]{2,1,0:T(8,128)(2,1)S(1)}, u32[]{:S(2)}, u32[]{:S(2)}) async-start(bf16[64,32,128]{2,1,0:T(8,128)(2,1)} %bitcast.3), calls=%async_computation.1 | async-start | bytes 1048576 | tf_op jit(solution)/shard_map/all_to_all | solution.py:255
  33.7 7.0 %collective-permute-start.1 = (bf16[128,640]{1,0:T(8,128)(2,1)}, bf16[128,640]{1,0:T(8,128)(2,1)S(1)}, u32[]{:S(2)}, u32[]{:S(2)}) collective-permute-start(bf16[128,640]{1,0:T(8,128)(2,1)} %refs_0_.1), channel_id=1, source_target_pairs={{0,2},{1,3},{2,0},{3,1},{4,6},{5,7},{6,4},{7,5},{8,10},{9,11},{10,... | collective-permute-start | bytes 491528 | tf_op jit(solution)/shard_map/ppermute | solution.py:267
  36.5 7.8 %collective-permute-start = (bf16[128,640]{1,0:T(8,128)(2,1)}, bf16[128,640]{1,0:T(8,128)(2,1)S(1)}, u32[]{:S(2)}, u32[]{:S(2)}) collective-permute-start(bf16[128,640]{1,0:T(8,128)(2,1)} %refs_0_.1), channel_id=1, source_target_pairs={{0,3},{1,0},{2,1},{3,2},{4,7},{5,4},{6,5},{7,6},{8,11},{9,8},{10,9... | collective-permute-start | bytes 491528 | tf_op jit(solution)/shard_map/ppermute | solution.py:267
  37.4 7.2 %collective-permute-start.2 = (bf16[128,640]{1,0:T(8,128)(2,1)}, bf16[128,640]{1,0:T(8,128)(2,1)S(1)}, u32[]{:S(2)}, u32[]{:S(2)}) collective-permute-start(bf16[128,640]{1,0:T(8,128)(2,1)} %refs_0_.1), channel_id=1, source_target_pairs={{0,1},{1,2},{2,3},{3,0},{4,5},{5,6},{6,7},{7,4},{8,9},{9,10},{10,1... | collective-permute-start | bytes 491528 | tf_op jit(solution)/shard_map/ppermute | solution.py:267
  44.6 2.5 %copy-start = (bf16[1024,2560]{1,0:T(8,128)(2,1)S(1)}, bf16[1024,2560]{1,0:T(8,128)(2,1)}, u32[]{:S(2)}) copy-start(bf16[1024,2560]{1,0:T(8,128)(2,1)} %w_ref.1) | copy-start | bytes 15728644
  47.1 0.9 copy-start.3
  58.5 27.2 %all-to-all-start.2 = ((bf16[64,32,128]{2,1,0:T(8,128)(2,1)}), bf16[64,32,128]{2,1,0:T(8,128)(2,1)S(1)}, u32[]{:S(2)}, u32[]{:S(2)}) async-start(bf16[64,32,128]{2,1,0:T(8,128)(2,1)} %get-tuple-element.27), calls=%async_computation.2 | async-start | bytes 1048576 | tf_op jit(solution)/shard_map/all_to_all | solution.py:312
  68.0 2.5 %copy-start.1 = (bf16[1024,2560]{1,0:T(8,128)(2,1)S(1)}, bf16[1024,2560]{1,0:T(8,128)(2,1)}, u32[]{:S(2)}) copy-start(bf16[1024,2560]{1,0:T(8,128)(2,1)} %w_ref.1) | copy-start | bytes 15728644
  71.5 21.0 %collective-permute-start.3 = (bf16[128,640]{1,0:T(8,128)(2,1)S(1)}, bf16[128,640]{1,0:T(8,128)(2,1)S(1)}, u32[]{:S(2)}, u32[]{:S(2)}) collective-permute-start(bf16[128,640]{1,0:T(8,128)(2,1)S(1)} %get-tuple-element.21), channel_id=1, source_target_pairs={{0,1},{1,2},{2,3},{3,0},{4,5},{5,6},{6,7},{7,4},{8,9},{9,10},{10,1... | collective-permute-start | bytes 491528 | tf_op jit(solution)/shard_map/ppermute | solution.py:267
  72.6 19.9 %collective-permute-start.4 = (bf16[128,640]{1,0:T(8,128)(2,1)S(1)}, bf16[128,640]{1,0:T(8,128)(2,1)S(1)}, u32[]{:S(2)}, u32[]{:S(2)}) collective-permute-start(bf16[128,640]{1,0:T(8,128)(2,1)S(1)} %get-tuple-element.22), channel_id=1, source_target_pairs={{0,2},{1,3},{2,0},{3,1},{4,6},{5,7},{6,4},{7,5},{8,10},{9,11},{10,... | collective-permute-start | bytes 491528 | tf_op jit(solution)/shard_map/ppermute | solution.py:267
  75.0 17.5 %collective-permute-start.5 = (bf16[128,640]{1,0:T(8,128)(2,1)S(1)}, bf16[128,640]{1,0:T(8,128)(2,1)S(1)}, u32[]{:S(2)}, u32[]{:S(2)}) collective-permute-start(bf16[128,640]{1,0:T(8,128)(2,1)S(1)} %get-tuple-element.23), channel_id=1, source_target_pairs={{0,3},{1,0},{2,1},{3,2},{4,7},{5,4},{6,5},{7,6},{8,11},{9,8},{10,9... | collective-permute-start | bytes 491528 | tf_op jit(solution)/shard_map/ppermute | solution.py:267
  86.8 15.8 %all-to-all-start.3 = ((bf16[64,4,128]{2,1,0:T(4,128)(2,1)}), bf16[64,4,128]{2,1,0:T(4,128)(2,1)S(1)}, u32[]{:S(2)}, u32[]{:S(2)}) async-start(bf16[64,4,128]{2,1,0:T(4,128)(2,1)} %bitcast.5), calls=%async_computation.3 | async-start | bytes 131072 | tf_op jit(solution)/shard_map/all_to_all | solution.py:321

commit v3 on v2

--- a/solution.py
+++ b/solution.py
@@ -9,6 +9,7 @@
 
 HEAD_WIDTH = 128
 PROMPTS = 8
+SERVERS = 16
 F32 = jnp.float32
 BF16 = jnp.bfloat16
 NT = (((1,), (1,)), ((), ()))
@@ -44,69 +45,107 @@
     packed = packed + dot(one_hot(source - total, col), values_ref[...])
     row, lane = iota(packed.shape, 0), iota(packed.shape, 1)
     names = jnp.where(lane == 0, block_ref[0], jnp.where(lane == 1, rollout_ref[0], 0))
-    packed = jnp.where(row % group == rows, names.astype(F32), packed)
+    packed = jnp.where(row % group >= rows, names.astype(F32), packed)
     sent_ref[...] = packed.astype(BF16)
 
 
-def block_codes(pieces, *, blocks, per_prompt, group):
-    tall = pieces.shape[0]
-    take = one_hot(iota((blocks, tall), 0) * group + group - 2, iota((blocks, tall), 1))
-    meta = dot(take, pieces)
-    block_prompt, rollout_prompt = meta[:, 0:1], meta[:, 1:2]
+def swap_pairs(tall, outer):
+    row, col = iota((tall, tall), 0), iota((tall, tall), 1)
+    pair = row // 2
+    return one_hot((pair % outer * (tall // 2 // outer) + pair // outer) * 2 + row % 2, col)
+
+
+def by_place_kernel(pieces_ref, out_ref, *, servers):
+    tall = pieces_ref.shape[0]
+    out_ref[...] = dot(swap_pairs(tall, servers), pieces_ref[...]).astype(BF16)
+
+
+def block_codes(refs, *, blocks, per_prompt, rows):
+    each = 2 * blocks // len(refs)
+    meta = jnp.concatenate([ref[rows // 2 * each : (rows // 2 + 1) * each] for ref in refs])
+    meta = dot(one_hot(iota((blocks, 2 * blocks), 0) * 2, iota((blocks, 2 * blocks), 1)), meta)
+    block_prompt = meta[:, 0:1]
     named = one_hot(block_prompt, fiota((blocks, 128), 1))
     same = dot_nt(named, named)
     row, col = iota((blocks, blocks), 0), iota((blocks, blocks), 1)
     rank = jnp.sum(jnp.where(col < row, same, 0.0), axis=1, keepdims=True)
-    return block_prompt * per_prompt + rank, rollout_prompt, meta
-
-
-def select_kernel(pieces_ref, picked_ref, *, blocks, per_prompt, rows):
-    group = rows + 2
-    pieces = pieces_ref[...]
-    code, _, meta = block_codes(pieces, blocks=blocks, per_prompt=per_prompt, group=group)
-    tall, wants = pieces.shape[0], picked_ref.shape[0]
-    span = per_prompt * rows
-    spread = iota((blocks, tall), 1) // group == iota((blocks, tall), 0)
-    have = jnp.sum(jnp.where(spread, code, 0.0), axis=0, keepdims=True) * rows
-    place = iota((1, tall), 1) % group
-    have = jnp.where(place < rows, have + place.astype(F32), -1.0)
-    expand = one_hot(iota((wants, blocks), 0) // span, iota((wants, blocks), 1))
-    want = dot(expand, meta.astype(BF16))[:, 1:2] * span
-    want = want + (iota((wants, 1), 0) % span).astype(F32)
-    picked_ref[...] = dot(one_hot(want, have), pieces).astype(BF16)
-
-
-def map_kernel(pieces_ref, map_ref, *, blocks, per_prompt, rows):
-    code, rollout, _ = block_codes(
-        pieces_ref[...], blocks=blocks, per_prompt=per_prompt, group=rows + 2
-    )
+    return block_prompt * per_prompt + rank, meta[: blocks // len(refs), 1:2]
+
+
+def select_kernel(*refs, blocks, per_prompt, rows):
+    *refs, picked_ref = refs
+    code, rollout = block_codes(refs, blocks=blocks, per_prompt=per_prompt, rows=rows)
+    servers, each = rollout.shape[0], 2 * blocks // len(refs)
+    span, wants = 2 * per_prompt, 2 * per_prompt * servers
+    spread = iota((blocks, 2 * blocks), 1) // 2 == iota((blocks, 2 * blocks), 0)
+    have = jnp.sum(jnp.where(spread, code, 0.0), axis=0, keepdims=True) * 2
+    have = have + (iota((1, 2 * blocks), 1) % 2).astype(F32)
+    want = jnp.broadcast_to(rollout.reshape(servers, 1, 1), (servers, span, 1))
+    want = want.reshape(wants, 1) * span + (iota((wants, 1), 0) % span).astype(F32)
+    choose = one_hot(want, have)
+    for p in range(rows // 2):
+        pieces = jnp.concatenate([ref[p * each : (p + 1) * each] for ref in refs])
+        picked = dot(choose, pieces).astype(BF16)
+        picked_ref[:, p * span : (p + 1) * span, :] = picked.reshape(servers, span, HEAD_WIDTH)
+
+
+def map_kernel(*refs, blocks, per_prompt, rows):
+    *refs, map_ref = refs
+    code, rollout = block_codes(refs, blocks=blocks, per_prompt=per_prompt, rows=rows)
     tall, wants = map_ref.shape
-    span = per_prompt * rows
-    row, col = iota((tall, blocks), 0), iota((tall, blocks), 1)
+    servers, span = rollout.shape[0], 2 * per_prompt
     eye = iota((blocks, blocks), 0) == iota((blocks, blocks), 1)
     code_row = jnp.sum(jnp.where(eye, code, 0.0), axis=0, keepdims=True)
-    have = jnp.sum(jnp.where(row // rows == col, code_row, 0.0), axis=1, keepdims=True) * rows
-    have = have + (iota((tall, 1), 0) % rows).astype(F32)
-    spread = iota((blocks, wants), 1) // span == iota((blocks, wants), 0)
+    mine = iota((tall, blocks), 0) // 2 == iota((tall, blocks), 1)
+    have = jnp.sum(jnp.where(mine, code_row, 0.0), axis=1, keepdims=True) * 2
+    have = have + (iota((tall, 1), 0) % 2).astype(F32)
+    spread = iota((servers, wants), 1) // span == iota((servers, wants), 0)
     want = jnp.sum(jnp.where(spread, rollout, 0.0), axis=0, keepdims=True) * span
     want = want + (iota((1, wants), 1) % span).astype(F32)
     map_ref[...] = one_hot(have, want)
 
 
-def combine_kernel(map_ref, terms_ref, out_ref):
-    out_ref[...] = dot(map_ref[...], terms_ref[...]).astype(BF16)
+def combine_kernel(map_ref, terms_ref, *out_refs):
+    servers, tall, _ = terms_ref.shape
+    wants = map_ref.shape[1]
+    span, each = wants // servers, map_ref.shape[0] // len(out_refs)
+    for p in range(tall // span):
+        terms = terms_ref[:, p * span : (p + 1) * span, :].reshape(wants, HEAD_WIDTH)
+        sums = dot(map_ref[...], terms)
+        for d, ref in enumerate(out_refs):
+            ref[p * each : (p + 1) * each, :] = sums[d * each : (d + 1) * each].astype(ref.dtype)
+
+
+def home_sum_kernel(*refs, servers):
+    *refs, out_ref = refs
+    total = refs[0][...]
+    for ref in refs[1:]:
+        total = total + ref[...].astype(F32)
+    tall = total.shape[0]
+    out_ref[...] = dot(swap_pairs(tall, tall // 2 // servers), total.astype(BF16)).astype(BF16)
 
 
 def turned(at_ref, d, cuts, width):
     return pl.ds(pl.multiple_of(lax.rem(at_ref[0] + d, cuts) * width, width), width)
 
 
+def fetch(at_ref, w_ref, held, sems):
+    cuts, _, width = held.shape
+    copies = [
+        pltpu.make_async_copy(w_ref.at[:, turned(at_ref, d, cuts, width)], held.at[d], sems.at[d])
+        for d in range(cuts)
+    ]
+    for copy in copies:
+        copy.start()
+    return copies
+
+
 def grad_rows_kernel(at_ref, len_ref, *refs):
-    *g_refs, w_ref, rows_ref, cols_ref = refs
-    cuts, width = len(g_refs), g_refs[0].shape[1]
+    *g_refs, w_ref, rows_ref, cols_ref, held, sems = refs
     total = None
-    for d, g in enumerate(g_refs):
-        term = dot_nt(w_ref[:, turned(at_ref, d, cuts, width)], g[...])
+    for d, copy in enumerate(fetch(at_ref, w_ref, held, sems)):
+        copy.wait()
+        term = dot_nt(held[d], g_refs[d][...])
         total = term if total is None else total + term
     live = iota(total.shape, 1) < len_ref[0]
     total = jnp.where(live, total, 0.0)
@@ -116,10 +155,11 @@
         rows_ref[:, part] = total[part].T.astype(BF16)
 
 
-def project_kernel(at_ref, a_ref, w_ref, *out_refs):
-    cuts, width = len(out_refs), out_refs[0].shape[1]
-    for d, o in enumerate(out_refs):
-        o[...] = dot(a_ref[...], w_ref[:, turned(at_ref, d, cuts, width)]).astype(o.dtype)
+def project_kernel(at_ref, a_ref, w_ref, *refs):
+    *out_refs, held, sems = refs
+    for d, copy in enumerate(fetch(at_ref, w_ref, held, sems)):
+        copy.wait()
+        out_refs[d][...] = dot(a_ref[...], held[d]).astype(out_refs[d].dtype)
 
 
 def attention_kernel(
@@ -227,50 +267,70 @@
     features = out_grad.shape[1]
     per_prompt = homes // PROMPTS
     prefix_rows = prefix_keys.shape[0]
-    served = 2 * prefix_rows // homes
-    group = served + 2
+    served = 2 * prefix_rows // SERVERS
+    tall = SERVERS * (served + 2)
     span = per_prompt * served
+    groups = [[g + i for i in range(SERVERS)] for g in range(0, homes, SERVERS)]
     at = lax.axis_index("tensor").astype(jnp.int32).reshape(1)
+
+    def swap(x):
+        return lax.all_to_all(x, "seq", 0, 0, tiled=True, axis_index_groups=groups)
+
+    def group_turn(x, d):
+        to = [(i, (i + d * SERVERS) % homes) for i in range(homes)]
+        return lax.ppermute(x, "seq", to)
 
     sent = pl.pallas_call(
         functools.partial(pack_kernel, rows=served),
-        out_shape=shape(homes * group, HEAD_WIDTH),
+        out_shape=shape(tall, HEAD_WIDTH),
         in_specs=[whole(pltpu.SMEM)] * 2 + [whole()] * 2,
         out_specs=whole(),
         compiler_params=params(),
         name="pack",
     )(block_prompt, rollout_prompt, prefix_keys, prefix_values)
-    pieces = lax.all_to_all(
-        sent.reshape(homes, group // 2, 2, HEAD_WIDTH), "seq", 0, 0, tiled=True
-    ).reshape(homes * group, HEAD_WIDTH)
+    pieces = swap(sent.reshape(SERVERS, served // 2 + 1, 2, HEAD_WIDTH)).reshape(tall, HEAD_WIDTH)
+    pieces = pl.pallas_call(
+        functools.partial(by_place_kernel, servers=SERVERS),
+        out_shape=shape(tall, HEAD_WIDTH),
+        in_specs=[whole()],
+        out_specs=whole(),
+        compiler_params=params(),
+        name="by_place",
+    )(pieces)
+    turns = homes // SERVERS
+    pieces = [pieces] + [group_turn(pieces, d) for d in range(1, turns)]
     sizes = dict(blocks=homes, per_prompt=per_prompt, rows=served)
     picked = pl.pallas_call(
         functools.partial(select_kernel, **sizes),
-        out_shape=shape(homes * span, HEAD_WIDTH),
-        in_specs=[whole()],
+        out_shape=shape(SERVERS, span, HEAD_WIDTH),
+        in_specs=[whole()] * turns,
         out_specs=whole(),
         compiler_params=params(),
         name="select",
-    )(pieces)
-    gathered = lax.all_to_all(
-        picked.reshape(homes, span, HEAD_WIDTH), "seq", 0, 0, tiled=True
-    )
+    )(*pieces)
+    gathered = swap(picked)
     home_map = pl.pallas_call(
         functools.partial(map_kernel, **sizes),
-        out_shape=shape(homes * served, homes * span),
-        in_specs=[whole()],
+        out_shape=shape(2 * homes, 2 * per_prompt * SERVERS),
+        in_specs=[whole()] * turns,
         out_specs=whole(),
         compiler_params=params(),
         name="home_map",
-    )(pieces)
+    )(*pieces)
 
     turn = lambda x, d: lax.ppermute(x, "tensor", [(i, (i + d) % cuts) for i in range(cuts)])
     grads = [out_grad] + [turn(out_grad, cuts - d) for d in range(1, cuts)]
+    weight = whole(pltpu.HBM)
+    held = [
+        pltpu.VMEM((cuts, width, features), BF16),
+        pltpu.SemaphoreType.DMA((cuts,)),
+    ]
     d_rows, d_cols = pl.pallas_call(
         grad_rows_kernel,
         out_shape=(shape(rows, width), shape(width, rows)),
-        in_specs=[whole(pltpu.SMEM)] * 2 + [whole()] * (cuts + 1),
+        in_specs=[whole(pltpu.SMEM)] * 2 + [whole()] * cuts + [weight],
         out_specs=(whole(), whole()),
+        scratch_shapes=held,
         compiler_params=params(),
         name="grad_rows",
     )(at, suffix_length, *grads, out_weight)
@@ -283,7 +343,7 @@
             shape(rows, width),
             shape(rows, HEAD_WIDTH),
             shape(rows, HEAD_WIDTH),
-            shape(homes, span, HEAD_WIDTH),
+            shape(SERVERS, span, HEAD_WIDTH),
         ),
         in_specs=[whole(pltpu.SMEM)] + [whole()] * 6,
         out_specs=(whole(),) * 5,
@@ -300,8 +360,9 @@
     head_terms = pl.pallas_call(
         project_kernel,
         out_shape=(shape(rows, features, dtype=F32),) + (shape(rows, features),) * (cuts - 1),
-        in_specs=[whole(pltpu.SMEM), whole(), whole()],
+        in_specs=[whole(pltpu.SMEM), whole(), weight],
         out_specs=(whole(),) * cuts,
+        scratch_shapes=held,
         compiler_params=params(),
         name="project",
     )(at, attended, out_weight)
@@ -309,18 +370,26 @@
     for d in range(1, cuts):
         projected = projected + turn(head_terms[d], d).astype(F32)
 
-    terms = lax.all_to_all(d_gathered, "seq", 0, 0, tiled=True)
+    half = SERVERS * served
     sums = pl.pallas_call(
         combine_kernel,
-        out_shape=shape(homes * served, HEAD_WIDTH),
+        out_shape=(shape(half, HEAD_WIDTH, dtype=F32),)
+        + (shape(half, HEAD_WIDTH),) * (turns - 1),
         in_specs=[whole(), whole()],
+        out_specs=(whole(),) * turns,
+        compiler_params=params(),
+        name="combine",
+    )(home_map, swap(d_gathered))
+    sums = [sums[0]] + [group_turn(sums[d], turns - d) for d in range(1, turns)]
+    home_sums = pl.pallas_call(
+        functools.partial(home_sum_kernel, servers=SERVERS),
+        out_shape=shape(half, HEAD_WIDTH),
+        in_specs=[whole()] * turns,
         out_specs=whole(),
         compiler_params=params(),
-        name="combine",
-    )(home_map, terms.reshape(homes * span, HEAD_WIDTH))
-    back = lax.all_to_all(
-        sums.reshape(homes, served, HEAD_WIDTH), "seq", 0, 0, tiled=True
-    ).reshape(homes * served, HEAD_WIDTH)
+        name="home_sum",
+    )(*sums)
+    back = swap(home_sums.reshape(SERVERS, served, HEAD_WIDTH)).reshape(half, HEAD_WIDTH)
     d_prefix_keys, d_prefix_values = back[:prefix_rows], back[prefix_rows:]
     return (
         projected.astype(BF16),

time: 104 us -> 107 us (1.029)
  starting transfers between devices: 28.6 us -> 43.5 us
  blocking collectives: 23.5 us -> 13 us
  waiting for transfers between devices: 26 us -> 22.5 us
  Pallas kernels: 13.6 us -> 15.6 us
    all_to_all x3, waiting for transfers between devices: 20 us -> 5.13 us  [swap(): return lax.all_to_all(x, 'seq', 0, 0, tiled=True, axis_index_groups=groups)]
    ppermute x0 -> x6, starting transfers between devices: none -> 13.6 us  [group_turn(): return lax.ppermute(x, 'seq', to)]
    ppermute x0 -> x6, waiting for transfers between devices: none -> 11.4 us  [group_turn(): return lax.ppermute(x, 'seq', to)]
    all_to_all x1, blocking collectives: 23.5 us -> 13 us  [swap(): return lax.all_to_all(x, 'seq', 0, 0, tiled=True, axis_index_groups=groups)]
    all_to_all x3, starting transfers between devices: 19.7 us -> 21.2 us  [swap(): return lax.all_to_all(x, 'seq', 0, 0, tiled=True, axis_index_groups=groups)]
    pallas_call x1, Pallas kernels: 1.64 us -> 2.89 us  [shards(): pl.pallas_call(grad_rows_kernel, out_shape=(shape(rows, width), shape(wid...]
  transfers between devices with their start and end apart: 9 -> 15, of which waited for: 6 -> 9; matrix products, arithmetic and copies ran while one was open for 1% -> 1% of each run, Pallas kernels for 4% -> 6%
where the time goes in v3:
time: 107 us; the launch traced here: 106 us
  starting transfers between devices  43.5 us (41%)
  waiting for transfers between devices  22.5 us (21%)
  Pallas kernels  15.6 us (15%)
  blocking collectives  13 us (12%)
  local copies, waits for them, and re-layouts  8.03 us (8%)
  between operations  2.76 us (3%)
    all_to_all x3, starting transfers between devices, swap(): return lax.all_to_all(x, 'seq', 0, 0, tiled=True, axis_index_groups=groups)  21.2 us
    ppermute x6, starting transfers between devices, group_turn(): return lax.ppermute(x, 'seq', to)  13.6 us
    all_to_all x1, blocking collectives, swap(): return lax.all_to_all(x, 'seq', 0, 0, tiled=True, axis_index_groups=groups)  13 us
    ppermute x6, waiting for transfers between devices, group_turn(): return lax.ppermute(x, 'seq', to)  11.4 us
    ppermute x6, starting transfers between devices, shards(): lax.ppermute(x, 'tensor', [(i, (i + d) % cuts) for i in range(cuts)])  8.82 us
    unnamed x16, local copies, waits for them, and re-layouts  7.4 us
    pallas_call x1, Pallas kernels, shards(): pl.pallas_call(functools.partial(attention_kernel, scale=HEAD_WIDTH ** (-...  6.97 us
    ppermute x6, waiting for transfers between devices, shards(): lax.ppermute(x, 'tensor', [(i, (i + d) % cuts) for i in range(cuts)])  5.99 us
  transfers between devices with their start and end apart: 15, of which 9 were waited for; matrix products, arithmetic and copies ran while one was open for 1% of the time, Pallas kernels for 6%

profile of v3, /device:TPU:1, one launch (start us, length us, event | category | flops | bytes accessed | tf_op | source)
XLA Modules:
  0.0 106.2 jit_solution(18433241408839948585)
XLA Ops:
  2.0 0.7 copy-done.4
  2.7 0.8 copy-done.5
  3.5 0.2 pack.1
  3.7 13.0 %all_to_all.20 = bf16[16,9,2,128]{3,2,1,0:T(2,128)(2,1)S(1)} all-to-all(bf16[16,9,2,128]{3,2,1,0:T(2,128)(2,1)S(1)} %bitcast.6), channel_id=1, replica_groups={{0,4,8,12,16,20,24,28,32,36,40,44,48,52,56,60},{64,68,72,76,80,84,88,92..., dimensions={0} | all-to-all | bytes 147456 | tf_op jit(solution)/shard_map/all_to_all | solution.py:277
  16.7 0.2 by_place.1.refs_0_
  16.9 5.2 %collective-permute-start.2 = (bf16[288,128]{1,0:T(8,128)(2,1)S(1)}, bf16[288,128]{1,0:T(8,128)(2,1)S(1)}, u32[]{:S(2)}, u32[]{:S(2)}) collective-permute-start(bf16[288,128]{1,0:T(8,128)(2,1)S(1)} %by_place.1.refs_0_), channel_id=1, source_target_pairs={{0,192},{4,196},{8,200},{12,204},{16,208},{20,212},{24,216},{28,22... | collective-permute-start | bytes 221192 | tf_op jit(solution)/shard_map/ppermute | solution.py:281
  22.1 1.2 %collective-permute-start.1 = (bf16[288,128]{1,0:T(8,128)(2,1)S(1)}, bf16[288,128]{1,0:T(8,128)(2,1)S(1)}, u32[]{:S(2)}, u32[]{:S(2)}) collective-permute-start(bf16[288,128]{1,0:T(8,128)(2,1)S(1)} %by_place.1.refs_0_), channel_id=1, source_target_pairs={{0,128},{4,132},{8,136},{12,140},{16,144},{20,148},{24,152},{28,15... | collective-permute-start | bytes 221192 | tf_op jit(solution)/shard_map/ppermute | solution.py:281
  23.3 2.1 %collective-permute-start = (bf16[288,128]{1,0:T(8,128)(2,1)S(1)}, bf16[288,128]{1,0:T(8,128)(2,1)S(1)}, u32[]{:S(2)}, u32[]{:S(2)}) collective-permute-start(bf16[288,128]{1,0:T(8,128)(2,1)S(1)} %by_place.1.refs_0_), channel_id=1, source_target_pairs={{0,64},{4,68},{8,72},{12,76},{16,80},{20,84},{24,88},{28,92},{32,9... | collective-permute-start | bytes 221192 | tf_op jit(solution)/shard_map/ppermute | solution.py:281
  25.4 0.0 collective-permute-done.2.refs_3_
  25.4 4.0 %collective-permute-done.1.refs_2_ = bf16[288,128]{1,0:T(8,128)(2,1)S(1)} collective-permute-done((bf16[288,128]{1,0:T(8,128)(2,1)S(1)}, bf16[288,128]{1,0:T(8,128)(2,1)S(1)}, u32[]{:S(2)}, u32[]{:S(2)}) %collective-permute-start.1) | collective-permute-done | bytes 73760 | tf_op jit(solution)/shard_map/ppermute | solution.py:281
  29.4 1.8 %collective-permute-done.refs_1_ = bf16[288,128]{1,0:T(8,128)(2,1)S(1)} collective-permute-done((bf16[288,128]{1,0:T(8,128)(2,1)S(1)}, bf16[288,128]{1,0:T(8,128)(2,1)S(1)}, u32[]{:S(2)}, u32[]{:S(2)}) %collective-permute-start) | collective-permute-done | bytes 73760 | tf_op jit(solution)/shard_map/ppermute | solution.py:281
  31.2 1.6 %select.1 = bf16[16,128,128]{2,1,0:T(8,128)(2,1)} custom-call(bf16[288,128]{1,0:T(8,128)(2,1)S(1)} %by_place.1.refs_0_, bf16[288,128]{1,0:T(8,128)(2,1)S(1)} %collective-permute-done.refs_1_, bf16[288,128]{1,0:T(8,128)(2,1)S(1)} %collective-permute-done.1.refs_2_, bf16[288,128]{1,0:T(8,128)(2,1)S(1)} %collective-permute-done.2.refs_3_), custom_call_target="tpu_custom_call" | custom-call | tf_op jit(solution)/shard_map/select/pallas_call | solution.py:303
  32.8 5.7 %all-to-all-start.1 = ((bf16[16,128,128]{2,1,0:T(8,128)(2,1)}), bf16[16,128,128]{2,1,0:T(8,128)(2,1)S(1)}, u32[]{:S(2)}, u32[]{:S(2)}) async-start(bf16[16,128,128]{2,1,0:T(8,128)(2,1)} %select.1), calls=%async_computation.1 | async-start | bytes 1048576 | tf_op jit(solution)/shard_map/all_to_all | solution.py:277
  38.5 2.7 %collective-permute-start.4 = (bf16[128,640]{1,0:T(8,128)(2,1)}, bf16[128,640]{1,0:T(8,128)(2,1)S(1)}, u32[]{:S(2)}, u32[]{:S(2)}) collective-permute-start(bf16[128,640]{1,0:T(8,128)(2,1)} %refs_0_.1), channel_id=1, source_target_pairs={{0,2},{1,3},{2,0},{3,1},{4,6},{5,7},{6,4},{7,5},{8,10},{9,11},{10,... | collective-permute-start | bytes 491528 | tf_op jit(solution)/shard_map/ppermute | solution.py:321
  41.2 0.9 collective-permute-start.3
  42.1 0.6 collective-permute-start.5
  43.3 2.3 %collective-permute-done.4.refs_2_ = bf16[128,640]{1,0:T(8,128)(2,1)S(1)} collective-permute-done((bf16[128,640]{1,0:T(8,128)(2,1)}, bf16[128,640]{1,0:T(8,128)(2,1)S(1)}, u32[]{:S(2)}, u32[]{:S(2)}) %collective-permute-start.4) | collective-permute-done | bytes 163872 | tf_op jit(solution)/shard_map/ppermute | solution.py:321
  45.7 3.6 %collective-permute-done.3.refs_1_ = bf16[128,640]{1,0:T(8,128)(2,1)S(1)} collective-permute-done((bf16[128,640]{1,0:T(8,128)(2,1)}, bf16[128,640]{1,0:T(8,128)(2,1)S(1)}, u32[]{:S(2)}, u32[]{:S(2)}) %collective-permute-start.3) | collective-permute-done | bytes 163872 | tf_op jit(solution)/shard_map/ppermute | solution.py:321
  49.3 0.0 collective-permute-done.5.refs_3_
  49.3 2.5 %copy-done = bf16[1024,2560]{1,0:T(8,128)(2,1)S(1)} copy-done((bf16[1024,2560]{1,0:T(8,128)(2,1)S(1)}, bf16[1024,2560]{1,0:T(8,128)(2,1)}, u32[]{:S(2)}) %copy-start) | copy-done | bytes 5242904
  51.8 0.9 copy-done.3
  52.7 2.9 %grad_rows.1 = (bf16[128,1024]{1,0:T(8,128)(2,1)S(1)}, bf16[1024,128]{1,0:T(8,128)(2,1)S(1)}) custom-call(s32[1]{0:T(128)} %bitcast.at_ref, s32[1]{0:T(128)S(6)} %copy.18.len_ref, bf16[128,640]{1,0:T(8,128)(2,1)S(1)} %copy-done.3, bf16[128,640]{1,0:T(8,128)(2,1)S(1)} %collective-permute-done.3.refs_1_, bf16[128,640]{1,0:T(8,128)(2,1)S(1)} %collective-permute-done.4.refs_2_, ...), custom_call_target="tpu_custom_call" | custom-call | tf_op jit(solution)/shard_map/grad_rows/pallas_call | solution.py:328
  55.6 0.0 all-to-all-done.1.g_ref
  55.6 0.0 copy-done.2
  55.7 7.0 %attention.1 = (bf16[128,1024]{1,0:T(8,128)(2,1)S(1)}, bf16[128,1024]{1,0:T(8,128)(2,1)}, bf16[128,128]{1,0:T(8,128)(2,1)}, bf16[128,128]{1,0:T(8,128)(2,1)}, bf16[16,128,128]{2,1,0:T(8,128)(2,1)}) custom-call(s32[1]{0:T(128)S(6)} %copy.18.len_ref, bf16[128,1024]{1,0:T(8,128)(2,1)S(1)} %copy-done.2, bf16[128,128]{1,0:T(8,128)(2,1)S(1)} %copy-done.6, ...), custom_call_target="tpu_custom_call" | custom-call | tf_op jit(solution)/shard_map/attention/pallas_call | solution.py:339
  62.6 6.7 %all-to-all-start.2 = ((bf16[16,128,128]{2,1,0:T(8,128)(2,1)}), bf16[16,128,128]{2,1,0:T(8,128)(2,1)S(1)}, u32[]{:S(2)}, u32[]{:S(2)}) async-start(bf16[16,128,128]{2,1,0:T(8,128)(2,1)} %get-tuple-element.31), calls=%async_computation.2 | async-start | bytes 1048576 | tf_op jit(solution)/shard_map/all_to_all | solution.py:277
  69.4 2.5 %copy-done.1 = bf16[1024,2560]{1,0:T(8,128)(2,1)S(1)} copy-done((bf16[1024,2560]{1,0:T(8,128)(2,1)S(1)}, bf16[1024,2560]{1,0:T(8,128)(2,1)}, u32[]{:S(2)}) %copy-start.1) | copy-done | bytes 5242904
  71.8 2.0 %project.1 = (f32[128,640]{1,0:T(8,128)S(1)}, bf16[128,640]{1,0:T(8,128)(2,1)S(1)}, bf16[128,640]{1,0:T(8,128)(2,1)S(1)}, bf16[128,640]{1,0:T(8,128)(2,1)S(1)}) custom-call(s32[1]{0:T(128)} %bitcast.at_ref, bf16[128,1024]{1,0:T(8,128)(2,1)S(1)} %get-tuple-element.23.a_ref, bf16[1024,2560]{1,0:T(8,128)(2,1)S(1)} %copy-done.1), custom_call_target="tpu_custom_call" | custom-call | tf_op jit(solution)/shard_map/project/pallas_call | solution.py:360
  73.9 1.1 %collective-permute-start.6 = (bf16[128,640]{1,0:T(8,128)(2,1)S(1)}, bf16[128,640]{1,0:T(8,128)(2,1)S(1)}, u32[]{:S(2)}, u32[]{:S(2)}) collective-permute-start(bf16[128,640]{1,0:T(8,128)(2,1)S(1)} %get-tuple-element.25), channel_id=1, source_target_pairs={{0,1},{1,2},{2,3},{3,0},{4,5},{5,6},{6,7},{7,4},{8,9},{9,10},{10,1... | collective-permute-start | bytes 491528 | tf_op jit(solution)/shard_map/ppermute | solution.py:321
  75.0 2.4 %collective-permute-start.7 = (bf16[128,640]{1,0:T(8,128)(2,1)S(1)}, bf16[128,640]{1,0:T(8,128)(2,1)S(1)}, u32[]{:S(2)}, u32[]{:S(2)}) collective-permute-start(bf16[128,640]{1,0:T(8,128)(2,1)S(1)} %get-tuple-element.26), channel_id=1, source_target_pairs={{0,2},{1,3},{2,0},{3,1},{4,6},{5,7},{6,4},{7,5},{8,10},{9,11},{10,... | collective-permute-start | bytes 491528 | tf_op jit(solution)/shard_map/ppermute | solution.py:321
  77.3 1.2 %collective-permute-start.8 = (bf16[128,640]{1,0:T(8,128)(2,1)S(1)}, bf16[128,640]{1,0:T(8,128)(2,1)S(1)}, u32[]{:S(2)}, u32[]{:S(2)}) collective-permute-start(bf16[128,640]{1,0:T(8,128)(2,1)S(1)} %get-tuple-element.27), channel_id=1, source_target_pairs={{0,3},{1,0},{2,1},{3,2},{4,7},{5,4},{6,5},{7,6},{8,11},{9,8},{10,9... | collective-permute-start | bytes 491528 | tf_op jit(solution)/shard_map/ppermute | solution.py:321
  78.5 0.6 home_map.1.map_ref
  79.1 0.1 all-to-all-done.2.terms_ref
  79.2 0.3 combine.1
  79.4 1.6 %collective-permute-start.9 = (bf16[256,128]{1,0:T(8,128)(2,1)S(1)}, bf16[256,128]{1,0:T(8,128)(2,1)S(1)}, u32[]{:S(2)}, u32[]{:S(2)}) collective-permute-start(bf16[256,128]{1,0:T(8,128)(2,1)S(1)} %get-tuple-element.33), channel_id=1, source_target_pairs={{0,192},{4,196},{8,200},{12,204},{16,208},{20,212},{24,216},{28,22... | collective-permute-start | bytes 196616 | tf_op jit(solution)/shard_map/ppermute | solution.py:281
  81.0 2.1 %collective-permute-start.10 = (bf16[256,128]{1,0:T(8,128)(2,1)S(1)}, bf16[256,128]{1,0:T(8,128)(2,1)S(1)}, u32[]{:S(2)}, u32[]{:S(2)}) collective-permute-start(bf16[256,128]{1,0:T(8,128)(2,1)S(1)} %get-tuple-element.34), channel_id=1, source_target_pairs={{0,128},{4,132},{8,136},{12,140},{16,144},{20,148},{24,152},{28,15... | collective-permute-start | bytes 196616 | tf_op jit(solution)/shard_map/ppermute | solution.py:281
  83.1 0.8 collective-permute-done.9.refs_1_
  83.8 1.5 %collective-permute-start.11 = (bf16[256,128]{1,0:T(8,128)(2,1)S(1)}, bf16[256,128]{1,0:T(8,128)(2,1)S(1)}, u32[]{:S(2)}, u32[]{:S(2)}) collective-permute-start(bf16[256,128]{1,0:T(8,128)(2,1)S(1)} %get-tuple-element.35), channel_id=1, source_target_pairs={{0,64},{4,68},{8,72},{12,76},{16,80},{20,84},{24,88},{28,92},{32,9... | collective-permute-start | bytes 196616 | tf_op jit(solution)/shard_map/ppermute | solution.py:281
  85.3 2.7 %collective-permute-done.10.refs_2_ = bf16[256,128]{1,0:T(8,128)(2,1)S(1)} collective-permute-done((bf16[256,128]{1,0:T(8,128)(2,1)S(1)}, bf16[256,128]{1,0:T(8,128)(2,1)S(1)}, u32[]{:S(2)}, u32[]{:S(2)}) %collective-permute-start.10) | collective-permute-done | bytes 65568 | tf_op jit(solution)/shard_map/ppermute | solution.py:281
  88.0 2.2 %collective-permute-done.11.refs_3_ = bf16[256,128]{1,0:T(8,128)(2,1)S(1)} collective-permute-done((bf16[256,128]{1,0:T(8,128)(2,1)S(1)}, bf16[256,128]{1,0:T(8,128)(2,1)S(1)}, u32[]{:S(2)}, u32[]{:S(2)}) %collective-permute-start.11) | collective-permute-done | bytes 65568 | tf_op jit(solution)/shard_map/ppermute | solution.py:281
  90.2 0.8 home_sum.1
  91.0 8.7 %all-to-all-start.3 = ((bf16[16,16,128]{2,1,0:T(8,128)(2,1)}), bf16[16,16,128]{2,1,0:T(8,128)(2,1)S(1)}, u32[]{:S(2)}, u32[]{:S(2)}) async-start(bf16[16,16,128]{2,1,0:T(8,128)(2,1)} %bitcast.3), calls=%async_computation.3 | async-start | bytes 131072 | tf_op jit(solution)/shard_map/all_to_all | solution.py:277
  99.8 0.0 collective-permute-done.6
  99.8 0.0 collective-permute-done.7
  99.8 0.0 collective-permute-done.8
  99.8 0.8 add_convert_fusion
  100.5 5.0 %all-to-all-done.3 = bf16[16,16,128]{2,1,0:T(8,128)(2,1)S(1)} async-done(((bf16[16,16,128]{2,1,0:T(8,128)(2,1)}), bf16[16,16,128]{2,1,0:T(8,128)(2,1)S(1)}, u32[]{:S(2)}, u32[]{:S(2)}) %all-to-all-start.3) | async-done | bytes 65568 | tf_op jit(solution)/shard_map/all_to_all | solution.py:277
  105.6 0.6 fusion
  (10 shorter events, 0.0 us)
Async XLA Ops:
  0.6 55.0 %copy-start.2 = (bf16[128,1024]{1,0:T(8,128)(2,1)S(1)}, bf16[128,1024]{1,0:T(8,128)(2,1)}, u32[]{:S(2)}) copy-start(bf16[128,1024]{1,0:T(8,128)(2,1)} %q_ref.1) | copy-start | bytes 786436
  2.0 0.8 copy-start.4
  2.7 0.8 copy-start.5
  3.5 52.2 %copy-start.6 = (bf16[128,128]{1,0:T(8,128)(2,1)S(1)}, bf16[128,128]{1,0:T(8,128)(2,1)}, u32[]{:S(2)}) copy-start(bf16[128,128]{1,0:T(8,128)(2,1)} %ks_ref.1) | copy-start | bytes 98308
  3.5 52.2 %copy-start.7 = (bf16[128,128]{1,0:T(8,128)(2,1)S(1)}, bf16[128,128]{1,0:T(8,128)(2,1)}, u32[]{:S(2)}) copy-start(bf16[128,128]{1,0:T(8,128)(2,1)} %vs_ref.1) | copy-start | bytes 98308
  16.9 8.5 %collective-permute-start.2 = (bf16[288,128]{1,0:T(8,128)(2,1)S(1)}, bf16[288,128]{1,0:T(8,128)(2,1)S(1)}, u32[]{:S(2)}, u32[]{:S(2)}) collective-permute-start(bf16[288,128]{1,0:T(8,128)(2,1)S(1)} %by_place.1.refs_0_), channel_id=1, source_target_pairs={{0,192},{4,196},{8,200},{12,204},{16,208},{20,212},{24,216},{28,22... | collective-permute-start | bytes 221192 | tf_op jit(solution)/shard_map/ppermute | solution.py:281
  22.1 7.3 %collective-permute-start.1 = (bf16[288,128]{1,0:T(8,128)(2,1)S(1)}, bf16[288,128]{1,0:T(8,128)(2,1)S(1)}, u32[]{:S(2)}, u32[]{:S(2)}) collective-permute-start(bf16[288,128]{1,0:T(8,128)(2,1)S(1)} %by_place.1.refs_0_), channel_id=1, source_target_pairs={{0,128},{4,132},{8,136},{12,140},{16,144},{20,148},{24,152},{28,15... | collective-permute-start | bytes 221192 | tf_op jit(solution)/shard_map/ppermute | solution.py:281
  23.3 7.9 %collective-permute-start = (bf16[288,128]{1,0:T(8,128)(2,1)S(1)}, bf16[288,128]{1,0:T(8,128)(2,1)S(1)}, u32[]{:S(2)}, u32[]{:S(2)}) collective-permute-start(bf16[288,128]{1,0:T(8,128)(2,1)S(1)} %by_place.1.refs_0_), channel_id=1, source_target_pairs={{0,64},{4,68},{8,72},{12,76},{16,80},{20,84},{24,88},{28,92},{32,9... | collective-permute-start | bytes 221192 | tf_op jit(solution)/shard_map/ppermute | solution.py:281
  32.8 22.8 %all-to-all-start.1 = ((bf16[16,128,128]{2,1,0:T(8,128)(2,1)}), bf16[16,128,128]{2,1,0:T(8,128)(2,1)S(1)}, u32[]{:S(2)}, u32[]{:S(2)}) async-start(bf16[16,128,128]{2,1,0:T(8,128)(2,1)} %select.1), calls=%async_computation.1 | async-start | bytes 1048576 | tf_op jit(solution)/shard_map/all_to_all | solution.py:277
  38.5 7.2 %collective-permute-start.4 = (bf16[128,640]{1,0:T(8,128)(2,1)}, bf16[128,640]{1,0:T(8,128)(2,1)S(1)}, u32[]{:S(2)}, u32[]{:S(2)}) collective-permute-start(bf16[128,640]{1,0:T(8,128)(2,1)} %refs_0_.1), channel_id=1, source_target_pairs={{0,2},{1,3},{2,0},{3,1},{4,6},{5,7},{6,4},{7,5},{8,10},{9,11},{10,... | collective-permute-start | bytes 491528 | tf_op jit(solution)/shard_map/ppermute | solution.py:321
  41.2 8.1 %collective-permute-start.3 = (bf16[128,640]{1,0:T(8,128)(2,1)}, bf16[128,640]{1,0:T(8,128)(2,1)S(1)}, u32[]{:S(2)}, u32[]{:S(2)}) collective-permute-start(bf16[128,640]{1,0:T(8,128)(2,1)} %refs_0_.1), channel_id=1, source_target_pairs={{0,3},{1,0},{2,1},{3,2},{4,7},{5,4},{6,5},{7,6},{8,11},{9,8},{10,9... | collective-permute-start | bytes 491528 | tf_op jit(solution)/shard_map/ppermute | solution.py:321
  42.1 7.2 %collective-permute-start.5 = (bf16[128,640]{1,0:T(8,128)(2,1)}, bf16[128,640]{1,0:T(8,128)(2,1)S(1)}, u32[]{:S(2)}, u32[]{:S(2)}) collective-permute-start(bf16[128,640]{1,0:T(8,128)(2,1)} %refs_0_.1), channel_id=1, source_target_pairs={{0,1},{1,2},{2,3},{3,0},{4,5},{5,6},{6,7},{7,4},{8,9},{9,10},{10,1... | collective-permute-start | bytes 491528 | tf_op jit(solution)/shard_map/ppermute | solution.py:321
  49.3 2.5 %copy-start = (bf16[1024,2560]{1,0:T(8,128)(2,1)S(1)}, bf16[1024,2560]{1,0:T(8,128)(2,1)}, u32[]{:S(2)}) copy-start(bf16[1024,2560]{1,0:T(8,128)(2,1)} %w_ref.1) | copy-start | bytes 15728644
  51.8 0.9 copy-start.3
  62.6 16.5 %all-to-all-start.2 = ((bf16[16,128,128]{2,1,0:T(8,128)(2,1)}), bf16[16,128,128]{2,1,0:T(8,128)(2,1)S(1)}, u32[]{:S(2)}, u32[]{:S(2)}) async-start(bf16[16,128,128]{2,1,0:T(8,128)(2,1)} %get-tuple-element.31), calls=%async_computation.2 | async-start | bytes 1048576 | tf_op jit(solution)/shard_map/all_to_all | solution.py:277
  69.4 2.5 %copy-start.1 = (bf16[1024,2560]{1,0:T(8,128)(2,1)S(1)}, bf16[1024,2560]{1,0:T(8,128)(2,1)}, u32[]{:S(2)}) copy-start(bf16[1024,2560]{1,0:T(8,128)(2,1)} %w_ref.1) | copy-start | bytes 15728644
  73.9 25.9 %collective-permute-start.6 = (bf16[128,640]{1,0:T(8,128)(2,1)S(1)}, bf16[128,640]{1,0:T(8,128)(2,1)S(1)}, u32[]{:S(2)}, u32[]{:S(2)}) collective-permute-start(bf16[128,640]{1,0:T(8,128)(2,1)S(1)} %get-tuple-element.25), channel_id=1, source_target_pairs={{0,1},{1,2},{2,3},{3,0},{4,5},{5,6},{6,7},{7,4},{8,9},{9,10},{10,1... | collective-permute-start | bytes 491528 | tf_op jit(solution)/shard_map/ppermute | solution.py:321
  75.0 24.8 %collective-permute-start.7 = (bf16[128,640]{1,0:T(8,128)(2,1)S(1)}, bf16[128,640]{1,0:T(8,128)(2,1)S(1)}, u32[]{:S(2)}, u32[]{:S(2)}) collective-permute-start(bf16[128,640]{1,0:T(8,128)(2,1)S(1)} %get-tuple-element.26), channel_id=1, source_target_pairs={{0,2},{1,3},{2,0},{3,1},{4,6},{5,7},{6,4},{7,5},{8,10},{9,11},{10,... | collective-permute-start | bytes 491528 | tf_op jit(solution)/shard_map/ppermute | solution.py:321
  77.3 22.4 %collective-permute-start.8 = (bf16[128,640]{1,0:T(8,128)(2,1)S(1)}, bf16[128,640]{1,0:T(8,128)(2,1)S(1)}, u32[]{:S(2)}, u32[]{:S(2)}) collective-permute-start(bf16[128,640]{1,0:T(8,128)(2,1)S(1)} %get-tuple-element.27), channel_id=1, source_target_pairs={{0,3},{1,0},{2,1},{3,2},{4,7},{5,4},{6,5},{7,6},{8,11},{9,8},{10,9... | collective-permute-start | bytes 491528 | tf_op jit(solution)/shard_map/ppermute | solution.py:321
  79.4 4.4 %collective-permute-start.9 = (bf16[256,128]{1,0:T(8,128)(2,1)S(1)}, bf16[256,128]{1,0:T(8,128)(2,1)S(1)}, u32[]{:S(2)}, u32[]{:S(2)}) collective-permute-start(bf16[256,128]{1,0:T(8,128)(2,1)S(1)} %get-tuple-element.33), channel_id=1, source_target_pairs={{0,192},{4,196},{8,200},{12,204},{16,208},{20,212},{24,216},{28,22... | collective-permute-start | bytes 196616 | tf_op jit(solution)/shard_map/ppermute | solution.py:281
  81.0 7.0 %collective-permute-start.10 = (bf16[256,128]{1,0:T(8,128)(2,1)S(1)}, bf16[256,128]{1,0:T(8,128)(2,1)S(1)}, u32[]{:S(2)}, u32[]{:S(2)}) collective-permute-start(bf16[256,128]{1,0:T(8,128)(2,1)S(1)} %get-tuple-element.34), channel_id=1, source_target_pairs={{0,128},{4,132},{8,136},{12,140},{16,144},{20,148},{24,152},{28,15... | collective-permute-start | bytes 196616 | tf_op jit(solution)/shard_map/ppermute | solution.py:281
  83.8 6.4 %collective-permute-start.11 = (bf16[256,128]{1,0:T(8,128)(2,1)S(1)}, bf16[256,128]{1,0:T(8,128)(2,1)S(1)}, u32[]{:S(2)}, u32[]{:S(2)}) collective-permute-start(bf16[256,128]{1,0:T(8,128)(2,1)S(1)} %get-tuple-element.35), channel_id=1, source_target_pairs={{0,64},{4,68},{8,72},{12,76},{16,80},{20,84},{24,88},{28,92},{32,9... | collective-permute-start | bytes 196616 | tf_op jit(solution)/shard_map/ppermute | solution.py:281
  91.0 14.6 %all-to-all-start.3 = ((bf16[16,16,128]{2,1,0:T(8,128)(2,1)}), bf16[16,16,128]{2,1,0:T(8,128)(2,1)S(1)}, u32[]{:S(2)}, u32[]{:S(2)}) async-start(bf16[16,16,128]{2,1,0:T(8,128)(2,1)} %bitcast.3), calls=%async_computation.3 | async-start | bytes 131072 | tf_op jit(solution)/shard_map/all_to_all | solution.py:277

commit v4 on v3

--- a/solution.py
+++ b/solution.py
@@ -35,8 +35,8 @@
     return iota(shape, dim).astype(F32)
 
 
-def pack_kernel(block_ref, rollout_ref, keys_ref, values_ref, sent_ref, *, rows):
-    total, tall = keys_ref.shape[0], sent_ref.shape[0]
+def pack_kernel(block_ref, rollout_ref, keys_ref, values_ref, sent_ref, *, rows, turns):
+    total, tall = keys_ref.shape[0], sent_ref.shape[0] // turns
     group = rows + 2
     row, col = iota((tall, total), 0), iota((tall, total), 1)
     place = row % group
@@ -45,8 +45,9 @@
     packed = packed + dot(one_hot(source - total, col), values_ref[...])
     row, lane = iota(packed.shape, 0), iota(packed.shape, 1)
     names = jnp.where(lane == 0, block_ref[0], jnp.where(lane == 1, rollout_ref[0], 0))
-    packed = jnp.where(row % group >= rows, names.astype(F32), packed)
-    sent_ref[...] = packed.astype(BF16)
+    packed = jnp.where(row % group >= rows, names.astype(F32), packed).astype(BF16)
+    for g in range(turns):
+        sent_ref[g * tall : (g + 1) * tall, :] = packed
 
 
 def swap_pairs(tall, outer):
@@ -55,27 +56,29 @@
     return one_hot((pair % outer * (tall // 2 // outer) + pair // outer) * 2 + row % 2, col)
 
 
-def by_place_kernel(pieces_ref, out_ref, *, servers):
-    tall = pieces_ref.shape[0]
-    out_ref[...] = dot(swap_pairs(tall, servers), pieces_ref[...]).astype(BF16)
-
-
-def block_codes(refs, *, blocks, per_prompt, rows):
-    each = 2 * blocks // len(refs)
-    meta = jnp.concatenate([ref[rows // 2 * each : (rows // 2 + 1) * each] for ref in refs])
-    meta = dot(one_hot(iota((blocks, 2 * blocks), 0) * 2, iota((blocks, 2 * blocks), 1)), meta)
-    block_prompt = meta[:, 0:1]
+def block_codes(meta, own, *, per_prompt, servers):
+    blocks = meta.shape[0]
+    block_prompt = meta[:, 0:1].astype(F32)
     named = one_hot(block_prompt, fiota((blocks, 128), 1))
     same = dot_nt(named, named)
     row, col = iota((blocks, blocks), 0), iota((blocks, blocks), 1)
     rank = jnp.sum(jnp.where(col < row, same, 0.0), axis=1, keepdims=True)
-    return block_prompt * per_prompt + rank, meta[: blocks // len(refs), 1:2]
-
-
-def select_kernel(*refs, blocks, per_prompt, rows):
-    *refs, picked_ref = refs
-    code, rollout = block_codes(refs, blocks=blocks, per_prompt=per_prompt, rows=rows)
-    servers, each = rollout.shape[0], 2 * blocks // len(refs)
+    take = one_hot(iota((servers, blocks), 0) + own * servers, iota((servers, blocks), 1))
+    return block_prompt * per_prompt + rank, dot(take, meta)[:, 1:2]
+
+
+def select_kernel(own_ref, pieces_ref, picked_ref, meta_ref, *, per_prompt, servers, rows, turns):
+    tall = servers * (rows + 2)
+    swap = swap_pairs(tall, servers)
+    pieces = [
+        dot(swap, pieces_ref[g * tall : (g + 1) * tall]).astype(BF16) for g in range(turns)
+    ]
+    each, blocks = 2 * servers, servers * turns
+    meta = jnp.concatenate([p[rows // 2 * each :] for p in pieces])
+    one_each = one_hot(iota((blocks, 2 * blocks), 0) * 2, iota((blocks, 2 * blocks), 1))
+    meta = dot(one_each, meta).astype(BF16)
+    meta_ref[...] = meta
+    code, rollout = block_codes(meta, own_ref[0], per_prompt=per_prompt, servers=servers)
     span, wants = 2 * per_prompt, 2 * per_prompt * servers
     spread = iota((blocks, 2 * blocks), 1) // 2 == iota((blocks, 2 * blocks), 0)
     have = jnp.sum(jnp.where(spread, code, 0.0), axis=0, keepdims=True) * 2
@@ -84,16 +87,18 @@
     want = want.reshape(wants, 1) * span + (iota((wants, 1), 0) % span).astype(F32)
     choose = one_hot(want, have)
     for p in range(rows // 2):
-        pieces = jnp.concatenate([ref[p * each : (p + 1) * each] for ref in refs])
-        picked = dot(choose, pieces).astype(BF16)
+        from_all = jnp.concatenate([part[p * each : (p + 1) * each] for part in pieces])
+        picked = dot(choose, from_all).astype(BF16)
         picked_ref[:, p * span : (p + 1) * span, :] = picked.reshape(servers, span, HEAD_WIDTH)
 
 
-def map_kernel(*refs, blocks, per_prompt, rows):
-    *refs, map_ref = refs
-    code, rollout = block_codes(refs, blocks=blocks, per_prompt=per_prompt, rows=rows)
+def map_kernel(own_ref, meta_ref, map_ref, *, per_prompt, servers):
+    code, rollout = block_codes(
+        meta_ref[...], own_ref[0], per_prompt=per_prompt, servers=servers
+    )
+    blocks = code.shape[0]
     tall, wants = map_ref.shape
-    servers, span = rollout.shape[0], 2 * per_prompt
+    span = 2 * per_prompt
     eye = iota((blocks, blocks), 0) == iota((blocks, blocks), 1)
     code_row = jnp.sum(jnp.where(eye, code, 0.0), axis=0, keepdims=True)
     mine = iota((tall, blocks), 0) // 2 == iota((tall, blocks), 1)
@@ -105,24 +110,26 @@
     map_ref[...] = one_hot(have, want)
 
 
-def combine_kernel(map_ref, terms_ref, *out_refs):
+def combine_kernel(map_ref, terms_ref, out_ref, *, turns):
     servers, tall, _ = terms_ref.shape
     wants = map_ref.shape[1]
-    span, each = wants // servers, map_ref.shape[0] // len(out_refs)
+    span, each = wants // servers, map_ref.shape[0] // turns
+    sums = []
     for p in range(tall // span):
         terms = terms_ref[:, p * span : (p + 1) * span, :].reshape(wants, HEAD_WIDTH)
-        sums = dot(map_ref[...], terms)
-        for d, ref in enumerate(out_refs):
-            ref[p * each : (p + 1) * each, :] = sums[d * each : (d + 1) * each].astype(ref.dtype)
-
-
-def home_sum_kernel(*refs, servers):
-    *refs, out_ref = refs
-    total = refs[0][...]
-    for ref in refs[1:]:
-        total = total + ref[...].astype(F32)
-    tall = total.shape[0]
-    out_ref[...] = dot(swap_pairs(tall, tall // 2 // servers), total.astype(BF16)).astype(BF16)
+        sums.append(dot(map_ref[...], terms).astype(BF16))
+    rows = each * len(sums)
+    swap = swap_pairs(rows, len(sums))
+    for g in range(turns):
+        part = jnp.concatenate([s[g * each : (g + 1) * each] for s in sums])
+        out_ref[g * rows : (g + 1) * rows, :] = dot(swap, part).astype(BF16)
+
+
+def home_sum_kernel(terms_ref, keys_ref, values_ref):
+    total = jnp.sum(terms_ref[...].astype(F32), axis=0)
+    half = keys_ref.shape[0]
+    keys_ref[...] = total[:half].astype(BF16)
+    values_ref[...] = total[half:].astype(BF16)
 
 
 def turned(at_ref, d, cuts, width):
@@ -276,50 +283,42 @@
     def swap(x):
         return lax.all_to_all(x, "seq", 0, 0, tiled=True, axis_index_groups=groups)
 
-    def group_turn(x, d):
-        to = [(i, (i + d * SERVERS) % homes) for i in range(homes)]
-        return lax.ppermute(x, "seq", to)
-
+    turn = lambda x, d: lax.ppermute(x, "tensor", [(i, (i + d) % cuts) for i in range(cuts)])
+    grads = [out_grad] + [turn(out_grad, cuts - d) for d in range(1, cuts)]
+    turns = homes // SERVERS
+    own = (lax.axis_index("seq") // SERVERS).astype(jnp.int32).reshape(1)
     sent = pl.pallas_call(
-        functools.partial(pack_kernel, rows=served),
-        out_shape=shape(tall, HEAD_WIDTH),
+        functools.partial(pack_kernel, rows=served, turns=turns),
+        out_shape=shape(turns * tall, HEAD_WIDTH),
         in_specs=[whole(pltpu.SMEM)] * 2 + [whole()] * 2,
         out_specs=whole(),
         compiler_params=params(),
         name="pack",
     )(block_prompt, rollout_prompt, prefix_keys, prefix_values)
-    pieces = swap(sent.reshape(SERVERS, served // 2 + 1, 2, HEAD_WIDTH)).reshape(tall, HEAD_WIDTH)
-    pieces = pl.pallas_call(
-        functools.partial(by_place_kernel, servers=SERVERS),
-        out_shape=shape(tall, HEAD_WIDTH),
-        in_specs=[whole()],
-        out_specs=whole(),
-        compiler_params=params(),
-        name="by_place",
-    )(pieces)
-    turns = homes // SERVERS
-    pieces = [pieces] + [group_turn(pieces, d) for d in range(1, turns)]
-    sizes = dict(blocks=homes, per_prompt=per_prompt, rows=served)
-    picked = pl.pallas_call(
-        functools.partial(select_kernel, **sizes),
-        out_shape=shape(SERVERS, span, HEAD_WIDTH),
-        in_specs=[whole()] * turns,
-        out_specs=whole(),
+    pieces = lax.all_to_all(
+        sent.reshape(homes, served // 2 + 1, 2, HEAD_WIDTH), "seq", 0, 0, tiled=True
+    ).reshape(turns * tall, HEAD_WIDTH)
+    pieces, grads = lax.optimization_barrier((pieces, grads))
+    picked, meta = pl.pallas_call(
+        functools.partial(
+            select_kernel, per_prompt=per_prompt, servers=SERVERS, rows=served, turns=turns
+        ),
+        out_shape=(shape(SERVERS, span, HEAD_WIDTH), shape(homes, 128)),
+        in_specs=[whole(pltpu.SMEM), whole()],
+        out_specs=(whole(), whole()),
         compiler_params=params(),
         name="select",
-    )(*pieces)
+    )(own, pieces)
     gathered = swap(picked)
     home_map = pl.pallas_call(
-        functools.partial(map_kernel, **sizes),
+        functools.partial(map_kernel, per_prompt=per_prompt, servers=SERVERS),
         out_shape=shape(2 * homes, 2 * per_prompt * SERVERS),
-        in_specs=[whole()] * turns,
+        in_specs=[whole(pltpu.SMEM), whole()],
         out_specs=whole(),
         compiler_params=params(),
         name="home_map",
-    )(*pieces)
-
-    turn = lambda x, d: lax.ppermute(x, "tensor", [(i, (i + d) % cuts) for i in range(cuts)])
-    grads = [out_grad] + [turn(out_grad, cuts - d) for d in range(1, cuts)]
+    )(own, meta)
+
     weight = whole(pltpu.HBM)
     held = [
         pltpu.VMEM((cuts, width, features), BF16),
@@ -333,7 +332,7 @@
         scratch_shapes=held,
         compiler_params=params(),
         name="grad_rows",
-    )(at, suffix_length, *grads, out_weight)
+    )(at, suffix_length, *grads, pltpu.with_memory_space_constraint(out_weight, pltpu.HBM))
 
     keys = prefix_keys.shape[0] * per_prompt + rows
     attended, d_queries, d_suffix_keys, d_suffix_values, d_gathered = pl.pallas_call(
@@ -365,32 +364,30 @@
         scratch_shapes=held,
         compiler_params=params(),
         name="project",
-    )(at, attended, out_weight)
+    )(at, attended, pltpu.with_memory_space_constraint(out_weight, pltpu.HBM))
     projected = head_terms[0]
     for d in range(1, cuts):
         projected = projected + turn(head_terms[d], d).astype(F32)
 
-    half = SERVERS * served
     sums = pl.pallas_call(
-        combine_kernel,
-        out_shape=(shape(half, HEAD_WIDTH, dtype=F32),)
-        + (shape(half, HEAD_WIDTH),) * (turns - 1),
+        functools.partial(combine_kernel, turns=turns),
+        out_shape=shape(homes * served, HEAD_WIDTH),
         in_specs=[whole(), whole()],
-        out_specs=(whole(),) * turns,
+        out_specs=whole(),
         compiler_params=params(),
         name="combine",
     )(home_map, swap(d_gathered))
-    sums = [sums[0]] + [group_turn(sums[d], turns - d) for d in range(1, turns)]
-    home_sums = pl.pallas_call(
-        functools.partial(home_sum_kernel, servers=SERVERS),
-        out_shape=shape(half, HEAD_WIDTH),
-        in_specs=[whole()] * turns,
-        out_specs=whole(),
+    back = lax.all_to_all(
+        sums.reshape(homes, served, HEAD_WIDTH), "seq", 0, 0, tiled=True
+    ).reshape(turns, 2 * prefix_rows, HEAD_WIDTH)
+    d_prefix_keys, d_prefix_values = pl.pallas_call(
+        home_sum_kernel,
+        out_shape=(shape(prefix_rows, HEAD_WIDTH),) * 2,
+        in_specs=[whole()],
+        out_specs=(whole(), whole()),
         compiler_params=params(),
         name="home_sum",
-    )(*sums)
-    back = swap(home_sums.reshape(SERVERS, served, HEAD_WIDTH)).reshape(half, HEAD_WIDTH)
-    d_prefix_keys, d_prefix_values = back[:prefix_rows], back[prefix_rows:]
+    )(back)
     return (
         projected.astype(BF16),
         d_queries,

time: 107 us -> 95.4 us (0.89)
  blocking collectives: 13 us -> 0 us
  waiting for transfers between devices: 22.5 us -> 31.5 us
  local copies, waits for them, and re-layouts: 8.03 us -> 2.43 us
  starting transfers between devices: 43.5 us -> 38 us
  Pallas kernels: 15.6 us -> 19.2 us
    all_to_all x0 -> x2, starting transfers between devices: none -> 21.2 us  [the longest x1 13.2 us: shards(): lax.all_to_all(sent.reshape(homes, served // 2 + 1, 2, HEAD_WIDTH), 'seq'...]
    ppermute x6 -> x0, starting transfers between devices: 13.6 us -> none  [group_turn(): return lax.ppermute(x, 'seq', to)]
    all_to_all x1 -> x0, blocking collectives: 13 us -> none  [swap(): return lax.all_to_all(x, 'seq', 0, 0, tiled=True, axis_index_groups=groups)]
    ppermute x6, waiting for transfers between devices: 5.99 us -> 17.9 us  [shards(): lax.ppermute(x, 'tensor', [(i, (i + d) % cuts) for i in range(cuts)])]
    ppermute x6 -> x0, waiting for transfers between devices: 11.4 us -> none  [group_turn(): return lax.ppermute(x, 'seq', to)]
    all_to_all x3 -> x2, starting transfers between devices: 21.2 us -> 10.4 us  [swap(): return lax.all_to_all(x, 'seq', 0, 0, tiled=True, axis_index_groups=groups)]
    all_to_all x3 -> x2, waiting for transfers between devices: 5.13 us -> 13.6 us  [swap(): return lax.all_to_all(x, 'seq', 0, 0, tiled=True, axis_index_groups=groups)]
    unnamed x16 -> x12, local copies, waits for them, and re-layouts: 7.4 us -> 2.43 us
  transfers between devices with their start and end apart: 15 -> 10, of which waited for: 9 -> 7; matrix products, arithmetic and copies ran while one was open for 1% -> 1% of each run, Pallas kernels for 6% -> 8%
where the time goes in v4:
time: 95.4 us; the launch traced here: 94.6 us
  starting transfers between devices  38 us (40%)
  waiting for transfers between devices  31.5 us (33%)
  Pallas kernels  19.2 us (20%)
  between operations  2.72 us (3%)
  local copies, waits for them, and re-layouts  2.43 us (3%)
    ppermute x6, waiting for transfers between devices, shards(): lax.ppermute(x, 'tensor', [(i, (i + d) % cuts) for i in range(cuts)])  17.9 us
    all_to_all x2, waiting for transfers between devices, swap(): return lax.all_to_all(x, 'seq', 0, 0, tiled=True, axis_index_groups=groups)  13.6 us
    all_to_all x1, starting transfers between devices, shards(): lax.all_to_all(sent.reshape(homes, served // 2 + 1, 2, HEAD_WIDTH), 'seq'...  13.2 us
    all_to_all x2, starting transfers between devices, swap(): return lax.all_to_all(x, 'seq', 0, 0, tiled=True, axis_index_groups=groups)  10.4 us
    all_to_all x1, starting transfers between devices, shards(): lax.all_to_all(sums.reshape(homes, served, HEAD_WIDTH), 'seq', 0, 0, tile...  8.03 us
    pallas_call x1, Pallas kernels, shards(): pl.pallas_call(functools.partial(attention_kernel, scale=HEAD_WIDTH ** (-...  6.94 us
    ppermute x6, starting transfers between devices, shards(): lax.ppermute(x, 'tensor', [(i, (i + d) % cuts) for i in range(cuts)])  6.43 us
    pallas_call x1, Pallas kernels, shards(): pl.pallas_call(grad_rows_kernel, out_shape=(shape(rows, width), shape(wid...  4.05 us
  transfers between devices with their start and end apart: 10, of which 7 were waited for; matrix products, arithmetic and copies ran while one was open for 1% of the time, Pallas kernels for 8%

profile of v4, /device:TPU:1, one launch (start us, length us, event | category | flops | bytes accessed | tf_op | source)
XLA Modules:
  0.0 94.6 jit_solution(9481674263333885759)
XLA Ops:
  0.6 0.0 copy-start
  0.6 0.0 copy-start.2
  0.7 0.0 copy-start.3
  2.0 0.0 copy-start.4
  2.0 0.7 copy-done.4
  2.8 0.0 copy-start.5
  2.8 0.8 copy-done.5
  3.5 0.9 pack.1
  4.4 13.2 %all-to-all-start = ((bf16[64,9,2,128]{3,2,1,0:T(2,128)(2,1)}), bf16[64,9,2,128]{3,2,1,0:T(2,128)(2,1)S(1)}, u32[]{:S(2)}, u32[]{:S(2)}) async-start(bf16[64,9,2,128]{3,2,1,0:T(2,128)(2,1)} %bitcast.2), calls=%async_computation | async-start | bytes 589824 | tf_op jit(solution)/shard_map/all_to_all | solution.py:298
  17.6 2.6 %collective-permute-start = (bf16[128,640]{1,0:T(8,128)(2,1)}, bf16[128,640]{1,0:T(8,128)(2,1)S(1)}, u32[]{:S(2)}, u32[]{:S(2)}) collective-permute-start(bf16[128,640]{1,0:T(8,128)(2,1)} %refs_0_), channel_id=1, source_target_pairs={{0,3},{1,0},{2,1},{3,2},{4,7},{5,4},{6,5},{7,6},{8,11},{9,8},{10,9... | collective-permute-start | bytes 491528 | tf_op jit(solution)/shard_map/ppermute | solution.py:286
  20.2 0.5 collective-permute-start.1
  20.7 0.6 collective-permute-start.2
  21.3 3.1 %collective-permute-done.refs_1_ = bf16[128,640]{1,0:T(8,128)(2,1)S(1)} collective-permute-done((bf16[128,640]{1,0:T(8,128)(2,1)}, bf16[128,640]{1,0:T(8,128)(2,1)S(1)}, u32[]{:S(2)}, u32[]{:S(2)}) %collective-permute-start) | collective-permute-done | bytes 163872 | tf_op jit(solution)/shard_map/ppermute | solution.py:286
  24.4 2.6 %collective-permute-done.1.refs_2_ = bf16[128,640]{1,0:T(8,128)(2,1)S(1)} collective-permute-done((bf16[128,640]{1,0:T(8,128)(2,1)}, bf16[128,640]{1,0:T(8,128)(2,1)S(1)}, u32[]{:S(2)}, u32[]{:S(2)}) %collective-permute-start.1) | collective-permute-done | bytes 163872 | tf_op jit(solution)/shard_map/ppermute | solution.py:286
  26.9 4.6 %collective-permute-done.2.refs_3_ = bf16[128,640]{1,0:T(8,128)(2,1)S(1)} collective-permute-done((bf16[128,640]{1,0:T(8,128)(2,1)}, bf16[128,640]{1,0:T(8,128)(2,1)S(1)}, u32[]{:S(2)}, u32[]{:S(2)}) %collective-permute-start.2) | collective-permute-done | bytes 163872 | tf_op jit(solution)/shard_map/ppermute | solution.py:286
  31.5 0.0 all-to-all-done
  31.5 2.0 %select.5 = (bf16[16,128,128]{2,1,0:T(8,128)(2,1)}, bf16[64,128]{1,0:T(8,128)(2,1)S(1)}) custom-call(s32[1]{0:T(128)} %bitcast.1.own_ref, bf16[1152,128]{1,0:T(8,128)(2,1)S(1)} %bitcast.6), custom_call_target="tpu_custom_call" | custom-call | tf_op jit(solution)/shard_map/select/pallas_call | solution.py:302
  33.5 5.9 %all-to-all-start.1 = ((bf16[16,128,128]{2,1,0:T(8,128)(2,1)}), bf16[16,128,128]{2,1,0:T(8,128)(2,1)S(1)}, u32[]{:S(2)}, u32[]{:S(2)}) async-start(bf16[16,128,128]{2,1,0:T(8,128)(2,1)} %get-tuple-element.27), calls=%async_computation.1 | async-start | bytes 1048576 | tf_op jit(solution)/shard_map/all_to_all | solution.py:284
  40.0 0.0 copy-start.1
  40.0 0.9 copy-done.1
  40.9 4.1 %grad_rows.1 = (bf16[128,1024]{1,0:T(8,128)(2,1)S(1)}, bf16[1024,128]{1,0:T(8,128)(2,1)S(1)}) custom-call(s32[1]{0:T(128)} %bitcast.at_ref, s32[1]{0:T(128)S(6)} %copy.18.len_ref, bf16[128,640]{1,0:T(8,128)(2,1)S(1)} %copy-done.1, bf16[128,640]{1,0:T(8,128)(2,1)S(1)} %collective-permute-done.refs_1_, bf16[128,640]{1,0:T(8,128)(2,1)S(1)} %collective-permute-done.1.refs_2_, ...), custom_call_target="tpu_custom_call" | custom-call | tf_op jit(solution)/shard_map/grad_rows/pallas_call | solution.py:327
  45.0 4.2 %all-to-all-done.1.g_ref = bf16[16,128,128]{2,1,0:T(8,128)(2,1)S(1)} async-done(((bf16[16,128,128]{2,1,0:T(8,128)(2,1)}), bf16[16,128,128]{2,1,0:T(8,128)(2,1)S(1)}, u32[]{:S(2)}, u32[]{:S(2)}) %all-to-all-start.1) | async-done | bytes 524320 | tf_op jit(solution)/shard_map/all_to_all | solution.py:284
  49.1 0.0 copy-done
  49.1 0.0 copy-done.2
  49.1 0.0 copy-done.3
  49.2 6.9 %attention.1 = (bf16[128,1024]{1,0:T(8,128)(2,1)S(1)}, bf16[128,1024]{1,0:T(8,128)(2,1)}, bf16[128,128]{1,0:T(8,128)(2,1)}, bf16[128,128]{1,0:T(8,128)(2,1)}, bf16[16,128,128]{2,1,0:T(8,128)(2,1)}) custom-call(s32[1]{0:T(128)S(6)} %copy.18.len_ref, bf16[128,1024]{1,0:T(8,128)(2,1)S(1)} %copy-done, bf16[128,128]{1,0:T(8,128)(2,1)S(1)} %copy-done.2, ...), custom_call_target="tpu_custom_call" | custom-call | tf_op jit(solution)/shard_map/attention/pallas_call | solution.py:338
  56.1 4.5 %all-to-all-start.2 = ((bf16[16,128,128]{2,1,0:T(8,128)(2,1)}), bf16[16,128,128]{2,1,0:T(8,128)(2,1)S(1)}, u32[]{:S(2)}, u32[]{:S(2)}) async-start(bf16[16,128,128]{2,1,0:T(8,128)(2,1)} %get-tuple-element.43), calls=%async_computation.2 | async-start | bytes 1048576 | tf_op jit(solution)/shard_map/all_to_all | solution.py:284
  60.6 0.5 home_map.1.map_ref
  61.1 9.4 %all-to-all-done.2.terms_ref = bf16[16,128,128]{2,1,0:T(8,128)(2,1)S(1)} async-done(((bf16[16,128,128]{2,1,0:T(8,128)(2,1)}), bf16[16,128,128]{2,1,0:T(8,128)(2,1)S(1)}, u32[]{:S(2)}, u32[]{:S(2)}) %all-to-all-start.2) | async-done | bytes 524320 | tf_op jit(solution)/shard_map/all_to_all | solution.py:284
  70.5 1.3 %combine.1 = bf16[1024,128]{1,0:T(8,128)(2,1)} custom-call(bf16[128,256]{1,0:T(8,128)(2,1)S(1)} %home_map.1.map_ref, bf16[16,128,128]{2,1,0:T(8,128)(2,1)S(1)} %all-to-all-done.2.terms_ref), custom_call_target="tpu_custom_call" | custom-call | tf_op jit(solution)/shard_map/combine/pallas_call | solution.py:372
  71.8 8.0 %all-to-all-start.3 = ((bf16[64,16,128]{2,1,0:T(8,128)(2,1)}), bf16[64,16,128]{2,1,0:T(8,128)(2,1)S(1)}, u32[]{:S(2)}, u32[]{:S(2)}) async-start(bf16[64,16,128]{2,1,0:T(8,128)(2,1)} %bitcast.4), calls=%async_computation.3 | async-start | bytes 524288 | tf_op jit(solution)/shard_map/all_to_all | solution.py:380
  79.8 3.0 %project.1 = (f32[128,640]{1,0:T(8,128)S(1)}, bf16[128,640]{1,0:T(8,128)(2,1)S(1)}, bf16[128,640]{1,0:T(8,128)(2,1)S(1)}, bf16[128,640]{1,0:T(8,128)(2,1)S(1)}) custom-call(s32[1]{0:T(128)} %bitcast.at_ref, bf16[128,1024]{1,0:T(8,128)(2,1)S(1)} %get-tuple-element.34.a_ref, bf16[1024,2560]{1,0:T(8,128)(2,1)} %w_ref.1), custom_call_target="tpu_custom_call" | custom-call | tf_op jit(solution)/shard_map/project/pallas_call | solution.py:359
  82.8 0.1 collective-permute-start.3
  82.9 1.5 %collective-permute-start.4 = (bf16[128,640]{1,0:T(8,128)(2,1)S(1)}, bf16[128,640]{1,0:T(8,128)(2,1)S(1)}, u32[]{:S(2)}, u32[]{:S(2)}) collective-permute-start(bf16[128,640]{1,0:T(8,128)(2,1)S(1)} %get-tuple-element.37), channel_id=1, source_target_pairs={{0,2},{1,3},{2,0},{3,1},{4,6},{5,7},{6,4},{7,5},{8,10},{9,11},{10,... | collective-permute-start | bytes 491528 | tf_op jit(solution)/shard_map/ppermute | solution.py:286
  84.4 1.2 %collective-permute-start.5 = (bf16[128,640]{1,0:T(8,128)(2,1)S(1)}, bf16[128,640]{1,0:T(8,128)(2,1)S(1)}, u32[]{:S(2)}, u32[]{:S(2)}) collective-permute-start(bf16[128,640]{1,0:T(8,128)(2,1)S(1)} %get-tuple-element.38), channel_id=1, source_target_pairs={{0,3},{1,0},{2,1},{3,2},{4,7},{5,4},{6,5},{7,6},{8,11},{9,8},{10,9... | collective-permute-start | bytes 491528 | tf_op jit(solution)/shard_map/ppermute | solution.py:286
  85.5 7.4 %collective-permute-done.3 = bf16[128,640]{1,0:T(8,128)(2,1)S(1)} collective-permute-done((bf16[128,640]{1,0:T(8,128)(2,1)S(1)}, bf16[128,640]{1,0:T(8,128)(2,1)S(1)}, u32[]{:S(2)}, u32[]{:S(2)}) %collective-permute-start.3) | collective-permute-done | bytes 163872 | tf_op jit(solution)/shard_map/ppermute | solution.py:286
  92.9 0.0 collective-permute-done.4
  92.9 0.3 collective-permute-done.5
  93.2 0.7 add_convert_fusion
  94.0 0.0 all-to-all-done.3
  94.0 0.7 home_sum.1
Async XLA Ops:
  0.6 48.5 %copy-start = (bf16[128,1024]{1,0:T(8,128)(2,1)S(1)}, bf16[128,1024]{1,0:T(8,128)(2,1)}, u32[]{:S(2)}) copy-start(bf16[128,1024]{1,0:T(8,128)(2,1)} %q_ref.1) | copy-start | bytes 786436
  0.6 48.5 %copy-start.2 = (bf16[128,128]{1,0:T(8,128)(2,1)S(1)}, bf16[128,128]{1,0:T(8,128)(2,1)}, u32[]{:S(2)}) copy-start(bf16[128,128]{1,0:T(8,128)(2,1)} %ks_ref.1) | copy-start | bytes 98308
  0.7 48.5 %copy-start.3 = (bf16[128,128]{1,0:T(8,128)(2,1)S(1)}, bf16[128,128]{1,0:T(8,128)(2,1)}, u32[]{:S(2)}) copy-start(bf16[128,128]{1,0:T(8,128)(2,1)} %vs_ref.1) | copy-start | bytes 98308
  2.0 0.8 copy-start.4
  2.8 0.8 copy-start.5
  4.4 27.1 %all-to-all-start = ((bf16[64,9,2,128]{3,2,1,0:T(2,128)(2,1)}), bf16[64,9,2,128]{3,2,1,0:T(2,128)(2,1)S(1)}, u32[]{:S(2)}, u32[]{:S(2)}) async-start(bf16[64,9,2,128]{3,2,1,0:T(2,128)(2,1)} %bitcast.2), calls=%async_computation | async-start | bytes 589824 | tf_op jit(solution)/shard_map/all_to_all | solution.py:298
  17.6 6.8 %collective-permute-start = (bf16[128,640]{1,0:T(8,128)(2,1)}, bf16[128,640]{1,0:T(8,128)(2,1)S(1)}, u32[]{:S(2)}, u32[]{:S(2)}) collective-permute-start(bf16[128,640]{1,0:T(8,128)(2,1)} %refs_0_), channel_id=1, source_target_pairs={{0,3},{1,0},{2,1},{3,2},{4,7},{5,4},{6,5},{7,6},{8,11},{9,8},{10,9... | collective-permute-start | bytes 491528 | tf_op jit(solution)/shard_map/ppermute | solution.py:286
  20.2 6.8 %collective-permute-start.1 = (bf16[128,640]{1,0:T(8,128)(2,1)}, bf16[128,640]{1,0:T(8,128)(2,1)S(1)}, u32[]{:S(2)}, u32[]{:S(2)}) collective-permute-start(bf16[128,640]{1,0:T(8,128)(2,1)} %refs_0_), channel_id=1, source_target_pairs={{0,2},{1,3},{2,0},{3,1},{4,6},{5,7},{6,4},{7,5},{8,10},{9,11},{10,... | collective-permute-start | bytes 491528 | tf_op jit(solution)/shard_map/ppermute | solution.py:286
  20.7 10.8 %collective-permute-start.2 = (bf16[128,640]{1,0:T(8,128)(2,1)}, bf16[128,640]{1,0:T(8,128)(2,1)S(1)}, u32[]{:S(2)}, u32[]{:S(2)}) collective-permute-start(bf16[128,640]{1,0:T(8,128)(2,1)} %refs_0_), channel_id=1, source_target_pairs={{0,1},{1,2},{2,3},{3,0},{4,5},{5,6},{6,7},{7,4},{8,9},{9,10},{10,1... | collective-permute-start | bytes 491528 | tf_op jit(solution)/shard_map/ppermute | solution.py:286
  33.5 15.7 %all-to-all-start.1 = ((bf16[16,128,128]{2,1,0:T(8,128)(2,1)}), bf16[16,128,128]{2,1,0:T(8,128)(2,1)S(1)}, u32[]{:S(2)}, u32[]{:S(2)}) async-start(bf16[16,128,128]{2,1,0:T(8,128)(2,1)} %get-tuple-element.27), calls=%async_computation.1 | async-start | bytes 1048576 | tf_op jit(solution)/shard_map/all_to_all | solution.py:284
  40.0 0.9 copy-start.1
  56.1 14.4 %all-to-all-start.2 = ((bf16[16,128,128]{2,1,0:T(8,128)(2,1)}), bf16[16,128,128]{2,1,0:T(8,128)(2,1)S(1)}, u32[]{:S(2)}, u32[]{:S(2)}) async-start(bf16[16,128,128]{2,1,0:T(8,128)(2,1)} %get-tuple-element.43), calls=%async_computation.2 | async-start | bytes 1048576 | tf_op jit(solution)/shard_map/all_to_all | solution.py:284
  71.8 22.2 %all-to-all-start.3 = ((bf16[64,16,128]{2,1,0:T(8,128)(2,1)}), bf16[64,16,128]{2,1,0:T(8,128)(2,1)S(1)}, u32[]{:S(2)}, u32[]{:S(2)}) async-start(bf16[64,16,128]{2,1,0:T(8,128)(2,1)} %bitcast.4), calls=%async_computation.3 | async-start | bytes 524288 | tf_op jit(solution)/shard_map/all_to_all | solution.py:380
  82.8 10.1 %collective-permute-start.3 = (bf16[128,640]{1,0:T(8,128)(2,1)S(1)}, bf16[128,640]{1,0:T(8,128)(2,1)S(1)}, u32[]{:S(2)}, u32[]{:S(2)}) collective-permute-start(bf16[128,640]{1,0:T(8,128)(2,1)S(1)} %get-tuple-element.36), channel_id=1, source_target_pairs={{0,1},{1,2},{2,3},{3,0},{4,5},{5,6},{6,7},{7,4},{8,9},{9,10},{10,1... | collective-permute-start | bytes 491528 | tf_op jit(solution)/shard_map/ppermute | solution.py:286
  82.9 10.0 %collective-permute-start.4 = (bf16[128,640]{1,0:T(8,128)(2,1)S(1)}, bf16[128,640]{1,0:T(8,128)(2,1)S(1)}, u32[]{:S(2)}, u32[]{:S(2)}) collective-permute-start(bf16[128,640]{1,0:T(8,128)(2,1)S(1)} %get-tuple-element.37), channel_id=1, source_target_pairs={{0,2},{1,3},{2,0},{3,1},{4,6},{5,7},{6,4},{7,5},{8,10},{9,11},{10,... | collective-permute-start | bytes 491528 | tf_op jit(solution)/shard_map/ppermute | solution.py:286
  84.4 8.9 %collective-permute-start.5 = (bf16[128,640]{1,0:T(8,128)(2,1)S(1)}, bf16[128,640]{1,0:T(8,128)(2,1)S(1)}, u32[]{:S(2)}, u32[]{:S(2)}) collective-permute-start(bf16[128,640]{1,0:T(8,128)(2,1)S(1)} %get-tuple-element.38), channel_id=1, source_target_pairs={{0,3},{1,0},{2,1},{3,2},{4,7},{5,4},{6,5},{7,6},{8,11},{9,8},{10,9... | collective-permute-start | bytes 491528 | tf_op jit(solution)/shard_map/ppermute | solution.py:286

commit v5 on v4

--- a/solution.py
+++ b/solution.py
@@ -35,14 +35,25 @@
     return iota(shape, dim).astype(F32)
 
 
-def pack_kernel(block_ref, rollout_ref, keys_ref, values_ref, sent_ref, *, rows, turns):
+def pack_kernel(
+    block_ref, rollout_ref, keys_hbm, values_hbm, sent_ref, keys_ref, values_ref, sems, *, rows, turns
+):
+    copies = [
+        pltpu.make_async_copy(keys_hbm, keys_ref, sems.at[0]),
+        pltpu.make_async_copy(values_hbm, values_ref, sems.at[1]),
+    ]
+    for copy in copies:
+        copy.start()
     total, tall = keys_ref.shape[0], sent_ref.shape[0] // turns
     group = rows + 2
     row, col = iota((tall, total), 0), iota((tall, total), 1)
     place = row % group
     source = jnp.where(place < rows, (row // group) * rows + place, -1)
-    packed = dot(one_hot(source, col), keys_ref[...])
-    packed = packed + dot(one_hot(source - total, col), values_ref[...])
+    take_keys, take_values = one_hot(source, col), one_hot(source - total, col)
+    for copy in copies:
+        copy.wait()
+    packed = dot(take_keys, keys_ref[...])
+    packed = packed + dot(take_values, values_ref[...])
     row, lane = iota(packed.shape, 0), iota(packed.shape, 1)
     names = jnp.where(lane == 0, block_ref[0], jnp.where(lane == 1, rollout_ref[0], 0))
     packed = jnp.where(row % group >= rows, names.astype(F32), packed).astype(BF16)
@@ -132,28 +143,34 @@
     values_ref[...] = total[half:].astype(BF16)
 
 
-def turned(at_ref, d, cuts, width):
-    return pl.ds(pl.multiple_of(lax.rem(at_ref[0] + d, cuts) * width, width), width)
-
-
-def fetch(at_ref, w_ref, held, sems):
-    cuts, _, width = held.shape
-    copies = [
-        pltpu.make_async_copy(w_ref.at[:, turned(at_ref, d, cuts, width)], held.at[d], sems.at[d])
-        for d in range(cuts)
-    ]
-    for copy in copies:
-        copy.start()
+def fetch(at_ref, w_ref, held, sems, turns, cuts):
+    width = held.shape[2]
+    copies = []
+    for i, d in enumerate(turns):
+        start = pl.multiple_of(lax.rem(at_ref[0] + d, cuts) * width, width)
+        copies.append(
+            pltpu.make_async_copy(w_ref.at[:, pl.ds(start, width)], held.at[i], sems.at[i])
+        )
+        copies[i].start()
     return copies
 
 
-def grad_rows_kernel(at_ref, len_ref, *refs):
-    *g_refs, w_ref, rows_ref, cols_ref, held, sems = refs
+def grad_rows_kernel(at_ref, *refs, turns, cuts):
+    *g_refs, w_ref, total_ref, held, sems = refs
     total = None
-    for d, copy in enumerate(fetch(at_ref, w_ref, held, sems)):
+    for i, copy in enumerate(fetch(at_ref, w_ref, held, sems, turns, cuts)):
         copy.wait()
-        term = dot_nt(held[d], g_refs[d][...])
+        term = dot_nt(held[i], g_refs[i][...])
         total = term if total is None else total + term
+    total_ref[...] = total
+
+
+def grad_rows_end_kernel(
+    at_ref, len_ref, first_ref, g_ref, w_ref, rows_ref, cols_ref, held, sems, *, turns, cuts
+):
+    (copy,) = fetch(at_ref, w_ref, held, sems, turns, cuts)
+    copy.wait()
+    total = first_ref[...] + dot_nt(held[0], g_ref[...])
     live = iota(total.shape, 1) < len_ref[0]
     total = jnp.where(live, total, 0.0)
     cols_ref[...] = total.astype(BF16)
@@ -162,11 +179,11 @@
         rows_ref[:, part] = total[part].T.astype(BF16)
 
 
-def project_kernel(at_ref, a_ref, w_ref, *refs):
+def project_kernel(at_ref, a_ref, w_ref, *refs, turns, cuts):
     *out_refs, held, sems = refs
-    for d, copy in enumerate(fetch(at_ref, w_ref, held, sems)):
+    for i, copy in enumerate(fetch(at_ref, w_ref, held, sems, turns, cuts)):
         copy.wait()
-        out_refs[d][...] = dot(a_ref[...], held[d]).astype(out_refs[d].dtype)
+        out_refs[i][...] = dot(a_ref[...], held[i]).astype(out_refs[i].dtype)
 
 
 def attention_kernel(
@@ -188,6 +205,7 @@
     dv_acc,
     *,
     scale,
+    together,
 ):
     n = len_ref[0]
     half = g_ref.shape[0] // 2
@@ -199,40 +217,55 @@
     v_all[prefix:, :] = vs_ref[...]
     k_t = k_all[...].T
     v_t = v_all[...].T
-    heads = q_ref.shape[1] // 128
-    key_at = iota((suffix, 2 * suffix), 0)
-    slot_at = iota((suffix, 2 * suffix), 1) % suffix
+    lanes = together * suffix
+    key_at = iota((suffix, lanes), 0)
+    slot_at = iota((suffix, lanes), 1) % suffix
     hidden = jnp.logical_or(key_at > slot_at, key_at >= n)
-    live = iota((1, 2 * suffix), 1) % suffix < n
+    live = iota((1, lanes), 1) % suffix < n
     to_log2 = scale * 1.4426950408889634
-    for pair in range(heads // 2):
-        one = slice(pair * 256, pair * 256 + 128)
-        two = slice(pair * 256 + 128, pair * 256 + 256)
-        q2 = jnp.concatenate([q_ref[:, one], q_ref[:, two]], axis=0)
-        da2 = jnp.concatenate([da_ref[:, one], da_ref[:, two]], axis=0)
-        dat2 = jnp.concatenate([dat_ref[one, :], dat_ref[two, :]], axis=1)
-        s_pre = dot_nt(k_all[:prefix], q2)
-        s_suf = jnp.where(hidden, -jnp.inf, dot_nt(k_all[prefix:], q2))
-        peak = jnp.maximum(
-            jnp.max(s_pre, axis=0, keepdims=True), jnp.max(s_suf, axis=0, keepdims=True)
-        )
-        w = jnp.concatenate(
-            [jnp.exp2((s_pre - peak) * to_log2), jnp.exp2((s_suf - peak) * to_log2)], axis=0
-        )
-        inverse = 1.0 / jnp.sum(w, axis=0, keepdims=True)
-        out_t = dot(v_t, w.astype(BF16)) * inverse
+    steps = q_ref.shape[1] // (together * HEAD_WIDTH)
+
+    def heads(step):
+        first = step * together
+        return [slice((first + i) * HEAD_WIDTH, (first + i + 1) * HEAD_WIDTH) for i in range(together)]
+
+    def rows_of(ref, step):
+        return jnp.concatenate([ref[:, h] for h in heads(step)], axis=0)
+
+    def put_rows(ref, step, x):
+        for i, h in enumerate(heads(step)):
+            ref[:, h] = x[:, i * suffix : (i + 1) * suffix].T.astype(BF16)
+
+    def scores(step):
+        s = dot_nt(k_all[...], rows_of(q_ref, step))
+        return s[:prefix], jnp.where(hidden, -jnp.inf, s[prefix:])
+
+    def softmax(s):
+        peak = jnp.maximum(*[jnp.max(part, axis=0, keepdims=True) for part in s])
+        parts = [jnp.exp2((part - peak) * to_log2) for part in s]
+        total = sum(jnp.sum(part, axis=0, keepdims=True) for part in parts)
+        w = jnp.concatenate(parts, axis=0)
+        return w, w.astype(BF16), 1.0 / total
+
+    ready = softmax(scores(0))
+    for step in range(steps):
+        last = step + 1 == steps
+        if not last:
+            coming = scores(step + 1)
+        w, w_rounded, inverse = ready
+        out_t = dot(v_t, w_rounded) * inverse
         out_t = jnp.where(live, out_t, 0.0).astype(BF16).astype(F32)
-        att_ref[:, one] = out_t[:, :128].T.astype(BF16)
-        att_ref[:, two] = out_t[:, 128:].T.astype(BF16)
-        dots = jnp.sum(out_t * dat2.astype(F32), axis=0, keepdims=True)
+        put_rows(att_ref, step, out_t)
+        dat = jnp.concatenate([dat_ref[h, :] for h in heads(step)], axis=1)
+        dots = jnp.sum(out_t * dat.astype(F32), axis=0, keepdims=True)
+        if not last:
+            ready = softmax(coming)
         probs = w * inverse
-        ds = (probs * (dot(v_all[...], dat2) - dots)).astype(BF16)
-        dq_t = dot(k_t, ds) * scale
-        dq_ref[:, one] = dq_t[:, :128].T.astype(BF16)
-        dq_ref[:, two] = dq_t[:, 128:].T.astype(BF16)
-        dk = dot(ds, q2)
-        dv = dot(probs.astype(BF16), da2)
-        if pair == 0:
+        ds = (probs * (dot(v_all[...], dat) - dots)).astype(BF16)
+        put_rows(dq_ref, step, dot(k_t, ds) * scale)
+        dk = dot(ds, rows_of(q_ref, step))
+        dv = dot(probs.astype(BF16), rows_of(da_ref, step))
+        if step == 0:
             dk_acc[...] = dk
             dv_acc[...] = dv
         else:
@@ -242,6 +275,10 @@
     dg_ref[half:] = dv_acc[:prefix].astype(BF16).reshape(half, -1, HEAD_WIDTH)
     dks_ref[...] = (dk_acc[prefix:] * scale).astype(BF16)
     dvs_ref[...] = dv_acc[prefix:].astype(BF16)
+
+
+def in_hbm(x):
+    return pltpu.with_memory_space_constraint(x, pltpu.HBM)
 
 
 def whole(memory=pltpu.VMEM):
@@ -290,15 +327,20 @@
     sent = pl.pallas_call(
         functools.partial(pack_kernel, rows=served, turns=turns),
         out_shape=shape(turns * tall, HEAD_WIDTH),
-        in_specs=[whole(pltpu.SMEM)] * 2 + [whole()] * 2,
+        in_specs=[whole(pltpu.SMEM)] * 2 + [whole(pltpu.HBM)] * 2,
         out_specs=whole(),
+        scratch_shapes=[
+            pltpu.VMEM(prefix_keys.shape, BF16),
+            pltpu.VMEM(prefix_keys.shape, BF16),
+            pltpu.SemaphoreType.DMA((2,)),
+        ],
         compiler_params=params(),
         name="pack",
-    )(block_prompt, rollout_prompt, prefix_keys, prefix_values)
+    )(block_prompt, rollout_prompt, in_hbm(prefix_keys), in_hbm(prefix_values))
     pieces = lax.all_to_all(
         sent.reshape(homes, served // 2 + 1, 2, HEAD_WIDTH), "seq", 0, 0, tiled=True
     ).reshape(turns * tall, HEAD_WIDTH)
-    pieces, grads = lax.optimization_barrier((pieces, grads))
+    pieces, grads[1], grads[-1] = lax.optimization_barrier((pieces, grads[1], grads[-1]))
     picked, meta = pl.pallas_call(
         functools.partial(
             select_kernel, per_prompt=per_prompt, servers=SERVERS, rows=served, turns=turns
@@ -320,23 +362,39 @@
     )(own, meta)
 
     weight = whole(pltpu.HBM)
-    held = [
-        pltpu.VMEM((cuts, width, features), BF16),
-        pltpu.SemaphoreType.DMA((cuts,)),
-    ]
+    out_weight = in_hbm(out_weight)
+
+    def held(turns):
+        return [
+            pltpu.VMEM((len(turns), width, features), BF16),
+            pltpu.SemaphoreType.DMA((len(turns),)),
+        ]
+
+    near = tuple(d for d in range(cuts) if d != cuts // 2)
+    far = (cuts // 2,)
+    first = pl.pallas_call(
+        functools.partial(grad_rows_kernel, turns=near, cuts=cuts),
+        out_shape=shape(width, rows, dtype=F32),
+        in_specs=[whole(pltpu.SMEM)] + [whole()] * len(near) + [weight],
+        out_specs=whole(),
+        scratch_shapes=held(near),
+        compiler_params=params(),
+        name="grad_rows",
+    )(at, *[grads[d] for d in near], out_weight)
     d_rows, d_cols = pl.pallas_call(
-        grad_rows_kernel,
+        functools.partial(grad_rows_end_kernel, turns=far, cuts=cuts),
         out_shape=(shape(rows, width), shape(width, rows)),
-        in_specs=[whole(pltpu.SMEM)] * 2 + [whole()] * cuts + [weight],
+        in_specs=[whole(pltpu.SMEM)] * 2 + [whole()] * 2 + [weight],
         out_specs=(whole(), whole()),
-        scratch_shapes=held,
-        compiler_params=params(),
-        name="grad_rows",
-    )(at, suffix_length, *grads, pltpu.with_memory_space_constraint(out_weight, pltpu.HBM))
-
+        scratch_shapes=held(far),
+        compiler_params=params(),
+        name="grad_rows_end",
+    )(at, suffix_length, first, grads[cuts // 2], out_weight)
+
+    gathered, home_map = lax.optimization_barrier((gathered, home_map))
     keys = prefix_keys.shape[0] * per_prompt + rows
     attended, d_queries, d_suffix_keys, d_suffix_values, d_gathered = pl.pallas_call(
-        functools.partial(attention_kernel, scale=HEAD_WIDTH**-0.5),
+        functools.partial(attention_kernel, scale=HEAD_WIDTH**-0.5, together=4),
         out_shape=(
             shape(rows, width),
             shape(rows, width),
@@ -356,19 +414,25 @@
         name="attention",
     )(suffix_length, queries, suffix_keys, suffix_values, gathered, d_rows, d_cols)
 
-    head_terms = pl.pallas_call(
-        project_kernel,
-        out_shape=(shape(rows, features, dtype=F32),) + (shape(rows, features),) * (cuts - 1),
-        in_specs=[whole(pltpu.SMEM), whole(), weight],
-        out_specs=(whole(),) * cuts,
-        scratch_shapes=held,
-        compiler_params=params(),
-        name="project",
-    )(at, attended, pltpu.with_memory_space_constraint(out_weight, pltpu.HBM))
-    projected = head_terms[0]
-    for d in range(1, cuts):
-        projected = projected + turn(head_terms[d], d).astype(F32)
-
+    def project(turns, own):
+        return pl.pallas_call(
+            functools.partial(project_kernel, turns=turns, cuts=cuts),
+            out_shape=[shape(rows, features, dtype=F32 if d == own else BF16) for d in turns],
+            in_specs=[whole(pltpu.SMEM), whole(), weight],
+            out_specs=[whole()] * len(turns),
+            scratch_shapes=held(turns),
+            compiler_params=params(),
+            name="project",
+        )(at, attended, out_weight)
+
+    one_hop = [d for d in near if d > 0]
+    terms_near = project(one_hop, 0)
+    terms_far = project((cuts // 2, 0), 0)
+    arrived = [turn(term, d) for d, term in zip(one_hop, terms_near)]
+    projected = terms_far[1] + sum(x.astype(F32) for x in arrived)
+    projected = projected + turn(terms_far[0], cuts // 2).astype(F32)
+
+    terms, _ = lax.optimization_barrier((swap(d_gathered), (arrived, terms_far)))
     sums = pl.pallas_call(
         functools.partial(combine_kernel, turns=turns),
         out_shape=shape(homes * served, HEAD_WIDTH),
@@ -376,7 +440,7 @@
         out_specs=whole(),
         compiler_params=params(),
         name="combine",
-    )(home_map, swap(d_gathered))
+    )(home_map, terms)
     back = lax.all_to_all(
         sums.reshape(homes, served, HEAD_WIDTH), "seq", 0, 0, tiled=True
     ).reshape(turns, 2 * prefix_rows, HEAD_WIDTH)

time: 95.4 us -> 90.7 us (0.951)
  waiting for transfers between devices: 31.5 us -> 24.3 us
  starting transfers between devices: 38 us -> 40.6 us
  Pallas kernels: 19.2 us -> 20.9 us
  local copies, waits for them, and re-layouts: 2.43 us -> 0.92 us
    all_to_all x2, waiting for transfers between devices: 13.6 us -> 0.61 us  [swap(): return lax.all_to_all(x, 'seq', 0, 0, tiled=True, axis_index_groups=groups)]
    all_to_all x1, waiting for transfers between devices: 0.01 us -> 6.9 us  [shards(): lax.all_to_all(sent.reshape(homes, served // 2 + 1, 2, HEAD_WIDTH), 'seq'...]
    ppermute x6, waiting for transfers between devices: 17.9 us -> 11.3 us  [shards(): lax.ppermute(x, 'tensor', [(i, (i + d) % cuts) for i in range(cuts)])]
    all_to_all x1, waiting for transfers between devices: 0.01 us -> 5.51 us  [shards(): lax.all_to_all(sums.reshape(homes, served, HEAD_WIDTH), 'seq', 0, 0, tile...]
    ppermute x6, starting transfers between devices: 6.43 us -> 10.1 us  [shards(): lax.ppermute(x, 'tensor', [(i, (i + d) % cuts) for i in range(cuts)])]
    pallas_call x2 -> x4, Pallas kernels: 7.01 us -> 9.69 us  [the longest x2 4.23 us: project(): pl.pallas_call(functools.partial(project_kernel, turns=turns, cuts=cuts),...]
    pallas_call x1, Pallas kernels: 6.94 us -> 5.16 us  [shards(): pl.pallas_call(functools.partial(attention_kernel, scale=HEAD_WIDTH ** (-...]
    unnamed x12 -> x8, local copies, waits for them, and re-layouts: 2.43 us -> 0.92 us
  transfers between devices with their start and end apart: 10 -> 10, of which waited for: 7 -> 6; matrix products, arithmetic and copies ran while one was open for 1% -> 1% of each run, Pallas kernels for 8% -> 11%
where the time goes in v5:
time: 90.7 us; the launch traced here: 90.1 us
  starting transfers between devices  40.6 us (45%)
  waiting for transfers between devices  24.3 us (27%)
  Pallas kernels  20.9 us (23%)
  between operations  2.7 us (3%)
  local copies, waits for them, and re-layouts  0.92 us (1%)
    all_to_all x1, starting transfers between devices, shards(): lax.all_to_all(sent.reshape(homes, served // 2 + 1, 2, HEAD_WIDTH), 'seq'...  13.2 us
    ppermute x6, waiting for transfers between devices, shards(): lax.ppermute(x, 'tensor', [(i, (i + d) % cuts) for i in range(cuts)])  11.3 us
    ppermute x6, starting transfers between devices, shards(): lax.ppermute(x, 'tensor', [(i, (i + d) % cuts) for i in range(cuts)])  10.1 us
    all_to_all x2, starting transfers between devices, swap(): return lax.all_to_all(x, 'seq', 0, 0, tiled=True, axis_index_groups=groups)  10.1 us
    all_to_all x1, starting transfers between devices, shards(): lax.all_to_all(sums.reshape(homes, served, HEAD_WIDTH), 'seq', 0, 0, tile...  7.11 us
    all_to_all x1, waiting for transfers between devices, shards(): lax.all_to_all(sent.reshape(homes, served // 2 + 1, 2, HEAD_WIDTH), 'seq'...  6.9 us
    all_to_all x1, waiting for transfers between devices, shards(): lax.all_to_all(sums.reshape(homes, served, HEAD_WIDTH), 'seq', 0, 0, tile...  5.51 us
    pallas_call x1, Pallas kernels, shards(): pl.pallas_call(functools.partial(attention_kernel, scale=HEAD_WIDTH ** (-...  5.16 us
  transfers between devices with their start and end apart: 10, of which 6 were waited for; matrix products, arithmetic and copies ran while one was open for 1% of the time, Pallas kernels for 11%

profile of v5, /device:TPU:1, one launch (start us, length us, event | category | flops | bytes accessed | tf_op | source)
XLA Modules:
  0.0 90.1 jit_solution(9581979640227380631)
XLA Ops:
  1.9 1.7 %pack.1 = bf16[1152,128]{1,0:T(8,128)(2,1)} custom-call(s32[1]{0:T(128)S(6)} %copy.16.block_ref, s32[1]{0:T(128)S(6)} %copy.17.rollout_ref, bf16[128,128]{1,0:T(8,128)(2,1)} %keys_hbm.1, bf16[128,128]{1,0:T(8,128)(2,1)} %values_hbm.1), custom_call_target="tpu_custom_call" | custom-call | tf_op jit(solution)/shard_map/pack/pallas_call | solution.py:327
  3.6 13.2 %all-to-all-start = ((bf16[64,9,2,128]{3,2,1,0:T(2,128)(2,1)}), bf16[64,9,2,128]{3,2,1,0:T(2,128)(2,1)S(1)}, u32[]{:S(2)}, u32[]{:S(2)}) async-start(bf16[64,9,2,128]{3,2,1,0:T(2,128)(2,1)} %bitcast.2), calls=%async_computation | async-start | bytes 589824 | tf_op jit(solution)/shard_map/all_to_all | solution.py:340
  16.8 1.3 %collective-permute-start.1 = (bf16[128,640]{1,0:T(8,128)(2,1)}, bf16[128,640]{1,0:T(8,128)(2,1)S(1)}, u32[]{:S(2)}, u32[]{:S(2)}) collective-permute-start(bf16[128,640]{1,0:T(8,128)(2,1)} %refs_0_.1), channel_id=1, source_target_pairs={{0,1},{1,2},{2,3},{3,0},{4,5},{5,6},{6,7},{7,4},{8,9},{9,10},{10,1... | collective-permute-start | bytes 491528 | tf_op jit(solution)/shard_map/ppermute | solution.py:323
  18.1 1.5 %collective-permute-start = (bf16[128,640]{1,0:T(8,128)(2,1)}, bf16[128,640]{1,0:T(8,128)(2,1)S(1)}, u32[]{:S(2)}, u32[]{:S(2)}) collective-permute-start(bf16[128,640]{1,0:T(8,128)(2,1)} %refs_0_.1), channel_id=1, source_target_pairs={{0,3},{1,0},{2,1},{3,2},{4,7},{5,4},{6,5},{7,6},{8,11},{9,8},{10,9... | collective-permute-start | bytes 491528 | tf_op jit(solution)/shard_map/ppermute | solution.py:323
  19.6 4.1 %collective-permute-done.1.refs_2_ = bf16[128,640]{1,0:T(8,128)(2,1)S(1)} collective-permute-done((bf16[128,640]{1,0:T(8,128)(2,1)}, bf16[128,640]{1,0:T(8,128)(2,1)S(1)}, u32[]{:S(2)}, u32[]{:S(2)}) %collective-permute-start.1) | collective-permute-done | bytes 163872 | tf_op jit(solution)/shard_map/ppermute | solution.py:323
  23.6 0.0 collective-permute-done.refs_1_
  23.6 6.9 %all-to-all-done = bf16[64,9,2,128]{3,2,1,0:T(2,128)(2,1)S(1)} async-done(((bf16[64,9,2,128]{3,2,1,0:T(2,128)(2,1)}), bf16[64,9,2,128]{3,2,1,0:T(2,128)(2,1)S(1)}, u32[]{:S(2)}, u32[]{:S(2)}) %all-to-all-start) | async-done | bytes 294944 | tf_op jit(solution)/shard_map/all_to_all | solution.py:340
  30.5 2.0 %select.5 = (bf16[16,128,128]{2,1,0:T(8,128)(2,1)}, bf16[64,128]{1,0:T(8,128)(2,1)S(1)}) custom-call(s32[1]{0:T(128)} %bitcast.1.own_ref, bf16[1152,128]{1,0:T(8,128)(2,1)S(1)} %bitcast.6), custom_call_target="tpu_custom_call" | custom-call | tf_op jit(solution)/shard_map/select/pallas_call | solution.py:344
  32.5 4.1 %all-to-all-start.1 = ((bf16[16,128,128]{2,1,0:T(8,128)(2,1)}), bf16[16,128,128]{2,1,0:T(8,128)(2,1)S(1)}, u32[]{:S(2)}, u32[]{:S(2)}) async-start(bf16[16,128,128]{2,1,0:T(8,128)(2,1)} %get-tuple-element.28), calls=%async_computation.1 | async-start | bytes 1048576 | tf_op jit(solution)/shard_map/all_to_all | solution.py:321
  36.6 2.7 %collective-permute-start.2 = (bf16[128,640]{1,0:T(8,128)(2,1)}, bf16[128,640]{1,0:T(8,128)(2,1)S(1)}, u32[]{:S(2)}, u32[]{:S(2)}) collective-permute-start(bf16[128,640]{1,0:T(8,128)(2,1)} %refs_0_.1), channel_id=1, source_target_pairs={{0,2},{1,3},{2,0},{3,1},{4,6},{5,7},{6,4},{7,5},{8,10},{9,11},{10,... | collective-permute-start | bytes 491528 | tf_op jit(solution)/shard_map/ppermute | solution.py:323
  40.0 0.5 home_map.1.map_ref
  40.5 0.0 copy-start.1
  40.5 0.9 %copy-done.1 = bf16[128,640]{1,0:T(8,128)(2,1)S(1)} copy-done((bf16[128,640]{1,0:T(8,128)(2,1)S(1)}, bf16[128,640]{1,0:T(8,128)(2,1)}, u32[]{:S(2)}) %copy-start.1) | copy-done | bytes 163864
  41.4 0.0 copy-start
  41.4 0.0 copy-start.2
  41.4 0.0 copy-start.3
  41.4 3.5 %grad_rows.1.first_ref = f32[1024,128]{1,0:T(8,128)S(1)} custom-call(s32[1]{0:T(128)} %bitcast.at_ref, bf16[128,640]{1,0:T(8,128)(2,1)S(1)} %copy-done.1, bf16[128,640]{1,0:T(8,128)(2,1)S(1)} %collective-permute-done.refs_1_, bf16[128,640]{1,0:T(8,128)(2,1)S(1)} %collective-permute-done.1.refs_2_, bf16[1024,2560]{1,0:T(8,128)(2,1)} %w_ref.5), custom_call_target="tpu_custom_call" | custom-call | tf_op jit(solution)/shard_map/grad_rows/pallas_call | solution.py:375
  44.9 0.0 collective-permute-done.2.g_ref
  45.0 1.9 %grad_rows_end.1 = (bf16[128,1024]{1,0:T(8,128)(2,1)S(1)}, bf16[1024,128]{1,0:T(8,128)(2,1)S(1)}) custom-call(s32[1]{0:T(128)} %bitcast.at_ref, s32[1]{0:T(128)S(6)} %copy.18.len_ref, f32[1024,128]{1,0:T(8,128)S(1)} %grad_rows.1.first_ref, bf16[128,640]{1,0:T(8,128)(2,1)S(1)} %collective-permute-done.2.g_ref, bf16[1024,2560]{1,0:T(8,128)(2,1)} %w_ref.5), custom_call_target="tpu_custom_call" | custom-call | tf_op jit(solution)/shard_map/grad_rows_end/pallas_call | solution.py:384
  46.9 0.0 all-to-all-done.1.g_ref
  46.9 0.0 copy-done
  46.9 0.0 copy-done.2
  46.9 0.0 copy-done.3
  46.9 5.2 %attention.1 = (bf16[128,1024]{1,0:T(8,128)(2,1)S(1)}, bf16[128,1024]{1,0:T(8,128)(2,1)}, bf16[128,128]{1,0:T(8,128)(2,1)}, bf16[128,128]{1,0:T(8,128)(2,1)}, bf16[16,128,128]{2,1,0:T(8,128)(2,1)}) custom-call(s32[1]{0:T(128)S(6)} %copy.18.len_ref, bf16[128,1024]{1,0:T(8,128)(2,1)S(1)} %copy-done, bf16[128,128]{1,0:T(8,128)(2,1)S(1)} %copy-done.2, ...), custom_call_target="tpu_custom_call" | custom-call | tf_op jit(solution)/shard_map/attention/pallas_call | solution.py:396
  52.1 6.0 %all-to-all-start.2 = ((bf16[16,128,128]{2,1,0:T(8,128)(2,1)}), bf16[16,128,128]{2,1,0:T(8,128)(2,1)S(1)}, u32[]{:S(2)}, u32[]{:S(2)}) async-start(bf16[16,128,128]{2,1,0:T(8,128)(2,1)} %get-tuple-element.44), calls=%async_computation.2 | async-start | bytes 1048576 | tf_op jit(solution)/shard_map/all_to_all | solution.py:321
  58.1 2.1 %project.3 = (bf16[128,640]{1,0:T(8,128)(2,1)S(1)}, bf16[128,640]{1,0:T(8,128)(2,1)S(1)}) custom-call(s32[1]{0:T(128)} %bitcast.at_ref, bf16[128,1024]{1,0:T(8,128)(2,1)S(1)} %get-tuple-element.35.a_ref, bf16[1024,2560]{1,0:T(8,128)(2,1)} %w_ref.5), custom_call_target="tpu_custom_call" | custom-call | tf_op jit(solution)/shard_map/project/pallas_call | solution.py:418
  60.2 0.7 collective-permute-start.3
  60.9 2.1 %collective-permute-start.4 = (bf16[128,640]{1,0:T(8,128)(2,1)S(1)}, bf16[128,640]{1,0:T(8,128)(2,1)S(1)}, u32[]{:S(2)}, u32[]{:S(2)}) collective-permute-start(bf16[128,640]{1,0:T(8,128)(2,1)S(1)} %get-tuple-element.38), channel_id=1, source_target_pairs={{0,3},{1,0},{2,1},{3,2},{4,7},{5,4},{6,5},{7,6},{8,11},{9,8},{10,9... | collective-permute-start | bytes 491528 | tf_op jit(solution)/shard_map/ppermute | solution.py:323
  63.0 2.1 %project.2 = (bf16[128,640]{1,0:T(8,128)(2,1)S(1)}, f32[128,640]{1,0:T(8,128)S(1)}) custom-call(s32[1]{0:T(128)} %bitcast.at_ref, bf16[128,1024]{1,0:T(8,128)(2,1)S(1)} %get-tuple-element.35.a_ref, bf16[1024,2560]{1,0:T(8,128)(2,1)} %w_ref.5), custom_call_target="tpu_custom_call" | custom-call | tf_op jit(solution)/shard_map/project/pallas_call | solution.py:418
  65.1 2.2 %collective-permute-done.3 = bf16[128,640]{1,0:T(8,128)(2,1)S(1)} collective-permute-done((bf16[128,640]{1,0:T(8,128)(2,1)S(1)}, bf16[128,640]{1,0:T(8,128)(2,1)S(1)}, u32[]{:S(2)}, u32[]{:S(2)}) %collective-permute-start.3) | collective-permute-done | bytes 163872 | tf_op jit(solution)/shard_map/ppermute | solution.py:323
  67.3 0.0 collective-permute-done.4
  67.3 0.6 all-to-all-done.2.terms_ref
  67.9 1.3 %combine.1 = bf16[1024,128]{1,0:T(8,128)(2,1)} custom-call(bf16[128,256]{1,0:T(8,128)(2,1)S(1)} %home_map.1.map_ref, bf16[16,128,128]{2,1,0:T(8,128)(2,1)S(1)} %all-to-all-done.2.terms_ref), custom_call_target="tpu_custom_call" | custom-call | tf_op jit(solution)/shard_map/combine/pallas_call | solution.py:436
  69.2 7.1 %all-to-all-start.3 = ((bf16[64,16,128]{2,1,0:T(8,128)(2,1)}), bf16[64,16,128]{2,1,0:T(8,128)(2,1)S(1)}, u32[]{:S(2)}, u32[]{:S(2)}) async-start(bf16[64,16,128]{2,1,0:T(8,128)(2,1)} %bitcast.4), calls=%async_computation.3 | async-start | bytes 524288 | tf_op jit(solution)/shard_map/all_to_all | solution.py:444
  76.3 1.9 %collective-permute-start.5 = (bf16[128,640]{1,0:T(8,128)(2,1)S(1)}, bf16[128,640]{1,0:T(8,128)(2,1)S(1)}, u32[]{:S(2)}, u32[]{:S(2)}) collective-permute-start(bf16[128,640]{1,0:T(8,128)(2,1)S(1)} %get-tuple-element.39), channel_id=1, source_target_pairs={{0,2},{1,3},{2,0},{3,1},{4,6},{5,7},{6,4},{7,5},{8,10},{9,11},{10,... | collective-permute-start | bytes 491528 | tf_op jit(solution)/shard_map/ppermute | solution.py:323
  78.1 5.0 %collective-permute-done.5 = bf16[128,640]{1,0:T(8,128)(2,1)S(1)} collective-permute-done((bf16[128,640]{1,0:T(8,128)(2,1)S(1)}, bf16[128,640]{1,0:T(8,128)(2,1)S(1)}, u32[]{:S(2)}, u32[]{:S(2)}) %collective-permute-start.5) | collective-permute-done | bytes 163872 | tf_op jit(solution)/shard_map/ppermute | solution.py:323
  83.2 0.7 add_convert_fusion
  83.9 5.5 %all-to-all-done.3 = bf16[64,16,128]{2,1,0:T(8,128)(2,1)S(1)} async-done(((bf16[64,16,128]{2,1,0:T(8,128)(2,1)}), bf16[64,16,128]{2,1,0:T(8,128)(2,1)S(1)}, u32[]{:S(2)}, u32[]{:S(2)}) %all-to-all-start.3) | async-done | bytes 262176 | tf_op jit(solution)/shard_map/all_to_all | solution.py:444
  89.4 0.7 home_sum.1
Async XLA Ops:
  3.6 26.9 %all-to-all-start = ((bf16[64,9,2,128]{3,2,1,0:T(2,128)(2,1)}), bf16[64,9,2,128]{3,2,1,0:T(2,128)(2,1)S(1)}, u32[]{:S(2)}, u32[]{:S(2)}) async-start(bf16[64,9,2,128]{3,2,1,0:T(2,128)(2,1)} %bitcast.2), calls=%async_computation | async-start | bytes 589824 | tf_op jit(solution)/shard_map/all_to_all | solution.py:340
  16.8 6.8 %collective-permute-start.1 = (bf16[128,640]{1,0:T(8,128)(2,1)}, bf16[128,640]{1,0:T(8,128)(2,1)S(1)}, u32[]{:S(2)}, u32[]{:S(2)}) collective-permute-start(bf16[128,640]{1,0:T(8,128)(2,1)} %refs_0_.1), channel_id=1, source_target_pairs={{0,1},{1,2},{2,3},{3,0},{4,5},{5,6},{6,7},{7,4},{8,9},{9,10},{10,1... | collective-permute-start | bytes 491528 | tf_op jit(solution)/shard_map/ppermute | solution.py:323
  18.1 5.5 %collective-permute-start = (bf16[128,640]{1,0:T(8,128)(2,1)}, bf16[128,640]{1,0:T(8,128)(2,1)S(1)}, u32[]{:S(2)}, u32[]{:S(2)}) collective-permute-start(bf16[128,640]{1,0:T(8,128)(2,1)} %refs_0_.1), channel_id=1, source_target_pairs={{0,3},{1,0},{2,1},{3,2},{4,7},{5,4},{6,5},{7,6},{8,11},{9,8},{10,9... | collective-permute-start | bytes 491528 | tf_op jit(solution)/shard_map/ppermute | solution.py:323
  32.5 14.4 %all-to-all-start.1 = ((bf16[16,128,128]{2,1,0:T(8,128)(2,1)}), bf16[16,128,128]{2,1,0:T(8,128)(2,1)S(1)}, u32[]{:S(2)}, u32[]{:S(2)}) async-start(bf16[16,128,128]{2,1,0:T(8,128)(2,1)} %get-tuple-element.28), calls=%async_computation.1 | async-start | bytes 1048576 | tf_op jit(solution)/shard_map/all_to_all | solution.py:321
  36.6 8.3 %collective-permute-start.2 = (bf16[128,640]{1,0:T(8,128)(2,1)}, bf16[128,640]{1,0:T(8,128)(2,1)S(1)}, u32[]{:S(2)}, u32[]{:S(2)}) collective-permute-start(bf16[128,640]{1,0:T(8,128)(2,1)} %refs_0_.1), channel_id=1, source_target_pairs={{0,2},{1,3},{2,0},{3,1},{4,6},{5,7},{6,4},{7,5},{8,10},{9,11},{10,... | collective-permute-start | bytes 491528 | tf_op jit(solution)/shard_map/ppermute | solution.py:323
  40.5 0.9 %copy-start.1 = (bf16[128,640]{1,0:T(8,128)(2,1)S(1)}, bf16[128,640]{1,0:T(8,128)(2,1)}, u32[]{:S(2)}) copy-start(bf16[128,640]{1,0:T(8,128)(2,1)} %refs_0_.1) | copy-start | bytes 491524
  41.4 5.5 %copy-start = (bf16[128,1024]{1,0:T(8,128)(2,1)S(1)}, bf16[128,1024]{1,0:T(8,128)(2,1)}, u32[]{:S(2)}) copy-start(bf16[128,1024]{1,0:T(8,128)(2,1)} %q_ref.1) | copy-start | bytes 786436
  41.4 5.5 %copy-start.2 = (bf16[128,128]{1,0:T(8,128)(2,1)S(1)}, bf16[128,128]{1,0:T(8,128)(2,1)}, u32[]{:S(2)}) copy-start(bf16[128,128]{1,0:T(8,128)(2,1)} %ks_ref.1) | copy-start | bytes 98308
  41.4 5.5 %copy-start.3 = (bf16[128,128]{1,0:T(8,128)(2,1)S(1)}, bf16[128,128]{1,0:T(8,128)(2,1)}, u32[]{:S(2)}) copy-start(bf16[128,128]{1,0:T(8,128)(2,1)} %vs_ref.1) | copy-start | bytes 98308
  52.1 15.8 %all-to-all-start.2 = ((bf16[16,128,128]{2,1,0:T(8,128)(2,1)}), bf16[16,128,128]{2,1,0:T(8,128)(2,1)S(1)}, u32[]{:S(2)}, u32[]{:S(2)}) async-start(bf16[16,128,128]{2,1,0:T(8,128)(2,1)} %get-tuple-element.44), calls=%async_computation.2 | async-start | bytes 1048576 | tf_op jit(solution)/shard_map/all_to_all | solution.py:321
  60.2 7.1 %collective-permute-start.3 = (bf16[128,640]{1,0:T(8,128)(2,1)S(1)}, bf16[128,640]{1,0:T(8,128)(2,1)S(1)}, u32[]{:S(2)}, u32[]{:S(2)}) collective-permute-start(bf16[128,640]{1,0:T(8,128)(2,1)S(1)} %get-tuple-element.37), channel_id=1, source_target_pairs={{0,1},{1,2},{2,3},{3,0},{4,5},{5,6},{6,7},{7,4},{8,9},{9,10},{10,1... | collective-permute-start | bytes 491528 | tf_op jit(solution)/shard_map/ppermute | solution.py:323
  60.9 6.4 %collective-permute-start.4 = (bf16[128,640]{1,0:T(8,128)(2,1)S(1)}, bf16[128,640]{1,0:T(8,128)(2,1)S(1)}, u32[]{:S(2)}, u32[]{:S(2)}) collective-permute-start(bf16[128,640]{1,0:T(8,128)(2,1)S(1)} %get-tuple-element.38), channel_id=1, source_target_pairs={{0,3},{1,0},{2,1},{3,2},{4,7},{5,4},{6,5},{7,6},{8,11},{9,8},{10,9... | collective-permute-start | bytes 491528 | tf_op jit(solution)/shard_map/ppermute | solution.py:323
  69.2 20.3 %all-to-all-start.3 = ((bf16[64,16,128]{2,1,0:T(8,128)(2,1)}), bf16[64,16,128]{2,1,0:T(8,128)(2,1)S(1)}, u32[]{:S(2)}, u32[]{:S(2)}) async-start(bf16[64,16,128]{2,1,0:T(8,128)(2,1)} %bitcast.4), calls=%async_computation.3 | async-start | bytes 524288 | tf_op jit(solution)/shard_map/all_to_all | solution.py:444
  76.3 6.9 %collective-permute-start.5 = (bf16[128,640]{1,0:T(8,128)(2,1)S(1)}, bf16[128,640]{1,0:T(8,128)(2,1)S(1)}, u32[]{:S(2)}, u32[]{:S(2)}) collective-permute-start(bf16[128,640]{1,0:T(8,128)(2,1)S(1)} %get-tuple-element.39), channel_id=1, source_target_pairs={{0,2},{1,3},{2,0},{3,1},{4,6},{5,7},{6,4},{7,5},{8,10},{9,11},{10,... | collective-permute-start | bytes 491528 | tf_op jit(solution)/shard_map/ppermute | solution.py:323

commit v6 on v5

--- a/solution.py
+++ b/solution.py
@@ -2,6 +2,7 @@
 
 import jax
 import jax.numpy as jnp
+import numpy as np
 from jax import lax
 from jax.experimental import pallas as pl
 from jax.experimental.pallas import tpu as pltpu
@@ -62,40 +63,60 @@
 
 
 def swap_pairs(tall, outer):
-    row, col = iota((tall, tall), 0), iota((tall, tall), 1)
-    pair = row // 2
-    return one_hot((pair % outer * (tall // 2 // outer) + pair // outer) * 2 + row % 2, col)
-
-
-def block_codes(meta, own, *, per_prompt, servers):
+    rows = np.arange(tall).reshape(outer, -1, 2).swapaxes(0, 1).reshape(tall)
+    return jnp.asarray(np.eye(tall)[rows], BF16)
+
+
+def name_rows(blocks, group):
+    take = np.zeros((blocks, blocks, group))
+    take[np.arange(blocks), np.arange(blocks), group - 2] = 1
+    return jnp.asarray(take.reshape(blocks, blocks * group), BF16)
+
+
+def block_codes(meta, *, per_prompt):
     blocks = meta.shape[0]
-    block_prompt = meta[:, 0:1].astype(F32)
-    named = one_hot(block_prompt, fiota((blocks, 128), 1))
-    same = dot_nt(named, named)
-    row, col = iota((blocks, blocks), 0), iota((blocks, blocks), 1)
-    rank = jnp.sum(jnp.where(col < row, same, 0.0), axis=1, keepdims=True)
-    take = one_hot(iota((servers, blocks), 0) + own * servers, iota((servers, blocks), 1))
-    return block_prompt * per_prompt + rank, dot(take, meta)[:, 1:2]
-
-
-def select_kernel(own_ref, pieces_ref, picked_ref, meta_ref, *, per_prompt, servers, rows, turns):
-    tall = servers * (rows + 2)
-    swap = swap_pairs(tall, servers)
+    first_lane = one_hot(iota((8, 128), 1), 0)
+    prompt_row = dot_nt(first_lane, meta)[0:1]
+    same = meta[:, 0:1].astype(F32) == prompt_row
+    before = iota((blocks, blocks), 0) < iota((blocks, blocks), 1)
+    rank = jnp.sum(jnp.where(jnp.logical_and(same, before), 1.0, 0.0), axis=0, keepdims=True)
+    return prompt_row * per_prompt + rank
+
+
+def own_rollouts(meta, own, *, servers, span):
+    wants, blocks = servers * span, meta.shape[0]
+    take = one_hot(iota((wants, blocks), 0) // span + own * servers, iota((wants, blocks), 1))
+    return dot(take, meta)[:, 1:2]
+
+
+def select_kernel(
+    own_ref,
+    pieces_ref,
+    swap_ref,
+    take_ref,
+    picked_ref,
+    meta_ref,
+    *,
+    per_prompt,
+    servers,
+    rows,
+    turns,
+):
+    tall, blocks = servers * (rows + 2), servers * turns
+    each, span = 2 * servers, 2 * per_prompt
+    wants = span * servers
+    meta = dot(take_ref[...], pieces_ref[...]).astype(BF16)
+    meta_ref[...] = meta
+    swap = swap_ref[...]
     pieces = [
         dot(swap, pieces_ref[g * tall : (g + 1) * tall]).astype(BF16) for g in range(turns)
     ]
-    each, blocks = 2 * servers, servers * turns
-    meta = jnp.concatenate([p[rows // 2 * each :] for p in pieces])
-    one_each = one_hot(iota((blocks, 2 * blocks), 0) * 2, iota((blocks, 2 * blocks), 1))
-    meta = dot(one_each, meta).astype(BF16)
-    meta_ref[...] = meta
-    code, rollout = block_codes(meta, own_ref[0], per_prompt=per_prompt, servers=servers)
-    span, wants = 2 * per_prompt, 2 * per_prompt * servers
-    spread = iota((blocks, 2 * blocks), 1) // 2 == iota((blocks, 2 * blocks), 0)
-    have = jnp.sum(jnp.where(spread, code, 0.0), axis=0, keepdims=True) * 2
+    code = jnp.broadcast_to(block_codes(meta, per_prompt=per_prompt), (8, blocks))
+    spread = one_hot(iota((blocks, 2 * blocks), 1) // 2, iota((blocks, 2 * blocks), 0))
+    have = dot(code.astype(BF16), spread)[0:1] * 2
     have = have + (iota((1, 2 * blocks), 1) % 2).astype(F32)
-    want = jnp.broadcast_to(rollout.reshape(servers, 1, 1), (servers, span, 1))
-    want = want.reshape(wants, 1) * span + (iota((wants, 1), 0) % span).astype(F32)
+    want = own_rollouts(meta, own_ref[0], servers=servers, span=span) * span
+    want = want + (iota((wants, 1), 0) % span).astype(F32)
     choose = one_hot(want, have)
     for p in range(rows // 2):
         from_all = jnp.concatenate([part[p * each : (p + 1) * each] for part in pieces])
@@ -104,24 +125,22 @@
 
 
 def map_kernel(own_ref, meta_ref, map_ref, *, per_prompt, servers):
-    code, rollout = block_codes(
-        meta_ref[...], own_ref[0], per_prompt=per_prompt, servers=servers
-    )
-    blocks = code.shape[0]
+    meta = meta_ref[...]
+    blocks = meta.shape[0]
     tall, wants = map_ref.shape
     span = 2 * per_prompt
-    eye = iota((blocks, blocks), 0) == iota((blocks, blocks), 1)
-    code_row = jnp.sum(jnp.where(eye, code, 0.0), axis=0, keepdims=True)
+    code_row = block_codes(meta, per_prompt=per_prompt)
     mine = iota((tall, blocks), 0) // 2 == iota((tall, blocks), 1)
     have = jnp.sum(jnp.where(mine, code_row, 0.0), axis=1, keepdims=True) * 2
     have = have + (iota((tall, 1), 0) % 2).astype(F32)
+    rollout = own_rollouts(meta, own_ref[0], servers=servers, span=1)
     spread = iota((servers, wants), 1) // span == iota((servers, wants), 0)
     want = jnp.sum(jnp.where(spread, rollout, 0.0), axis=0, keepdims=True) * span
     want = want + (iota((1, wants), 1) % span).astype(F32)
     map_ref[...] = one_hot(have, want)
 
 
-def combine_kernel(map_ref, terms_ref, out_ref, *, turns):
+def combine_kernel(map_ref, terms_ref, swap_ref, out_ref, *, turns):
     servers, tall, _ = terms_ref.shape
     wants = map_ref.shape[1]
     span, each = wants // servers, map_ref.shape[0] // turns
@@ -130,7 +149,7 @@
         terms = terms_ref[:, p * span : (p + 1) * span, :].reshape(wants, HEAD_WIDTH)
         sums.append(dot(map_ref[...], terms).astype(BF16))
     rows = each * len(sums)
-    swap = swap_pairs(rows, len(sums))
+    swap = swap_ref[...]
     for g in range(turns):
         part = jnp.concatenate([s[g * each : (g + 1) * each] for s in sums])
         out_ref[g * rows : (g + 1) * rows, :] = dot(swap, part).astype(BF16)
@@ -156,11 +175,12 @@
 
 
 def grad_rows_kernel(at_ref, *refs, turns, cuts):
-    *g_refs, w_ref, total_ref, held, sems = refs
-    total = None
-    for i, copy in enumerate(fetch(at_ref, w_ref, held, sems, turns, cuts)):
+    *in_refs, w_ref, total_ref, held, sems = refs
+    copies = fetch(at_ref, w_ref, held, sems, turns, cuts)
+    total = in_refs[-1][...] if len(in_refs) > len(turns) else None
+    for i, copy in enumerate(copies):
         copy.wait()
-        term = dot_nt(held[i], g_refs[i][...])
+        term = dot_nt(held[i], in_refs[i][...])
         total = term if total is None else total + term
     total_ref[...] = total
 
@@ -261,10 +281,10 @@
         if not last:
             ready = softmax(coming)
         probs = w * inverse
+        dv = dot(probs.astype(BF16), rows_of(da_ref, step))
         ds = (probs * (dot(v_all[...], dat) - dots)).astype(BF16)
         put_rows(dq_ref, step, dot(k_t, ds) * scale)
         dk = dot(ds, rows_of(q_ref, step))
-        dv = dot(probs.astype(BF16), rows_of(da_ref, step))
         if step == 0:
             dk_acc[...] = dk
             dv_acc[...] = dv
@@ -322,6 +342,30 @@
 
     turn = lambda x, d: lax.ppermute(x, "tensor", [(i, (i + d) % cuts) for i in range(cuts)])
     grads = [out_grad] + [turn(out_grad, cuts - d) for d in range(1, cuts)]
+    weight = whole(pltpu.HBM)
+    out_weight = in_hbm(out_weight)
+
+    def held(turns):
+        return [
+            pltpu.VMEM((len(turns), width, features), BF16),
+            pltpu.SemaphoreType.DMA((len(turns),)),
+        ]
+
+    def grad_rows(turns, *before):
+        return pl.pallas_call(
+            functools.partial(grad_rows_kernel, turns=turns, cuts=cuts),
+            out_shape=shape(width, rows, dtype=F32),
+            in_specs=[whole(pltpu.SMEM)] + [whole()] * (len(turns) + len(before)) + [weight],
+            out_specs=whole(),
+            scratch_shapes=held(turns),
+            compiler_params=params(),
+            name="grad_rows",
+        )(at, *[grads[d] for d in turns], *before, out_weight)
+
+    one_hop = tuple(d for d in range(1, cuts) if d != cuts // 2)
+    far = (cuts // 2,)
+    first = grad_rows(one_hop, grad_rows((0,)))
+
     turns = homes // SERVERS
     own = (lax.axis_index("seq") // SERVERS).astype(jnp.int32).reshape(1)
     sent = pl.pallas_call(
@@ -340,17 +384,17 @@
     pieces = lax.all_to_all(
         sent.reshape(homes, served // 2 + 1, 2, HEAD_WIDTH), "seq", 0, 0, tiled=True
     ).reshape(turns * tall, HEAD_WIDTH)
-    pieces, grads[1], grads[-1] = lax.optimization_barrier((pieces, grads[1], grads[-1]))
+    pieces, first = lax.optimization_barrier((pieces, first))
     picked, meta = pl.pallas_call(
         functools.partial(
             select_kernel, per_prompt=per_prompt, servers=SERVERS, rows=served, turns=turns
         ),
         out_shape=(shape(SERVERS, span, HEAD_WIDTH), shape(homes, 128)),
-        in_specs=[whole(pltpu.SMEM), whole()],
+        in_specs=[whole(pltpu.SMEM)] + [whole()] * 3,
         out_specs=(whole(), whole()),
         compiler_params=params(),
         name="select",
-    )(own, pieces)
+    )(own, pieces, swap_pairs(tall, SERVERS), name_rows(homes, served + 2))
     gathered = swap(picked)
     home_map = pl.pallas_call(
         functools.partial(map_kernel, per_prompt=per_prompt, servers=SERVERS),
@@ -361,26 +405,6 @@
         name="home_map",
     )(own, meta)
 
-    weight = whole(pltpu.HBM)
-    out_weight = in_hbm(out_weight)
-
-    def held(turns):
-        return [
-            pltpu.VMEM((len(turns), width, features), BF16),
-            pltpu.SemaphoreType.DMA((len(turns),)),
-        ]
-
-    near = tuple(d for d in range(cuts) if d != cuts // 2)
-    far = (cuts // 2,)
-    first = pl.pallas_call(
-        functools.partial(grad_rows_kernel, turns=near, cuts=cuts),
-        out_shape=shape(width, rows, dtype=F32),
-        in_specs=[whole(pltpu.SMEM)] + [whole()] * len(near) + [weight],
-        out_specs=whole(),
-        scratch_shapes=held(near),
-        compiler_params=params(),
-        name="grad_rows",
-    )(at, *[grads[d] for d in near], out_weight)
     d_rows, d_cols = pl.pallas_call(
         functools.partial(grad_rows_end_kernel, turns=far, cuts=cuts),
         out_shape=(shape(rows, width), shape(width, rows)),
@@ -425,7 +449,6 @@
             name="project",
         )(at, attended, out_weight)
 
-    one_hop = [d for d in near if d > 0]
     terms_near = project(one_hop, 0)
     terms_far = project((cuts // 2, 0), 0)
     arrived = [turn(term, d) for d, term in zip(one_hop, terms_near)]
@@ -436,11 +459,11 @@
     sums = pl.pallas_call(
         functools.partial(combine_kernel, turns=turns),
         out_shape=shape(homes * served, HEAD_WIDTH),
-        in_specs=[whole(), whole()],
+        in_specs=[whole(), whole(), whole()],
         out_specs=whole(),
         compiler_params=params(),
         name="combine",
-    )(home_map, terms)
+    )(home_map, terms, swap_pairs(2 * prefix_rows, served // 2))
     back = lax.all_to_all(
         sums.reshape(homes, served, HEAD_WIDTH), "seq", 0, 0, tiled=True
     ).reshape(turns, 2 * prefix_rows, HEAD_WIDTH)

time: 90.7 us -> 90.1 us (level)
  waiting for transfers between devices: 24.3 us -> 21.8 us
  starting transfers between devices: 40.6 us -> 42 us
    all_to_all x1, waiting for transfers between devices: 6.9 us -> 4.13 us  [shards(): lax.all_to_all(sent.reshape(homes, served // 2 + 1, 2, HEAD_WIDTH), 'seq'...]
    pallas_call x1 -> x2, Pallas kernels: 3.52 us -> 4.6 us  [grad_rows(): pl.pallas_call(functools.partial(grad_rows_kernel, turns=turns, cuts=cuts...]
    ppermute x6, starting transfers between devices: 10.1 us -> 11.2 us  [shards(): lax.ppermute(x, 'tensor', [(i, (i + d) % cuts) for i in range(cuts)])]
  transfers between devices with their start and end apart: 10 -> 10, of which waited for: 6 -> 8; matrix products, arithmetic and copies ran while one was open for 1% -> 1% of each run, Pallas kernels for 11% -> 12%
where the time goes in v6:
time: 90.1 us; the launch traced here: 89.4 us
  starting transfers between devices  42 us (47%)
  waiting for transfers between devices  21.8 us (24%)
  Pallas kernels  21.2 us (24%)
  between operations  2.71 us (3%)
  local copies, waits for them, and re-layouts  0.99 us (1%)
    all_to_all x1, starting transfers between devices, shards(): lax.all_to_all(sent.reshape(homes, served // 2 + 1, 2, HEAD_WIDTH), 'seq'...  13.2 us
    ppermute x6, starting transfers between devices, shards(): lax.ppermute(x, 'tensor', [(i, (i + d) % cuts) for i in range(cuts)])  11.2 us
    ppermute x6, waiting for transfers between devices, shards(): lax.ppermute(x, 'tensor', [(i, (i + d) % cuts) for i in range(cuts)])  11.1 us
    all_to_all x2, starting transfers between devices, swap(): return lax.all_to_all(x, 'seq', 0, 0, tiled=True, axis_index_groups=groups)  9.88 us
    all_to_all x1, starting transfers between devices, shards(): lax.all_to_all(sums.reshape(homes, served, HEAD_WIDTH), 'seq', 0, 0, tile...  7.8 us
    all_to_all x1, waiting for transfers between devices, shards(): lax.all_to_all(sums.reshape(homes, served, HEAD_WIDTH), 'seq', 0, 0, tile...  5.51 us
    pallas_call x1, Pallas kernels, shards(): pl.pallas_call(functools.partial(attention_kernel, scale=HEAD_WIDTH ** (-...  4.91 us
    pallas_call x2, Pallas kernels, grad_rows(): pl.pallas_call(functools.partial(grad_rows_kernel, turns=turns, cuts=cuts...  4.6 us
  transfers between devices with their start and end apart: 10, of which 8 were waited for; matrix products, arithmetic and copies ran while one was open for 1% of the time, Pallas kernels for 12%

profile of v6, /device:TPU:1, one launch (start us, length us, event | category | flops | bytes accessed | tf_op | source)
XLA Modules:
  0.0 89.4 jit_solution(13479310993932849343)
XLA Ops:
  1.9 1.7 %pack.1 = bf16[1152,128]{1,0:T(8,128)(2,1)} custom-call(s32[1]{0:T(128)S(6)} %copy.19.block_ref, s32[1]{0:T(128)S(6)} %copy.20.rollout_ref, bf16[128,128]{1,0:T(8,128)(2,1)} %keys_hbm.1, bf16[128,128]{1,0:T(8,128)(2,1)} %values_hbm.1), custom_call_target="tpu_custom_call" | custom-call | tf_op jit(solution)/shard_map/pack/pallas_call | solution.py:371
  3.6 13.2 %all-to-all-start = ((bf16[64,9,2,128]{3,2,1,0:T(2,128)(2,1)}), bf16[64,9,2,128]{3,2,1,0:T(2,128)(2,1)S(1)}, u32[]{:S(2)}, u32[]{:S(2)}) async-start(bf16[64,9,2,128]{3,2,1,0:T(2,128)(2,1)} %bitcast.2), calls=%async_computation | async-start | bytes 589824 | tf_op jit(solution)/shard_map/all_to_all | solution.py:384
  16.8 1.3 %collective-permute-start.1 = (bf16[128,640]{1,0:T(8,128)(2,1)}, bf16[128,640]{1,0:T(8,128)(2,1)S(1)}, u32[]{:S(2)}, u32[]{:S(2)}) collective-permute-start(bf16[128,640]{1,0:T(8,128)(2,1)} %refs_0_.1), channel_id=1, source_target_pairs={{0,1},{1,2},{2,3},{3,0},{4,5},{5,6},{6,7},{7,4},{8,9},{9,10},{10,1... | collective-permute-start | bytes 491528 | tf_op jit(solution)/shard_map/ppermute | solution.py:343
  18.1 1.5 %collective-permute-start = (bf16[128,640]{1,0:T(8,128)(2,1)}, bf16[128,640]{1,0:T(8,128)(2,1)S(1)}, u32[]{:S(2)}, u32[]{:S(2)}) collective-permute-start(bf16[128,640]{1,0:T(8,128)(2,1)} %refs_0_.1), channel_id=1, source_target_pairs={{0,3},{1,0},{2,1},{3,2},{4,7},{5,4},{6,5},{7,6},{8,11},{9,8},{10,9... | collective-permute-start | bytes 491528 | tf_op jit(solution)/shard_map/ppermute | solution.py:343
  19.6 0.0 copy-start.2
  19.6 0.9 %copy-done.2 = bf16[128,640]{1,0:T(8,128)(2,1)S(1)} copy-done((bf16[128,640]{1,0:T(8,128)(2,1)S(1)}, bf16[128,640]{1,0:T(8,128)(2,1)}, u32[]{:S(2)}) %copy-start.2) | copy-done | bytes 163864
  20.5 0.0 copy-start.1
  20.5 0.0 copy-start.4
  20.5 1.9 %grad_rows.2.refs_2_ = f32[1024,128]{1,0:T(8,128)S(1)} custom-call(s32[1]{0:T(128)} %bitcast.at_ref, bf16[128,640]{1,0:T(8,128)(2,1)S(1)} %copy-done.2, bf16[1024,2560]{1,0:T(8,128)(2,1)} %w_ref.5), custom_call_target="tpu_custom_call" | custom-call | tf_op jit(solution)/shard_map/grad_rows/pallas_call | solution.py:355
  22.4 0.0 copy-start.3
  22.4 1.2 %collective-permute-done.1.refs_1_ = bf16[128,640]{1,0:T(8,128)(2,1)S(1)} collective-permute-done((bf16[128,640]{1,0:T(8,128)(2,1)}, bf16[128,640]{1,0:T(8,128)(2,1)S(1)}, u32[]{:S(2)}, u32[]{:S(2)}) %collective-permute-start.1) | collective-permute-done | bytes 163872 | tf_op jit(solution)/shard_map/ppermute | solution.py:343
  23.6 0.0 collective-permute-done.refs_0_
  23.6 2.7 %grad_rows.3.first_ref = f32[1024,128]{1,0:T(8,128)S(1)} custom-call(s32[1]{0:T(128)} %bitcast.at_ref, bf16[128,640]{1,0:T(8,128)(2,1)S(1)} %collective-permute-done.refs_0_, bf16[128,640]{1,0:T(8,128)(2,1)S(1)} %collective-permute-done.1.refs_1_, f32[1024,128]{1,0:T(8,128)S(1)} %grad_rows.2.refs_2_, bf16[1024,2560]{1,0:T(8,128)(2,1)} %w_ref.5), custom_call_target="tpu_custom_call" | custom-call | tf_op jit(solution)/shard_map/grad_rows/pallas_call | solution.py:355
  26.3 0.0 copy-start
  26.4 0.0 copy-start.6
  26.4 0.0 copy-start.7
  26.4 4.1 %all-to-all-done = bf16[64,9,2,128]{3,2,1,0:T(2,128)(2,1)S(1)} async-done(((bf16[64,9,2,128]{3,2,1,0:T(2,128)(2,1)}), bf16[64,9,2,128]{3,2,1,0:T(2,128)(2,1)S(1)}, u32[]{:S(2)}, u32[]{:S(2)}) %all-to-all-start) | async-done | bytes 294944 | tf_op jit(solution)/shard_map/all_to_all | solution.py:384
  30.5 0.0 copy-done.1
  30.5 0.0 copy-done.4
  30.5 1.7 %select.5 = (bf16[16,128,128]{2,1,0:T(8,128)(2,1)}, bf16[64,128]{1,0:T(8,128)(2,1)S(1)}) custom-call(s32[1]{0:T(128)} %bitcast.1.own_ref, bf16[1152,128]{1,0:T(8,128)(2,1)S(1)} %bitcast.6, bf16[288,288]{1,0:T(8,128)(2,1)S(1)} %copy-done.1, bf16[64,1152]{1,0:T(8,128)(2,1)S(1)} %copy-done.4), custom_call_target="tpu_custom_call" | custom-call | tf_op jit(solution)/shard_map/select/pallas_call | solution.py:388
  32.2 4.1 %all-to-all-start.1 = ((bf16[16,128,128]{2,1,0:T(8,128)(2,1)}), bf16[16,128,128]{2,1,0:T(8,128)(2,1)S(1)}, u32[]{:S(2)}, u32[]{:S(2)}) async-start(bf16[16,128,128]{2,1,0:T(8,128)(2,1)} %get-tuple-element.27), calls=%async_computation.1 | async-start | bytes 1048576 | tf_op jit(solution)/shard_map/all_to_all | solution.py:341
  36.3 0.0 copy-done.3
  36.3 2.8 %collective-permute-start.2 = (bf16[128,640]{1,0:T(8,128)(2,1)S(1)}, bf16[128,640]{1,0:T(8,128)(2,1)S(1)}, u32[]{:S(2)}, u32[]{:S(2)}) collective-permute-start(bf16[128,640]{1,0:T(8,128)(2,1)S(1)} %copy-done.3), channel_id=1, source_target_pairs={{0,2},{1,3},{2,0},{3,1},{4,6},{5,7},{6,4},{7,5},{8,10},{9,11},{10,... | collective-permute-start | bytes 491528 | tf_op jit(solution)/shard_map/ppermute | solution.py:343
  39.8 0.2 home_map.1.map_ref
  40.1 3.6 %collective-permute-done.2.g_ref = bf16[128,640]{1,0:T(8,128)(2,1)S(1)} collective-permute-done((bf16[128,640]{1,0:T(8,128)(2,1)S(1)}, bf16[128,640]{1,0:T(8,128)(2,1)S(1)}, u32[]{:S(2)}, u32[]{:S(2)}) %collective-permute-start.2) | collective-permute-done | bytes 163872 | tf_op jit(solution)/shard_map/ppermute | solution.py:343
  43.7 1.9 %grad_rows_end.1 = (bf16[128,1024]{1,0:T(8,128)(2,1)S(1)}, bf16[1024,128]{1,0:T(8,128)(2,1)S(1)}) custom-call(s32[1]{0:T(128)} %bitcast.at_ref, s32[1]{0:T(128)S(6)} %copy.21.len_ref, f32[1024,128]{1,0:T(8,128)S(1)} %grad_rows.3.first_ref, bf16[128,640]{1,0:T(8,128)(2,1)S(1)} %collective-permute-done.2.g_ref, bf16[1024,2560]{1,0:T(8,128)(2,1)} %w_ref.5), custom_call_target="tpu_custom_call" | custom-call | tf_op jit(solution)/shard_map/grad_rows_end/pallas_call | solution.py:408
  45.6 0.5 all-to-all-done.1.g_ref
  46.1 0.0 copy-done
  46.1 0.0 copy-done.6
  46.1 0.0 copy-done.7
  46.1 4.9 %attention.1 = (bf16[128,1024]{1,0:T(8,128)(2,1)S(1)}, bf16[128,1024]{1,0:T(8,128)(2,1)}, bf16[128,128]{1,0:T(8,128)(2,1)}, bf16[128,128]{1,0:T(8,128)(2,1)}, bf16[16,128,128]{2,1,0:T(8,128)(2,1)}) custom-call(s32[1]{0:T(128)S(6)} %copy.21.len_ref, bf16[128,1024]{1,0:T(8,128)(2,1)S(1)} %copy-done, bf16[128,128]{1,0:T(8,128)(2,1)S(1)} %copy-done.6, ...), custom_call_target="tpu_custom_call" | custom-call | tf_op jit(solution)/shard_map/attention/pallas_call | solution.py:420
  51.0 5.7 %all-to-all-start.2 = ((bf16[16,128,128]{2,1,0:T(8,128)(2,1)}), bf16[16,128,128]{2,1,0:T(8,128)(2,1)S(1)}, u32[]{:S(2)}, u32[]{:S(2)}) async-start(bf16[16,128,128]{2,1,0:T(8,128)(2,1)} %get-tuple-element.42), calls=%async_computation.2 | async-start | bytes 1048576 | tf_op jit(solution)/shard_map/all_to_all | solution.py:341
  56.8 0.0 copy-start.5
  56.8 2.2 %project.3 = (bf16[128,640]{1,0:T(8,128)(2,1)S(1)}, bf16[128,640]{1,0:T(8,128)(2,1)S(1)}) custom-call(s32[1]{0:T(128)} %bitcast.at_ref, bf16[128,1024]{1,0:T(8,128)(2,1)S(1)} %get-tuple-element.33.a_ref, bf16[1024,2560]{1,0:T(8,128)(2,1)} %w_ref.5), custom_call_target="tpu_custom_call" | custom-call | tf_op jit(solution)/shard_map/project/pallas_call | solution.py:442
  59.0 1.3 %collective-permute-start.3 = (bf16[128,640]{1,0:T(8,128)(2,1)S(1)}, bf16[128,640]{1,0:T(8,128)(2,1)S(1)}, u32[]{:S(2)}, u32[]{:S(2)}) collective-permute-start(bf16[128,640]{1,0:T(8,128)(2,1)S(1)} %get-tuple-element.35), channel_id=1, source_target_pairs={{0,1},{1,2},{2,3},{3,0},{4,5},{5,6},{6,7},{7,4},{8,9},{9,10},{10,1... | collective-permute-start | bytes 491528 | tf_op jit(solution)/shard_map/ppermute | solution.py:343
  60.3 1.5 %collective-permute-start.4 = (bf16[128,640]{1,0:T(8,128)(2,1)S(1)}, bf16[128,640]{1,0:T(8,128)(2,1)S(1)}, u32[]{:S(2)}, u32[]{:S(2)}) collective-permute-start(bf16[128,640]{1,0:T(8,128)(2,1)S(1)} %get-tuple-element.36), channel_id=1, source_target_pairs={{0,3},{1,0},{2,1},{3,2},{4,7},{5,4},{6,5},{7,6},{8,11},{9,8},{10,9... | collective-permute-start | bytes 491528 | tf_op jit(solution)/shard_map/ppermute | solution.py:343
  61.8 2.1 %project.2 = (bf16[128,640]{1,0:T(8,128)(2,1)S(1)}, f32[128,640]{1,0:T(8,128)S(1)}) custom-call(s32[1]{0:T(128)} %bitcast.at_ref, bf16[128,1024]{1,0:T(8,128)(2,1)S(1)} %get-tuple-element.33.a_ref, bf16[1024,2560]{1,0:T(8,128)(2,1)} %w_ref.5), custom_call_target="tpu_custom_call" | custom-call | tf_op jit(solution)/shard_map/project/pallas_call | solution.py:442
  63.9 2.1 %collective-permute-done.3 = bf16[128,640]{1,0:T(8,128)(2,1)S(1)} collective-permute-done((bf16[128,640]{1,0:T(8,128)(2,1)S(1)}, bf16[128,640]{1,0:T(8,128)(2,1)S(1)}, u32[]{:S(2)}, u32[]{:S(2)}) %collective-permute-start.3) | collective-permute-done | bytes 163872 | tf_op jit(solution)/shard_map/ppermute | solution.py:343
  66.0 0.0 collective-permute-done.4
  66.0 0.6 all-to-all-done.2.terms_ref
  66.6 0.0 copy-done.5
  66.6 1.2 %combine.1 = bf16[1024,128]{1,0:T(8,128)(2,1)} custom-call(bf16[128,256]{1,0:T(8,128)(2,1)S(1)} %home_map.1.map_ref, bf16[16,128,128]{2,1,0:T(8,128)(2,1)S(1)} %all-to-all-done.2.terms_ref, bf16[256,256]{1,0:T(8,128)(2,1)S(1)} %copy-done.5), custom_call_target="tpu_custom_call" | custom-call | tf_op jit(solution)/shard_map/combine/pallas_call | solution.py:459
  67.8 7.8 %all-to-all-start.3 = ((bf16[64,16,128]{2,1,0:T(8,128)(2,1)}), bf16[64,16,128]{2,1,0:T(8,128)(2,1)S(1)}, u32[]{:S(2)}, u32[]{:S(2)}) async-start(bf16[64,16,128]{2,1,0:T(8,128)(2,1)} %bitcast.4), calls=%async_computation.3 | async-start | bytes 524288 | tf_op jit(solution)/shard_map/all_to_all | solution.py:467
  75.6 2.7 %collective-permute-start.5 = (bf16[128,640]{1,0:T(8,128)(2,1)S(1)}, bf16[128,640]{1,0:T(8,128)(2,1)S(1)}, u32[]{:S(2)}, u32[]{:S(2)}) collective-permute-start(bf16[128,640]{1,0:T(8,128)(2,1)S(1)} %get-tuple-element.37), channel_id=1, source_target_pairs={{0,2},{1,3},{2,0},{3,1},{4,6},{5,7},{6,4},{7,5},{8,10},{9,11},{10,... | collective-permute-start | bytes 491528 | tf_op jit(solution)/shard_map/ppermute | solution.py:343
  78.4 4.2 %collective-permute-done.5 = bf16[128,640]{1,0:T(8,128)(2,1)S(1)} collective-permute-done((bf16[128,640]{1,0:T(8,128)(2,1)S(1)}, bf16[128,640]{1,0:T(8,128)(2,1)S(1)}, u32[]{:S(2)}, u32[]{:S(2)}) %collective-permute-start.5) | collective-permute-done | bytes 163872 | tf_op jit(solution)/shard_map/ppermute | solution.py:343
  82.5 0.7 add_convert_fusion
  83.3 5.5 %all-to-all-done.3 = bf16[64,16,128]{2,1,0:T(8,128)(2,1)S(1)} async-done(((bf16[64,16,128]{2,1,0:T(8,128)(2,1)}), bf16[64,16,128]{2,1,0:T(8,128)(2,1)S(1)}, u32[]{:S(2)}, u32[]{:S(2)}) %all-to-all-start.3) | async-done | bytes 262176 | tf_op jit(solution)/shard_map/all_to_all | solution.py:467
  88.8 0.7 home_sum.1
Async XLA Ops:
  3.6 26.9 %all-to-all-start = ((bf16[64,9,2,128]{3,2,1,0:T(2,128)(2,1)}), bf16[64,9,2,128]{3,2,1,0:T(2,128)(2,1)S(1)}, u32[]{:S(2)}, u32[]{:S(2)}) async-start(bf16[64,9,2,128]{3,2,1,0:T(2,128)(2,1)} %bitcast.2), calls=%async_computation | async-start | bytes 589824 | tf_op jit(solution)/shard_map/all_to_all | solution.py:384
  16.8 6.8 %collective-permute-start.1 = (bf16[128,640]{1,0:T(8,128)(2,1)}, bf16[128,640]{1,0:T(8,128)(2,1)S(1)}, u32[]{:S(2)}, u32[]{:S(2)}) collective-permute-start(bf16[128,640]{1,0:T(8,128)(2,1)} %refs_0_.1), channel_id=1, source_target_pairs={{0,1},{1,2},{2,3},{3,0},{4,5},{5,6},{6,7},{7,4},{8,9},{9,10},{10,1... | collective-permute-start | bytes 491528 | tf_op jit(solution)/shard_map/ppermute | solution.py:343
  18.1 5.5 %collective-permute-start = (bf16[128,640]{1,0:T(8,128)(2,1)}, bf16[128,640]{1,0:T(8,128)(2,1)S(1)}, u32[]{:S(2)}, u32[]{:S(2)}) collective-permute-start(bf16[128,640]{1,0:T(8,128)(2,1)} %refs_0_.1), channel_id=1, source_target_pairs={{0,3},{1,0},{2,1},{3,2},{4,7},{5,4},{6,5},{7,6},{8,11},{9,8},{10,9... | collective-permute-start | bytes 491528 | tf_op jit(solution)/shard_map/ppermute | solution.py:343
  19.6 0.9 %copy-start.2 = (bf16[128,640]{1,0:T(8,128)(2,1)S(1)}, bf16[128,640]{1,0:T(8,128)(2,1)}, u32[]{:S(2)}) copy-start(bf16[128,640]{1,0:T(8,128)(2,1)} %refs_0_.1) | copy-start | bytes 491524
  20.5 10.0 %copy-start.1 = (bf16[288,288]{1,0:T(8,128)(2,1)S(1)}, bf16[288,288]{1,0:T(8,128)(2,1)}, u32[]{:S(2)}) copy-start(bf16[288,288]{1,0:T(8,128)(2,1)} %constant.31.clone.swap_ref) | copy-start | bytes 497668
  20.5 10.0 %copy-start.4 = (bf16[64,1152]{1,0:T(8,128)(2,1)S(1)}, bf16[64,1152]{1,0:T(8,128)(2,1)}, u32[]{:S(2)}) copy-start(bf16[64,1152]{1,0:T(8,128)(2,1)} %constant.32.clone.take_ref) | copy-start | bytes 442372
  22.4 13.9 %copy-start.3 = (bf16[128,640]{1,0:T(8,128)(2,1)S(1)}, bf16[128,640]{1,0:T(8,128)(2,1)}, u32[]{:S(2)}) copy-start(bf16[128,640]{1,0:T(8,128)(2,1)} %refs_0_.1) | copy-start | bytes 491524
  26.3 19.8 %copy-start = (bf16[128,1024]{1,0:T(8,128)(2,1)S(1)}, bf16[128,1024]{1,0:T(8,128)(2,1)}, u32[]{:S(2)}) copy-start(bf16[128,1024]{1,0:T(8,128)(2,1)} %q_ref.1) | copy-start | bytes 786436
  26.4 19.8 %copy-start.6 = (bf16[128,128]{1,0:T(8,128)(2,1)S(1)}, bf16[128,128]{1,0:T(8,128)(2,1)}, u32[]{:S(2)}) copy-start(bf16[128,128]{1,0:T(8,128)(2,1)} %ks_ref.1) | copy-start | bytes 98308
  26.4 19.8 %copy-start.7 = (bf16[128,128]{1,0:T(8,128)(2,1)S(1)}, bf16[128,128]{1,0:T(8,128)(2,1)}, u32[]{:S(2)}) copy-start(bf16[128,128]{1,0:T(8,128)(2,1)} %vs_ref.1) | copy-start | bytes 98308
  32.2 13.9 %all-to-all-start.1 = ((bf16[16,128,128]{2,1,0:T(8,128)(2,1)}), bf16[16,128,128]{2,1,0:T(8,128)(2,1)S(1)}, u32[]{:S(2)}, u32[]{:S(2)}) async-start(bf16[16,128,128]{2,1,0:T(8,128)(2,1)} %get-tuple-element.27), calls=%async_computation.1 | async-start | bytes 1048576 | tf_op jit(solution)/shard_map/all_to_all | solution.py:341
  36.3 7.4 %collective-permute-start.2 = (bf16[128,640]{1,0:T(8,128)(2,1)S(1)}, bf16[128,640]{1,0:T(8,128)(2,1)S(1)}, u32[]{:S(2)}, u32[]{:S(2)}) collective-permute-start(bf16[128,640]{1,0:T(8,128)(2,1)S(1)} %copy-done.3), channel_id=1, source_target_pairs={{0,2},{1,3},{2,0},{3,1},{4,6},{5,7},{6,4},{7,5},{8,10},{9,11},{10,... | collective-permute-start | bytes 491528 | tf_op jit(solution)/shard_map/ppermute | solution.py:343
  51.0 15.5 %all-to-all-start.2 = ((bf16[16,128,128]{2,1,0:T(8,128)(2,1)}), bf16[16,128,128]{2,1,0:T(8,128)(2,1)S(1)}, u32[]{:S(2)}, u32[]{:S(2)}) async-start(bf16[16,128,128]{2,1,0:T(8,128)(2,1)} %get-tuple-element.42), calls=%async_computation.2 | async-start | bytes 1048576 | tf_op jit(solution)/shard_map/all_to_all | solution.py:341
  56.8 9.8 %copy-start.5 = (bf16[256,256]{1,0:T(8,128)(2,1)S(1)}, bf16[256,256]{1,0:T(8,128)(2,1)}, u32[]{:S(2)}) copy-start(bf16[256,256]{1,0:T(8,128)(2,1)} %constant.33.clone.swap_ref) | copy-start | bytes 393220
  59.0 7.1 %collective-permute-start.3 = (bf16[128,640]{1,0:T(8,128)(2,1)S(1)}, bf16[128,640]{1,0:T(8,128)(2,1)S(1)}, u32[]{:S(2)}, u32[]{:S(2)}) collective-permute-start(bf16[128,640]{1,0:T(8,128)(2,1)S(1)} %get-tuple-element.35), channel_id=1, source_target_pairs={{0,1},{1,2},{2,3},{3,0},{4,5},{5,6},{6,7},{7,4},{8,9},{9,10},{10,1... | collective-permute-start | bytes 491528 | tf_op jit(solution)/shard_map/ppermute | solution.py:343
  60.3 5.7 %collective-permute-start.4 = (bf16[128,640]{1,0:T(8,128)(2,1)S(1)}, bf16[128,640]{1,0:T(8,128)(2,1)S(1)}, u32[]{:S(2)}, u32[]{:S(2)}) collective-permute-start(bf16[128,640]{1,0:T(8,128)(2,1)S(1)} %get-tuple-element.36), channel_id=1, source_target_pairs={{0,3},{1,0},{2,1},{3,2},{4,7},{5,4},{6,5},{7,6},{8,11},{9,8},{10,9... | collective-permute-start | bytes 491528 | tf_op jit(solution)/shard_map/ppermute | solution.py:343
  67.8 21.0 %all-to-all-start.3 = ((bf16[64,16,128]{2,1,0:T(8,128)(2,1)}), bf16[64,16,128]{2,1,0:T(8,128)(2,1)S(1)}, u32[]{:S(2)}, u32[]{:S(2)}) async-start(bf16[64,16,128]{2,1,0:T(8,128)(2,1)} %bitcast.4), calls=%async_computation.3 | async-start | bytes 524288 | tf_op jit(solution)/shard_map/all_to_all | solution.py:467
  75.6 6.9 %collective-permute-start.5 = (bf16[128,640]{1,0:T(8,128)(2,1)S(1)}, bf16[128,640]{1,0:T(8,128)(2,1)S(1)}, u32[]{:S(2)}, u32[]{:S(2)}) collective-permute-start(bf16[128,640]{1,0:T(8,128)(2,1)S(1)} %get-tuple-element.37), channel_id=1, source_target_pairs={{0,2},{1,3},{2,0},{3,1},{4,6},{5,7},{6,4},{7,5},{8,10},{9,11},{10,... | collective-permute-start | bytes 491528 | tf_op jit(solution)/shard_map/ppermute | solution.py:343

commit v7 on v6

--- a/solution.py
+++ b/solution.py
@@ -174,23 +174,24 @@
     return copies
 
 
-def grad_rows_kernel(at_ref, *refs, turns, cuts):
-    *in_refs, w_ref, total_ref, held, sems = refs
-    copies = fetch(at_ref, w_ref, held, sems, turns, cuts)
-    total = in_refs[-1][...] if len(in_refs) > len(turns) else None
-    for i, copy in enumerate(copies):
-        copy.wait()
+def grad_rows_kernel(at_ref, *refs, turns, cuts, after):
+    refs, (held, sems) = refs[:-2], refs[-2:]
+    count = len(refs) - 2 - len(after)
+    in_refs, w_ref, total_ref = refs[:count], refs[count], refs[count + 1]
+    copies = fetch(at_ref, w_ref, held, sems, turns + after, cuts)
+    total = in_refs[-1][...] if count > len(turns) else None
+    for i in range(len(turns)):
+        copies[i].wait()
         term = dot_nt(held[i], in_refs[i][...])
         total = term if total is None else total + term
     total_ref[...] = total
-
-
-def grad_rows_end_kernel(
-    at_ref, len_ref, first_ref, g_ref, w_ref, rows_ref, cols_ref, held, sems, *, turns, cuts
-):
-    (copy,) = fetch(at_ref, w_ref, held, sems, turns, cuts)
-    copy.wait()
-    total = first_ref[...] + dot_nt(held[0], g_ref[...])
+    for i, ref in enumerate(refs[count + 2 :]):
+        copies[len(turns) + i].wait()
+        ref[...] = held[len(turns) + i]
+
+
+def grad_rows_end_kernel(len_ref, first_ref, g_ref, w_ref, rows_ref, cols_ref):
+    total = first_ref[...] + dot_nt(w_ref[...], g_ref[...])
     live = iota(total.shape, 1) < len_ref[0]
     total = jnp.where(live, total, 0.0)
     cols_ref[...] = total.astype(BF16)
@@ -351,20 +352,20 @@
             pltpu.SemaphoreType.DMA((len(turns),)),
         ]
 
-    def grad_rows(turns, *before):
+    def grad_rows(turns, before, after):
         return pl.pallas_call(
-            functools.partial(grad_rows_kernel, turns=turns, cuts=cuts),
-            out_shape=shape(width, rows, dtype=F32),
+            functools.partial(grad_rows_kernel, turns=turns, cuts=cuts, after=after),
+            out_shape=[shape(width, rows, dtype=F32)] + [shape(width, features)] * len(after),
             in_specs=[whole(pltpu.SMEM)] + [whole()] * (len(turns) + len(before)) + [weight],
-            out_specs=whole(),
-            scratch_shapes=held(turns),
+            out_specs=[whole()] * (1 + len(after)),
+            scratch_shapes=held(turns + after),
             compiler_params=params(),
             name="grad_rows",
         )(at, *[grads[d] for d in turns], *before, out_weight)
 
     one_hop = tuple(d for d in range(1, cuts) if d != cuts // 2)
     far = (cuts // 2,)
-    first = grad_rows(one_hop, grad_rows((0,)))
+    (own_terms,) = grad_rows((0,), (), ())
 
     turns = homes // SERVERS
     own = (lax.axis_index("seq") // SERVERS).astype(jnp.int32).reshape(1)
@@ -384,7 +385,10 @@
     pieces = lax.all_to_all(
         sent.reshape(homes, served // 2 + 1, 2, HEAD_WIDTH), "seq", 0, 0, tiled=True
     ).reshape(turns * tall, HEAD_WIDTH)
-    pieces, first = lax.optimization_barrier((pieces, first))
+    pieces, own_terms, grads[1], grads[-1] = lax.optimization_barrier(
+        (pieces, own_terms, grads[1], grads[-1])
+    )
+    first, far_weight = grad_rows(one_hop, [own_terms], far)
     picked, meta = pl.pallas_call(
         functools.partial(
             select_kernel, per_prompt=per_prompt, servers=SERVERS, rows=served, turns=turns
@@ -406,14 +410,13 @@
     )(own, meta)
 
     d_rows, d_cols = pl.pallas_call(
-        functools.partial(grad_rows_end_kernel, turns=far, cuts=cuts),
+        grad_rows_end_kernel,
         out_shape=(shape(rows, width), shape(width, rows)),
-        in_specs=[whole(pltpu.SMEM)] * 2 + [whole()] * 2 + [weight],
+        in_specs=[whole(pltpu.SMEM)] + [whole()] * 3,
         out_specs=(whole(), whole()),
-        scratch_shapes=held(far),
         compiler_params=params(),
         name="grad_rows_end",
-    )(at, suffix_length, first, grads[cuts // 2], out_weight)
+    )(suffix_length, first, grads[cuts // 2], far_weight)
 
     gathered, home_map = lax.optimization_barrier((gathered, home_map))
     keys = prefix_keys.shape[0] * per_prompt + rows

time: 90.1 us -> 88.7 us (0.984)
  starting transfers between devices: 42 us -> 39.8 us
  waiting for transfers between devices: 21.8 us -> 23.8 us
  Pallas kernels: 21.2 us -> 20 us
    all_to_all x2, waiting for transfers between devices: 1.07 us -> 2.68 us  [swap(): return lax.all_to_all(x, 'seq', 0, 0, tiled=True, axis_index_groups=groups)]
    pallas_call x1, Pallas kernels: 1.92 us -> 0.6 us  [shards(): pl.pallas_call(grad_rows_end_kernel, out_shape=(shape(rows, width), shape...]
    all_to_all x2, starting transfers between devices: 9.88 us -> 8.65 us  [swap(): return lax.all_to_all(x, 'seq', 0, 0, tiled=True, axis_index_groups=groups)]
  transfers between devices with their start and end apart: 10 -> 10, of which waited for: 8 -> 9; matrix products, arithmetic and copies ran while one was open for 1% -> 1% of each run, Pallas kernels for 12% -> 11%
where the time goes in v7:
time: 88.7 us; the launch traced here: 88.1 us
  starting transfers between devices  39.8 us (45%)
  waiting for transfers between devices  23.8 us (27%)
  Pallas kernels  20 us (23%)
  between operations  2.77 us (3%)
  local copies, waits for them, and re-layouts  1.02 us (1%)
    all_to_all x1, starting transfers between devices, shards(): lax.all_to_all(sent.reshape(homes, served // 2 + 1, 2, HEAD_WIDTH), 'seq'...  13.2 us
    ppermute x6, waiting for transfers between devices, shards(): lax.ppermute(x, 'tensor', [(i, (i + d) % cuts) for i in range(cuts)])  10.9 us
    ppermute x6, starting transfers between devices, shards(): lax.ppermute(x, 'tensor', [(i, (i + d) % cuts) for i in range(cuts)])  10.5 us
    all_to_all x2, starting transfers between devices, swap(): return lax.all_to_all(x, 'seq', 0, 0, tiled=True, axis_index_groups=groups)  8.65 us
    all_to_all x1, starting transfers between devices, shards(): lax.all_to_all(sums.reshape(homes, served, HEAD_WIDTH), 'seq', 0, 0, tile...  7.46 us
    all_to_all x1, waiting for transfers between devices, shards(): lax.all_to_all(sums.reshape(homes, served, HEAD_WIDTH), 'seq', 0, 0, tile...  5.51 us
    pallas_call x1, Pallas kernels, shards(): pl.pallas_call(functools.partial(attention_kernel, scale=HEAD_WIDTH ** (-...  4.9 us
    all_to_all x1, waiting for transfers between devices, shards(): lax.all_to_all(sent.reshape(homes, served // 2 + 1, 2, HEAD_WIDTH), 'seq'...  4.75 us
  transfers between devices with their start and end apart: 10, of which 9 were waited for; matrix products, arithmetic and copies ran while one was open for 1% of the time, Pallas kernels for 11%

profile of v7, /device:TPU:1, one launch (start us, length us, event | category | flops | bytes accessed | tf_op | source)
XLA Modules:
  0.0 88.1 jit_solution(9953485113485333764)
XLA Ops:
  0.6 0.0 copy-start.1
  0.6 0.0 copy-start.4
  0.7 0.0 copy-start.3
  2.0 1.7 %pack.1 = bf16[1152,128]{1,0:T(8,128)(2,1)} custom-call(s32[1]{0:T(128)S(6)} %copy.19.block_ref, s32[1]{0:T(128)S(6)} %copy.20.rollout_ref, bf16[128,128]{1,0:T(8,128)(2,1)} %keys_hbm.1, bf16[128,128]{1,0:T(8,128)(2,1)} %values_hbm.1), custom_call_target="tpu_custom_call" | custom-call | tf_op jit(solution)/shard_map/pack/pallas_call | solution.py:372
  3.7 13.2 %all-to-all-start = ((bf16[64,9,2,128]{3,2,1,0:T(2,128)(2,1)}), bf16[64,9,2,128]{3,2,1,0:T(2,128)(2,1)S(1)}, u32[]{:S(2)}, u32[]{:S(2)}) async-start(bf16[64,9,2,128]{3,2,1,0:T(2,128)(2,1)} %bitcast.2), calls=%async_computation | async-start | bytes 589824 | tf_op jit(solution)/shard_map/all_to_all | solution.py:385
  16.9 2.6 %collective-permute-start = (bf16[128,640]{1,0:T(8,128)(2,1)}, bf16[128,640]{1,0:T(8,128)(2,1)S(1)}, u32[]{:S(2)}, u32[]{:S(2)}) collective-permute-start(bf16[128,640]{1,0:T(8,128)(2,1)} %refs_0_.1), channel_id=1, source_target_pairs={{0,3},{1,0},{2,1},{3,2},{4,7},{5,4},{6,5},{7,6},{8,11},{9,8},{10,9... | collective-permute-start | bytes 491528 | tf_op jit(solution)/shard_map/ppermute | solution.py:344
  19.4 0.0 collective-permute-start.1
  19.5 0.0 copy-start.2
  19.5 1.0 %copy-done.2 = bf16[128,640]{1,0:T(8,128)(2,1)S(1)} copy-done((bf16[128,640]{1,0:T(8,128)(2,1)S(1)}, bf16[128,640]{1,0:T(8,128)(2,1)}, u32[]{:S(2)}) %copy-start.2) | copy-done | bytes 163864
  20.4 1.8 %grad_rows.2.refs_2_ = f32[1024,128]{1,0:T(8,128)S(1)} custom-call(s32[1]{0:T(128)} %bitcast.at_ref, bf16[128,640]{1,0:T(8,128)(2,1)S(1)} %copy-done.2, bf16[1024,2560]{1,0:T(8,128)(2,1)} %w_ref.3), custom_call_target="tpu_custom_call" | custom-call | tf_op jit(solution)/shard_map/grad_rows/pallas_call | solution.py:356
  22.3 0.0 copy-start
  22.3 0.0 copy-start.6
  22.3 0.0 copy-start.7
  22.3 0.6 collective-permute-done.refs_0_
  22.9 3.0 %collective-permute-done.1.refs_1_ = bf16[128,640]{1,0:T(8,128)(2,1)S(1)} collective-permute-done((bf16[128,640]{1,0:T(8,128)(2,1)}, bf16[128,640]{1,0:T(8,128)(2,1)S(1)}, u32[]{:S(2)}, u32[]{:S(2)}) %collective-permute-start.1) | collective-permute-done | bytes 163872 | tf_op jit(solution)/shard_map/ppermute | solution.py:344
  25.9 4.7 %all-to-all-done = bf16[64,9,2,128]{3,2,1,0:T(2,128)(2,1)S(1)} async-done(((bf16[64,9,2,128]{3,2,1,0:T(2,128)(2,1)}), bf16[64,9,2,128]{3,2,1,0:T(2,128)(2,1)S(1)}, u32[]{:S(2)}, u32[]{:S(2)}) %all-to-all-start) | async-done | bytes 294944 | tf_op jit(solution)/shard_map/all_to_all | solution.py:385
  30.6 0.0 copy-done.1
  30.6 0.0 copy-done.4
  30.6 1.7 %select.5 = (bf16[16,128,128]{2,1,0:T(8,128)(2,1)}, bf16[64,128]{1,0:T(8,128)(2,1)S(1)}) custom-call(s32[1]{0:T(128)} %bitcast.1.own_ref, bf16[1152,128]{1,0:T(8,128)(2,1)S(1)} %bitcast.6, bf16[288,288]{1,0:T(8,128)(2,1)S(1)} %copy-done.1, bf16[64,1152]{1,0:T(8,128)(2,1)S(1)} %copy-done.4), custom_call_target="tpu_custom_call" | custom-call | tf_op jit(solution)/shard_map/select/pallas_call | solution.py:392
  32.3 4.1 %all-to-all-start.1 = ((bf16[16,128,128]{2,1,0:T(8,128)(2,1)}), bf16[16,128,128]{2,1,0:T(8,128)(2,1)S(1)}, u32[]{:S(2)}, u32[]{:S(2)}) async-start(bf16[16,128,128]{2,1,0:T(8,128)(2,1)} %get-tuple-element.31), calls=%async_computation.1 | async-start | bytes 1048576 | tf_op jit(solution)/shard_map/all_to_all | solution.py:342
  36.4 0.0 copy-done.3
  36.4 2.9 %collective-permute-start.2 = (bf16[128,640]{1,0:T(8,128)(2,1)S(1)}, bf16[128,640]{1,0:T(8,128)(2,1)S(1)}, u32[]{:S(2)}, u32[]{:S(2)}) collective-permute-start(bf16[128,640]{1,0:T(8,128)(2,1)S(1)} %copy-done.3), channel_id=1, source_target_pairs={{0,2},{1,3},{2,0},{3,1},{4,6},{5,7},{6,4},{7,5},{8,10},{9,11},{10,... | collective-permute-start | bytes 491528 | tf_op jit(solution)/shard_map/ppermute | solution.py:344
  39.9 0.2 home_map.1.map_ref
  40.2 2.8 %grad_rows.3 = (f32[1024,128]{1,0:T(8,128)S(1)}, bf16[1024,640]{1,0:T(8,128)(2,1)S(1)}) custom-call(s32[1]{0:T(128)} %bitcast.at_ref, bf16[128,640]{1,0:T(8,128)(2,1)S(1)} %collective-permute-done.refs_0_, bf16[128,640]{1,0:T(8,128)(2,1)S(1)} %collective-permute-done.1.refs_1_, f32[1024,128]{1,0:T(8,128)S(1)} %grad_rows.2.refs_2_, bf16[1024,2560]{1,0:T(8,128)(2,1)} %w_ref.3), custom_call_target="tpu_custom_call" | custom-call | tf_op jit(solution)/shard_map/grad_rows/pallas_call | solution.py:356
  43.0 0.7 collective-permute-done.2.g_ref
  43.8 0.6 grad_rows_end.1
  44.4 1.8 %all-to-all-done.1.g_ref = bf16[16,128,128]{2,1,0:T(8,128)(2,1)S(1)} async-done(((bf16[16,128,128]{2,1,0:T(8,128)(2,1)}), bf16[16,128,128]{2,1,0:T(8,128)(2,1)S(1)}, u32[]{:S(2)}, u32[]{:S(2)}) %all-to-all-start.1) | async-done | bytes 524320 | tf_op jit(solution)/shard_map/all_to_all | solution.py:342
  46.2 0.0 copy-done
  46.2 0.0 copy-done.6
  46.2 0.0 copy-done.7
  46.2 4.9 %attention.1 = (bf16[128,1024]{1,0:T(8,128)(2,1)S(1)}, bf16[128,1024]{1,0:T(8,128)(2,1)}, bf16[128,128]{1,0:T(8,128)(2,1)}, bf16[128,128]{1,0:T(8,128)(2,1)}, bf16[16,128,128]{2,1,0:T(8,128)(2,1)}) custom-call(s32[1]{0:T(128)S(6)} %copy.21.len_ref, bf16[128,1024]{1,0:T(8,128)(2,1)S(1)} %copy-done, bf16[128,128]{1,0:T(8,128)(2,1)S(1)} %copy-done.6, ...), custom_call_target="tpu_custom_call" | custom-call | tf_op jit(solution)/shard_map/attention/pallas_call | solution.py:423
  51.1 4.5 %all-to-all-start.2 = ((bf16[16,128,128]{2,1,0:T(8,128)(2,1)}), bf16[16,128,128]{2,1,0:T(8,128)(2,1)S(1)}, u32[]{:S(2)}, u32[]{:S(2)}) async-start(bf16[16,128,128]{2,1,0:T(8,128)(2,1)} %get-tuple-element.50), calls=%async_computation.2 | async-start | bytes 1048576 | tf_op jit(solution)/shard_map/all_to_all | solution.py:342
  55.7 0.0 copy-start.5
  55.7 2.2 %project.3 = (bf16[128,640]{1,0:T(8,128)(2,1)S(1)}, bf16[128,640]{1,0:T(8,128)(2,1)S(1)}) custom-call(s32[1]{0:T(128)} %bitcast.at_ref, bf16[128,1024]{1,0:T(8,128)(2,1)S(1)} %get-tuple-element.41.a_ref, bf16[1024,2560]{1,0:T(8,128)(2,1)} %w_ref.3), custom_call_target="tpu_custom_call" | custom-call | tf_op jit(solution)/shard_map/project/pallas_call | solution.py:445
  57.8 1.3 %collective-permute-start.3 = (bf16[128,640]{1,0:T(8,128)(2,1)S(1)}, bf16[128,640]{1,0:T(8,128)(2,1)S(1)}, u32[]{:S(2)}, u32[]{:S(2)}) collective-permute-start(bf16[128,640]{1,0:T(8,128)(2,1)S(1)} %get-tuple-element.43), channel_id=1, source_target_pairs={{0,1},{1,2},{2,3},{3,0},{4,5},{5,6},{6,7},{7,4},{8,9},{9,10},{10,1... | collective-permute-start | bytes 491528 | tf_op jit(solution)/shard_map/ppermute | solution.py:344
  59.1 1.6 %collective-permute-start.4 = (bf16[128,640]{1,0:T(8,128)(2,1)S(1)}, bf16[128,640]{1,0:T(8,128)(2,1)S(1)}, u32[]{:S(2)}, u32[]{:S(2)}) collective-permute-start(bf16[128,640]{1,0:T(8,128)(2,1)S(1)} %get-tuple-element.44), channel_id=1, source_target_pairs={{0,3},{1,0},{2,1},{3,2},{4,7},{5,4},{6,5},{7,6},{8,11},{9,8},{10,9... | collective-permute-start | bytes 491528 | tf_op jit(solution)/shard_map/ppermute | solution.py:344
  60.7 2.1 %project.2 = (bf16[128,640]{1,0:T(8,128)(2,1)S(1)}, f32[128,640]{1,0:T(8,128)S(1)}) custom-call(s32[1]{0:T(128)} %bitcast.at_ref, bf16[128,1024]{1,0:T(8,128)(2,1)S(1)} %get-tuple-element.41.a_ref, bf16[1024,2560]{1,0:T(8,128)(2,1)} %w_ref.3), custom_call_target="tpu_custom_call" | custom-call | tf_op jit(solution)/shard_map/project/pallas_call | solution.py:445
  62.8 1.9 %collective-permute-done.3 = bf16[128,640]{1,0:T(8,128)(2,1)S(1)} collective-permute-done((bf16[128,640]{1,0:T(8,128)(2,1)S(1)}, bf16[128,640]{1,0:T(8,128)(2,1)S(1)}, u32[]{:S(2)}, u32[]{:S(2)}) %collective-permute-start.3) | collective-permute-done | bytes 163872 | tf_op jit(solution)/shard_map/ppermute | solution.py:344
  64.7 0.0 collective-permute-done.4
  64.7 0.8 all-to-all-done.2.terms_ref
  65.5 0.0 copy-done.5
  65.5 1.3 %combine.1 = bf16[1024,128]{1,0:T(8,128)(2,1)} custom-call(bf16[128,256]{1,0:T(8,128)(2,1)S(1)} %home_map.1.map_ref, bf16[16,128,128]{2,1,0:T(8,128)(2,1)S(1)} %all-to-all-done.2.terms_ref, bf16[256,256]{1,0:T(8,128)(2,1)S(1)} %copy-done.5), custom_call_target="tpu_custom_call" | custom-call | tf_op jit(solution)/shard_map/combine/pallas_call | solution.py:462
  66.8 7.5 %all-to-all-start.3 = ((bf16[64,16,128]{2,1,0:T(8,128)(2,1)}), bf16[64,16,128]{2,1,0:T(8,128)(2,1)S(1)}, u32[]{:S(2)}, u32[]{:S(2)}) async-start(bf16[64,16,128]{2,1,0:T(8,128)(2,1)} %bitcast.4), calls=%async_computation.3 | async-start | bytes 524288 | tf_op jit(solution)/shard_map/all_to_all | solution.py:470
  74.3 2.2 %collective-permute-start.5 = (bf16[128,640]{1,0:T(8,128)(2,1)S(1)}, bf16[128,640]{1,0:T(8,128)(2,1)S(1)}, u32[]{:S(2)}, u32[]{:S(2)}) collective-permute-start(bf16[128,640]{1,0:T(8,128)(2,1)S(1)} %get-tuple-element.45), channel_id=1, source_target_pairs={{0,2},{1,3},{2,0},{3,1},{4,6},{5,7},{6,4},{7,5},{8,10},{9,11},{10,... | collective-permute-start | bytes 491528 | tf_op jit(solution)/shard_map/ppermute | solution.py:344
  76.5 4.7 %collective-permute-done.5 = bf16[128,640]{1,0:T(8,128)(2,1)S(1)} collective-permute-done((bf16[128,640]{1,0:T(8,128)(2,1)S(1)}, bf16[128,640]{1,0:T(8,128)(2,1)S(1)}, u32[]{:S(2)}, u32[]{:S(2)}) %collective-permute-start.5) | collective-permute-done | bytes 163872 | tf_op jit(solution)/shard_map/ppermute | solution.py:344
  81.2 0.7 add_convert_fusion
  81.9 5.5 %all-to-all-done.3 = bf16[64,16,128]{2,1,0:T(8,128)(2,1)S(1)} async-done(((bf16[64,16,128]{2,1,0:T(8,128)(2,1)}), bf16[64,16,128]{2,1,0:T(8,128)(2,1)S(1)}, u32[]{:S(2)}, u32[]{:S(2)}) %all-to-all-start.3) | async-done | bytes 262176 | tf_op jit(solution)/shard_map/all_to_all | solution.py:470
  87.4 0.7 home_sum.1
Async XLA Ops:
  0.6 30.0 %copy-start.1 = (bf16[288,288]{1,0:T(8,128)(2,1)S(1)}, bf16[288,288]{1,0:T(8,128)(2,1)}, u32[]{:S(2)}) copy-start(bf16[288,288]{1,0:T(8,128)(2,1)} %constant.31.clone.swap_ref) | copy-start | bytes 497668
  0.6 30.0 %copy-start.4 = (bf16[64,1152]{1,0:T(8,128)(2,1)S(1)}, bf16[64,1152]{1,0:T(8,128)(2,1)}, u32[]{:S(2)}) copy-start(bf16[64,1152]{1,0:T(8,128)(2,1)} %constant.32.clone.take_ref) | copy-start | bytes 442372
  0.7 35.8 %copy-start.3 = (bf16[128,640]{1,0:T(8,128)(2,1)S(1)}, bf16[128,640]{1,0:T(8,128)(2,1)}, u32[]{:S(2)}) copy-start(bf16[128,640]{1,0:T(8,128)(2,1)} %refs_0_.1) | copy-start | bytes 491524
  3.7 26.9 %all-to-all-start = ((bf16[64,9,2,128]{3,2,1,0:T(2,128)(2,1)}), bf16[64,9,2,128]{3,2,1,0:T(2,128)(2,1)S(1)}, u32[]{:S(2)}, u32[]{:S(2)}) async-start(bf16[64,9,2,128]{3,2,1,0:T(2,128)(2,1)} %bitcast.2), calls=%async_computation | async-start | bytes 589824 | tf_op jit(solution)/shard_map/all_to_all | solution.py:385
  16.9 6.0 %collective-permute-start = (bf16[128,640]{1,0:T(8,128)(2,1)}, bf16[128,640]{1,0:T(8,128)(2,1)S(1)}, u32[]{:S(2)}, u32[]{:S(2)}) collective-permute-start(bf16[128,640]{1,0:T(8,128)(2,1)} %refs_0_.1), channel_id=1, source_target_pairs={{0,3},{1,0},{2,1},{3,2},{4,7},{5,4},{6,5},{7,6},{8,11},{9,8},{10,9... | collective-permute-start | bytes 491528 | tf_op jit(solution)/shard_map/ppermute | solution.py:344
  19.4 6.4 %collective-permute-start.1 = (bf16[128,640]{1,0:T(8,128)(2,1)}, bf16[128,640]{1,0:T(8,128)(2,1)S(1)}, u32[]{:S(2)}, u32[]{:S(2)}) collective-permute-start(bf16[128,640]{1,0:T(8,128)(2,1)} %refs_0_.1), channel_id=1, source_target_pairs={{0,1},{1,2},{2,3},{3,0},{4,5},{5,6},{6,7},{7,4},{8,9},{9,10},{10,1... | collective-permute-start | bytes 491528 | tf_op jit(solution)/shard_map/ppermute | solution.py:344
  19.5 1.0 %copy-start.2 = (bf16[128,640]{1,0:T(8,128)(2,1)S(1)}, bf16[128,640]{1,0:T(8,128)(2,1)}, u32[]{:S(2)}) copy-start(bf16[128,640]{1,0:T(8,128)(2,1)} %refs_0_.1) | copy-start | bytes 491524
  22.3 24.0 %copy-start = (bf16[128,1024]{1,0:T(8,128)(2,1)S(1)}, bf16[128,1024]{1,0:T(8,128)(2,1)}, u32[]{:S(2)}) copy-start(bf16[128,1024]{1,0:T(8,128)(2,1)} %q_ref.1) | copy-start | bytes 786436
  22.3 23.9 %copy-start.6 = (bf16[128,128]{1,0:T(8,128)(2,1)S(1)}, bf16[128,128]{1,0:T(8,128)(2,1)}, u32[]{:S(2)}) copy-start(bf16[128,128]{1,0:T(8,128)(2,1)} %ks_ref.1) | copy-start | bytes 98308
  22.3 23.9 %copy-start.7 = (bf16[128,128]{1,0:T(8,128)(2,1)S(1)}, bf16[128,128]{1,0:T(8,128)(2,1)}, u32[]{:S(2)}) copy-start(bf16[128,128]{1,0:T(8,128)(2,1)} %vs_ref.1) | copy-start | bytes 98308
  32.3 13.9 %all-to-all-start.1 = ((bf16[16,128,128]{2,1,0:T(8,128)(2,1)}), bf16[16,128,128]{2,1,0:T(8,128)(2,1)S(1)}, u32[]{:S(2)}, u32[]{:S(2)}) async-start(bf16[16,128,128]{2,1,0:T(8,128)(2,1)} %get-tuple-element.31), calls=%async_computation.1 | async-start | bytes 1048576 | tf_op jit(solution)/shard_map/all_to_all | solution.py:342
  36.4 7.4 %collective-permute-start.2 = (bf16[128,640]{1,0:T(8,128)(2,1)S(1)}, bf16[128,640]{1,0:T(8,128)(2,1)S(1)}, u32[]{:S(2)}, u32[]{:S(2)}) collective-permute-start(bf16[128,640]{1,0:T(8,128)(2,1)S(1)} %copy-done.3), channel_id=1, source_target_pairs={{0,2},{1,3},{2,0},{3,1},{4,6},{5,7},{6,4},{7,5},{8,10},{9,11},{10,... | collective-permute-start | bytes 491528 | tf_op jit(solution)/shard_map/ppermute | solution.py:344
  51.1 14.4 %all-to-all-start.2 = ((bf16[16,128,128]{2,1,0:T(8,128)(2,1)}), bf16[16,128,128]{2,1,0:T(8,128)(2,1)S(1)}, u32[]{:S(2)}, u32[]{:S(2)}) async-start(bf16[16,128,128]{2,1,0:T(8,128)(2,1)} %get-tuple-element.50), calls=%async_computation.2 | async-start | bytes 1048576 | tf_op jit(solution)/shard_map/all_to_all | solution.py:342
  55.7 9.9 %copy-start.5 = (bf16[256,256]{1,0:T(8,128)(2,1)S(1)}, bf16[256,256]{1,0:T(8,128)(2,1)}, u32[]{:S(2)}) copy-start(bf16[256,256]{1,0:T(8,128)(2,1)} %constant.33.clone.swap_ref) | copy-start | bytes 393220
  57.8 6.9 %collective-permute-start.3 = (bf16[128,640]{1,0:T(8,128)(2,1)S(1)}, bf16[128,640]{1,0:T(8,128)(2,1)S(1)}, u32[]{:S(2)}, u32[]{:S(2)}) collective-permute-start(bf16[128,640]{1,0:T(8,128)(2,1)S(1)} %get-tuple-element.43), channel_id=1, source_target_pairs={{0,1},{1,2},{2,3},{3,0},{4,5},{5,6},{6,7},{7,4},{8,9},{9,10},{10,1... | collective-permute-start | bytes 491528 | tf_op jit(solution)/shard_map/ppermute | solution.py:344
  59.1 5.6 %collective-permute-start.4 = (bf16[128,640]{1,0:T(8,128)(2,1)S(1)}, bf16[128,640]{1,0:T(8,128)(2,1)S(1)}, u32[]{:S(2)}, u32[]{:S(2)}) collective-permute-start(bf16[128,640]{1,0:T(8,128)(2,1)S(1)} %get-tuple-element.44), channel_id=1, source_target_pairs={{0,3},{1,0},{2,1},{3,2},{4,7},{5,4},{6,5},{7,6},{8,11},{9,8},{10,9... | collective-permute-start | bytes 491528 | tf_op jit(solution)/shard_map/ppermute | solution.py:344
  66.8 20.6 %all-to-all-start.3 = ((bf16[64,16,128]{2,1,0:T(8,128)(2,1)}), bf16[64,16,128]{2,1,0:T(8,128)(2,1)S(1)}, u32[]{:S(2)}, u32[]{:S(2)}) async-start(bf16[64,16,128]{2,1,0:T(8,128)(2,1)} %bitcast.4), calls=%async_computation.3 | async-start | bytes 524288 | tf_op jit(solution)/shard_map/all_to_all | solution.py:470
  74.3 6.9 %collective-permute-start.5 = (bf16[128,640]{1,0:T(8,128)(2,1)S(1)}, bf16[128,640]{1,0:T(8,128)(2,1)S(1)}, u32[]{:S(2)}, u32[]{:S(2)}) collective-permute-start(bf16[128,640]{1,0:T(8,128)(2,1)S(1)} %get-tuple-element.45), channel_id=1, source_target_pairs={{0,2},{1,3},{2,0},{3,1},{4,6},{5,7},{6,4},{7,5},{8,10},{9,11},{10,... | collective-permute-start | bytes 491528 | tf_op jit(solution)/shard_map/ppermute | solution.py:344

commit v8 on v7

--- a/solution.py
+++ b/solution.py
@@ -342,7 +342,8 @@
         return lax.all_to_all(x, "seq", 0, 0, tiled=True, axis_index_groups=groups)
 
     turn = lambda x, d: lax.ppermute(x, "tensor", [(i, (i + d) % cuts) for i in range(cuts)])
-    grads = [out_grad] + [turn(out_grad, cuts - d) for d in range(1, cuts)]
+    grads = [turn(out_grad, cuts - d) for d in range(cuts - 1, 0, -1)]
+    grads = [out_grad] + grads[::-1]
     weight = whole(pltpu.HBM)
     out_weight = in_hbm(out_weight)
 
@@ -385,8 +386,8 @@
     pieces = lax.all_to_all(
         sent.reshape(homes, served // 2 + 1, 2, HEAD_WIDTH), "seq", 0, 0, tiled=True
     ).reshape(turns * tall, HEAD_WIDTH)
-    pieces, own_terms, grads[1], grads[-1] = lax.optimization_barrier(
-        (pieces, own_terms, grads[1], grads[-1])
+    pieces, own_terms, grads[-1], grads[1] = lax.optimization_barrier(
+        (pieces, own_terms, grads[-1], grads[1])
     )
     first, far_weight = grad_rows(one_hop, [own_terms], far)
     picked, meta = pl.pallas_call(

time: 88.7 us -> 88.4 us (level)
    ppermute x6, waiting for transfers between devices: 10.9 us -> 8.25 us  [shards(): lax.ppermute(x, 'tensor', [(i, (i + d) % cuts) for i in range(cuts)])]
    all_to_all x1, waiting for transfers between devices: 4.75 us -> 6.9 us  [shards(): lax.all_to_all(sent.reshape(homes, served // 2 + 1, 2, HEAD_WIDTH), 'seq'...]
  transfers between devices with their start and end apart: 10 -> 10, of which waited for: 9 -> 8; matrix products, arithmetic and copies ran while one was open for 1% -> 1% of each run, Pallas kernels for 11% -> 11%
where the time goes in v8:
time: 88.4 us; the launch traced here: 87.8 us
  starting transfers between devices  40 us (45%)
  waiting for transfers between devices  23.3 us (26%)
  Pallas kernels  20 us (23%)
  between operations  2.77 us (3%)
  local copies, waits for them, and re-layouts  0.99 us (1%)
    all_to_all x1, starting transfers between devices, shards(): lax.all_to_all(sent.reshape(homes, served // 2 + 1, 2, HEAD_WIDTH), 'seq'...  13.2 us
    ppermute x6, starting transfers between devices, shards(): lax.ppermute(x, 'tensor', [(i, (i + d) % cuts) for i in range(cuts)])  11 us
    all_to_all x2, starting transfers between devices, swap(): return lax.all_to_all(x, 'seq', 0, 0, tiled=True, axis_index_groups=groups)  8.65 us
    ppermute x6, waiting for transfers between devices, shards(): lax.ppermute(x, 'tensor', [(i, (i + d) % cuts) for i in range(cuts)])  8.25 us
    all_to_all x1, starting transfers between devices, shards(): lax.all_to_all(sums.reshape(homes, served, HEAD_WIDTH), 'seq', 0, 0, tile...  7.16 us
    all_to_all x1, waiting for transfers between devices, shards(): lax.all_to_all(sent.reshape(homes, served // 2 + 1, 2, HEAD_WIDTH), 'seq'...  6.9 us
    all_to_all x1, waiting for transfers between devices, shards(): lax.all_to_all(sums.reshape(homes, served, HEAD_WIDTH), 'seq', 0, 0, tile...  5.51 us
    pallas_call x1, Pallas kernels, shards(): pl.pallas_call(functools.partial(attention_kernel, scale=HEAD_WIDTH ** (-...  4.9 us
  transfers between devices with their start and end apart: 10, of which 8 were waited for; matrix products, arithmetic and copies ran while one was open for 1% of the time, Pallas kernels for 11%

profile of v8, /device:TPU:1, one launch (start us, length us, event | category | flops | bytes accessed | tf_op | source)
XLA Modules:
  0.0 87.8 jit_solution(7469208005241216969)
XLA Ops:
  0.6 0.0 copy-start.1
  0.6 0.0 copy-start.4
  0.7 0.0 copy-start.3
  2.0 1.7 %pack.1 = bf16[1152,128]{1,0:T(8,128)(2,1)} custom-call(s32[1]{0:T(128)S(6)} %copy.19.block_ref, s32[1]{0:T(128)S(6)} %copy.20.rollout_ref, bf16[128,128]{1,0:T(8,128)(2,1)} %keys_hbm.1, bf16[128,128]{1,0:T(8,128)(2,1)} %values_hbm.1), custom_call_target="tpu_custom_call" | custom-call | tf_op jit(solution)/shard_map/pack/pallas_call | solution.py:373
  3.7 13.2 %all-to-all-start = ((bf16[64,9,2,128]{3,2,1,0:T(2,128)(2,1)}), bf16[64,9,2,128]{3,2,1,0:T(2,128)(2,1)S(1)}, u32[]{:S(2)}, u32[]{:S(2)}) async-start(bf16[64,9,2,128]{3,2,1,0:T(2,128)(2,1)} %bitcast.2), calls=%async_computation | async-start | bytes 589824 | tf_op jit(solution)/shard_map/all_to_all | solution.py:386
  16.9 1.3 %collective-permute-start = (bf16[128,640]{1,0:T(8,128)(2,1)}, bf16[128,640]{1,0:T(8,128)(2,1)S(1)}, u32[]{:S(2)}, u32[]{:S(2)}) collective-permute-start(bf16[128,640]{1,0:T(8,128)(2,1)} %refs_0_.1), channel_id=1, source_target_pairs={{0,1},{1,2},{2,3},{3,0},{4,5},{5,6},{6,7},{7,4},{8,9},{9,10},{10,1... | collective-permute-start | bytes 491528 | tf_op jit(solution)/shard_map/ppermute | solution.py:344
  18.2 1.5 %collective-permute-start.1 = (bf16[128,640]{1,0:T(8,128)(2,1)}, bf16[128,640]{1,0:T(8,128)(2,1)S(1)}, u32[]{:S(2)}, u32[]{:S(2)}) collective-permute-start(bf16[128,640]{1,0:T(8,128)(2,1)} %refs_0_.1), channel_id=1, source_target_pairs={{0,3},{1,0},{2,1},{3,2},{4,7},{5,4},{6,5},{7,6},{8,11},{9,8},{10,9... | collective-permute-start | bytes 491528 | tf_op jit(solution)/shard_map/ppermute | solution.py:344
  19.6 0.0 copy-start.2
  19.7 0.9 %copy-done.2 = bf16[128,640]{1,0:T(8,128)(2,1)S(1)} copy-done((bf16[128,640]{1,0:T(8,128)(2,1)S(1)}, bf16[128,640]{1,0:T(8,128)(2,1)}, u32[]{:S(2)}) %copy-start.2) | copy-done | bytes 163864
  20.6 1.8 %grad_rows.2.refs_2_ = f32[1024,128]{1,0:T(8,128)S(1)} custom-call(s32[1]{0:T(128)} %bitcast.at_ref, bf16[128,640]{1,0:T(8,128)(2,1)S(1)} %copy-done.2, bf16[1024,2560]{1,0:T(8,128)(2,1)} %w_ref.3), custom_call_target="tpu_custom_call" | custom-call | tf_op jit(solution)/shard_map/grad_rows/pallas_call | solution.py:357
  22.4 0.0 copy-start
  22.5 0.0 copy-start.6
  22.5 0.0 copy-start.7
  22.5 1.2 %collective-permute-done.refs_1_ = bf16[128,640]{1,0:T(8,128)(2,1)S(1)} collective-permute-done((bf16[128,640]{1,0:T(8,128)(2,1)}, bf16[128,640]{1,0:T(8,128)(2,1)S(1)}, u32[]{:S(2)}, u32[]{:S(2)}) %collective-permute-start) | collective-permute-done | bytes 163872 | tf_op jit(solution)/shard_map/ppermute | solution.py:344
  23.7 0.0 collective-permute-done.1.refs_0_
  23.7 6.9 %all-to-all-done = bf16[64,9,2,128]{3,2,1,0:T(2,128)(2,1)S(1)} async-done(((bf16[64,9,2,128]{3,2,1,0:T(2,128)(2,1)}), bf16[64,9,2,128]{3,2,1,0:T(2,128)(2,1)S(1)}, u32[]{:S(2)}, u32[]{:S(2)}) %all-to-all-start) | async-done | bytes 294944 | tf_op jit(solution)/shard_map/all_to_all | solution.py:386
  30.6 0.0 copy-done.1
  30.6 0.0 copy-done.4
  30.6 1.7 %select.5 = (bf16[16,128,128]{2,1,0:T(8,128)(2,1)}, bf16[64,128]{1,0:T(8,128)(2,1)S(1)}) custom-call(s32[1]{0:T(128)} %bitcast.1.own_ref, bf16[1152,128]{1,0:T(8,128)(2,1)S(1)} %bitcast.6, bf16[288,288]{1,0:T(8,128)(2,1)S(1)} %copy-done.1, bf16[64,1152]{1,0:T(8,128)(2,1)S(1)} %copy-done.4), custom_call_target="tpu_custom_call" | custom-call | tf_op jit(solution)/shard_map/select/pallas_call | solution.py:393
  32.3 4.1 %all-to-all-start.1 = ((bf16[16,128,128]{2,1,0:T(8,128)(2,1)}), bf16[16,128,128]{2,1,0:T(8,128)(2,1)S(1)}, u32[]{:S(2)}, u32[]{:S(2)}) async-start(bf16[16,128,128]{2,1,0:T(8,128)(2,1)} %get-tuple-element.31), calls=%async_computation.1 | async-start | bytes 1048576 | tf_op jit(solution)/shard_map/all_to_all | solution.py:342
  36.4 0.0 copy-done.3
  36.4 2.9 %collective-permute-start.2 = (bf16[128,640]{1,0:T(8,128)(2,1)S(1)}, bf16[128,640]{1,0:T(8,128)(2,1)S(1)}, u32[]{:S(2)}, u32[]{:S(2)}) collective-permute-start(bf16[128,640]{1,0:T(8,128)(2,1)S(1)} %copy-done.3), channel_id=1, source_target_pairs={{0,2},{1,3},{2,0},{3,1},{4,6},{5,7},{6,4},{7,5},{8,10},{9,11},{10,... | collective-permute-start | bytes 491528 | tf_op jit(solution)/shard_map/ppermute | solution.py:344
  39.9 0.2 home_map.1.map_ref
  40.2 2.8 %grad_rows.3 = (f32[1024,128]{1,0:T(8,128)S(1)}, bf16[1024,640]{1,0:T(8,128)(2,1)S(1)}) custom-call(s32[1]{0:T(128)} %bitcast.at_ref, bf16[128,640]{1,0:T(8,128)(2,1)S(1)} %collective-permute-done.1.refs_0_, bf16[128,640]{1,0:T(8,128)(2,1)S(1)} %collective-permute-done.refs_1_, f32[1024,128]{1,0:T(8,128)S(1)} %grad_rows.2.refs_2_, bf16[1024,2560]{1,0:T(8,128)(2,1)} %w_ref.3), custom_call_target="tpu_custom_call" | custom-call | tf_op jit(solution)/shard_map/grad_rows/pallas_call | solution.py:357
  43.0 0.7 collective-permute-done.2.g_ref
  43.8 0.6 grad_rows_end.1
  44.4 1.8 %all-to-all-done.1.g_ref = bf16[16,128,128]{2,1,0:T(8,128)(2,1)S(1)} async-done(((bf16[16,128,128]{2,1,0:T(8,128)(2,1)}), bf16[16,128,128]{2,1,0:T(8,128)(2,1)S(1)}, u32[]{:S(2)}, u32[]{:S(2)}) %all-to-all-start.1) | async-done | bytes 524320 | tf_op jit(solution)/shard_map/all_to_all | solution.py:342
  46.2 0.0 copy-done
  46.2 0.0 copy-done.6
  46.2 0.0 copy-done.7
  46.2 4.9 %attention.1 = (bf16[128,1024]{1,0:T(8,128)(2,1)S(1)}, bf16[128,1024]{1,0:T(8,128)(2,1)}, bf16[128,128]{1,0:T(8,128)(2,1)}, bf16[128,128]{1,0:T(8,128)(2,1)}, bf16[16,128,128]{2,1,0:T(8,128)(2,1)}) custom-call(s32[1]{0:T(128)S(6)} %copy.21.len_ref, bf16[128,1024]{1,0:T(8,128)(2,1)S(1)} %copy-done, bf16[128,128]{1,0:T(8,128)(2,1)S(1)} %copy-done.6, ...), custom_call_target="tpu_custom_call" | custom-call | tf_op jit(solution)/shard_map/attention/pallas_call | solution.py:424
  51.1 4.5 %all-to-all-start.2 = ((bf16[16,128,128]{2,1,0:T(8,128)(2,1)}), bf16[16,128,128]{2,1,0:T(8,128)(2,1)S(1)}, u32[]{:S(2)}, u32[]{:S(2)}) async-start(bf16[16,128,128]{2,1,0:T(8,128)(2,1)} %get-tuple-element.50), calls=%async_computation.2 | async-start | bytes 1048576 | tf_op jit(solution)/shard_map/all_to_all | solution.py:342
  55.7 0.0 copy-start.5
  55.7 2.2 %project.3 = (bf16[128,640]{1,0:T(8,128)(2,1)S(1)}, bf16[128,640]{1,0:T(8,128)(2,1)S(1)}) custom-call(s32[1]{0:T(128)} %bitcast.at_ref, bf16[128,1024]{1,0:T(8,128)(2,1)S(1)} %get-tuple-element.41.a_ref, bf16[1024,2560]{1,0:T(8,128)(2,1)} %w_ref.3), custom_call_target="tpu_custom_call" | custom-call | tf_op jit(solution)/shard_map/project/pallas_call | solution.py:446
  57.8 1.3 %collective-permute-start.3 = (bf16[128,640]{1,0:T(8,128)(2,1)S(1)}, bf16[128,640]{1,0:T(8,128)(2,1)S(1)}, u32[]{:S(2)}, u32[]{:S(2)}) collective-permute-start(bf16[128,640]{1,0:T(8,128)(2,1)S(1)} %get-tuple-element.43), channel_id=1, source_target_pairs={{0,1},{1,2},{2,3},{3,0},{4,5},{5,6},{6,7},{7,4},{8,9},{9,10},{10,1... | collective-permute-start | bytes 491528 | tf_op jit(solution)/shard_map/ppermute | solution.py:344
  59.1 1.6 %collective-permute-start.4 = (bf16[128,640]{1,0:T(8,128)(2,1)S(1)}, bf16[128,640]{1,0:T(8,128)(2,1)S(1)}, u32[]{:S(2)}, u32[]{:S(2)}) collective-permute-start(bf16[128,640]{1,0:T(8,128)(2,1)S(1)} %get-tuple-element.44), channel_id=1, source_target_pairs={{0,3},{1,0},{2,1},{3,2},{4,7},{5,4},{6,5},{7,6},{8,11},{9,8},{10,9... | collective-permute-start | bytes 491528 | tf_op jit(solution)/shard_map/ppermute | solution.py:344
  60.7 2.1 %project.2 = (bf16[128,640]{1,0:T(8,128)(2,1)S(1)}, f32[128,640]{1,0:T(8,128)S(1)}) custom-call(s32[1]{0:T(128)} %bitcast.at_ref, bf16[128,1024]{1,0:T(8,128)(2,1)S(1)} %get-tuple-element.41.a_ref, bf16[1024,2560]{1,0:T(8,128)(2,1)} %w_ref.3), custom_call_target="tpu_custom_call" | custom-call | tf_op jit(solution)/shard_map/project/pallas_call | solution.py:446
  62.8 1.9 %collective-permute-done.3 = bf16[128,640]{1,0:T(8,128)(2,1)S(1)} collective-permute-done((bf16[128,640]{1,0:T(8,128)(2,1)S(1)}, bf16[128,640]{1,0:T(8,128)(2,1)S(1)}, u32[]{:S(2)}, u32[]{:S(2)}) %collective-permute-start.3) | collective-permute-done | bytes 163872 | tf_op jit(solution)/shard_map/ppermute | solution.py:344
  64.7 0.0 collective-permute-done.4
  64.7 0.8 all-to-all-done.2.terms_ref
  65.5 0.0 copy-done.5
  65.5 1.3 %combine.1 = bf16[1024,128]{1,0:T(8,128)(2,1)} custom-call(bf16[128,256]{1,0:T(8,128)(2,1)S(1)} %home_map.1.map_ref, bf16[16,128,128]{2,1,0:T(8,128)(2,1)S(1)} %all-to-all-done.2.terms_ref, bf16[256,256]{1,0:T(8,128)(2,1)S(1)} %copy-done.5), custom_call_target="tpu_custom_call" | custom-call | tf_op jit(solution)/shard_map/combine/pallas_call | solution.py:463
  66.8 7.2 %all-to-all-start.3 = ((bf16[64,16,128]{2,1,0:T(8,128)(2,1)}), bf16[64,16,128]{2,1,0:T(8,128)(2,1)S(1)}, u32[]{:S(2)}, u32[]{:S(2)}) async-start(bf16[64,16,128]{2,1,0:T(8,128)(2,1)} %bitcast.4), calls=%async_computation.3 | async-start | bytes 524288 | tf_op jit(solution)/shard_map/all_to_all | solution.py:471
  74.0 2.5 %collective-permute-start.5 = (bf16[128,640]{1,0:T(8,128)(2,1)S(1)}, bf16[128,640]{1,0:T(8,128)(2,1)S(1)}, u32[]{:S(2)}, u32[]{:S(2)}) collective-permute-start(bf16[128,640]{1,0:T(8,128)(2,1)S(1)} %get-tuple-element.45), channel_id=1, source_target_pairs={{0,2},{1,3},{2,0},{3,1},{4,6},{5,7},{6,4},{7,5},{8,10},{9,11},{10,... | collective-permute-start | bytes 491528 | tf_op jit(solution)/shard_map/ppermute | solution.py:344
  76.5 4.4 %collective-permute-done.5 = bf16[128,640]{1,0:T(8,128)(2,1)S(1)} collective-permute-done((bf16[128,640]{1,0:T(8,128)(2,1)S(1)}, bf16[128,640]{1,0:T(8,128)(2,1)S(1)}, u32[]{:S(2)}, u32[]{:S(2)}) %collective-permute-start.5) | collective-permute-done | bytes 163872 | tf_op jit(solution)/shard_map/ppermute | solution.py:344
  80.9 0.7 add_convert_fusion
  81.6 5.5 %all-to-all-done.3 = bf16[64,16,128]{2,1,0:T(8,128)(2,1)S(1)} async-done(((bf16[64,16,128]{2,1,0:T(8,128)(2,1)}), bf16[64,16,128]{2,1,0:T(8,128)(2,1)S(1)}, u32[]{:S(2)}, u32[]{:S(2)}) %all-to-all-start.3) | async-done | bytes 262176 | tf_op jit(solution)/shard_map/all_to_all | solution.py:471
  87.1 0.7 home_sum.1
Async XLA Ops:
  0.6 30.0 %copy-start.1 = (bf16[288,288]{1,0:T(8,128)(2,1)S(1)}, bf16[288,288]{1,0:T(8,128)(2,1)}, u32[]{:S(2)}) copy-start(bf16[288,288]{1,0:T(8,128)(2,1)} %constant.31.clone.swap_ref) | copy-start | bytes 497668
  0.6 30.0 %copy-start.4 = (bf16[64,1152]{1,0:T(8,128)(2,1)S(1)}, bf16[64,1152]{1,0:T(8,128)(2,1)}, u32[]{:S(2)}) copy-start(bf16[64,1152]{1,0:T(8,128)(2,1)} %constant.32.clone.take_ref) | copy-start | bytes 442372
  0.7 35.8 %copy-start.3 = (bf16[128,640]{1,0:T(8,128)(2,1)S(1)}, bf16[128,640]{1,0:T(8,128)(2,1)}, u32[]{:S(2)}) copy-start(bf16[128,640]{1,0:T(8,128)(2,1)} %refs_0_.1) | copy-start | bytes 491524
  3.7 26.9 %all-to-all-start = ((bf16[64,9,2,128]{3,2,1,0:T(2,128)(2,1)}), bf16[64,9,2,128]{3,2,1,0:T(2,128)(2,1)S(1)}, u32[]{:S(2)}, u32[]{:S(2)}) async-start(bf16[64,9,2,128]{3,2,1,0:T(2,128)(2,1)} %bitcast.2), calls=%async_computation | async-start | bytes 589824 | tf_op jit(solution)/shard_map/all_to_all | solution.py:386
  16.9 6.8 %collective-permute-start = (bf16[128,640]{1,0:T(8,128)(2,1)}, bf16[128,640]{1,0:T(8,128)(2,1)S(1)}, u32[]{:S(2)}, u32[]{:S(2)}) collective-permute-start(bf16[128,640]{1,0:T(8,128)(2,1)} %refs_0_.1), channel_id=1, source_target_pairs={{0,1},{1,2},{2,3},{3,0},{4,5},{5,6},{6,7},{7,4},{8,9},{9,10},{10,1... | collective-permute-start | bytes 491528 | tf_op jit(solution)/shard_map/ppermute | solution.py:344
  18.2 5.5 %collective-permute-start.1 = (bf16[128,640]{1,0:T(8,128)(2,1)}, bf16[128,640]{1,0:T(8,128)(2,1)S(1)}, u32[]{:S(2)}, u32[]{:S(2)}) collective-permute-start(bf16[128,640]{1,0:T(8,128)(2,1)} %refs_0_.1), channel_id=1, source_target_pairs={{0,3},{1,0},{2,1},{3,2},{4,7},{5,4},{6,5},{7,6},{8,11},{9,8},{10,9... | collective-permute-start | bytes 491528 | tf_op jit(solution)/shard_map/ppermute | solution.py:344
  19.6 0.9 %copy-start.2 = (bf16[128,640]{1,0:T(8,128)(2,1)S(1)}, bf16[128,640]{1,0:T(8,128)(2,1)}, u32[]{:S(2)}) copy-start(bf16[128,640]{1,0:T(8,128)(2,1)} %refs_0_.1) | copy-start | bytes 491524
  22.4 23.8 %copy-start = (bf16[128,1024]{1,0:T(8,128)(2,1)S(1)}, bf16[128,1024]{1,0:T(8,128)(2,1)}, u32[]{:S(2)}) copy-start(bf16[128,1024]{1,0:T(8,128)(2,1)} %q_ref.1) | copy-start | bytes 786436
  22.5 23.8 %copy-start.6 = (bf16[128,128]{1,0:T(8,128)(2,1)S(1)}, bf16[128,128]{1,0:T(8,128)(2,1)}, u32[]{:S(2)}) copy-start(bf16[128,128]{1,0:T(8,128)(2,1)} %ks_ref.1) | copy-start | bytes 98308
  22.5 23.8 %copy-start.7 = (bf16[128,128]{1,0:T(8,128)(2,1)S(1)}, bf16[128,128]{1,0:T(8,128)(2,1)}, u32[]{:S(2)}) copy-start(bf16[128,128]{1,0:T(8,128)(2,1)} %vs_ref.1) | copy-start | bytes 98308
  32.3 13.9 %all-to-all-start.1 = ((bf16[16,128,128]{2,1,0:T(8,128)(2,1)}), bf16[16,128,128]{2,1,0:T(8,128)(2,1)S(1)}, u32[]{:S(2)}, u32[]{:S(2)}) async-start(bf16[16,128,128]{2,1,0:T(8,128)(2,1)} %get-tuple-element.31), calls=%async_computation.1 | async-start | bytes 1048576 | tf_op jit(solution)/shard_map/all_to_all | solution.py:342
  36.4 7.4 %collective-permute-start.2 = (bf16[128,640]{1,0:T(8,128)(2,1)S(1)}, bf16[128,640]{1,0:T(8,128)(2,1)S(1)}, u32[]{:S(2)}, u32[]{:S(2)}) collective-permute-start(bf16[128,640]{1,0:T(8,128)(2,1)S(1)} %copy-done.3), channel_id=1, source_target_pairs={{0,2},{1,3},{2,0},{3,1},{4,6},{5,7},{6,4},{7,5},{8,10},{9,11},{10,... | collective-permute-start | bytes 491528 | tf_op jit(solution)/shard_map/ppermute | solution.py:344
  51.1 14.4 %all-to-all-start.2 = ((bf16[16,128,128]{2,1,0:T(8,128)(2,1)}), bf16[16,128,128]{2,1,0:T(8,128)(2,1)S(1)}, u32[]{:S(2)}, u32[]{:S(2)}) async-start(bf16[16,128,128]{2,1,0:T(8,128)(2,1)} %get-tuple-element.50), calls=%async_computation.2 | async-start | bytes 1048576 | tf_op jit(solution)/shard_map/all_to_all | solution.py:342
  55.7 9.9 %copy-start.5 = (bf16[256,256]{1,0:T(8,128)(2,1)S(1)}, bf16[256,256]{1,0:T(8,128)(2,1)}, u32[]{:S(2)}) copy-start(bf16[256,256]{1,0:T(8,128)(2,1)} %constant.33.clone.swap_ref) | copy-start | bytes 393220
  57.8 6.9 %collective-permute-start.3 = (bf16[128,640]{1,0:T(8,128)(2,1)S(1)}, bf16[128,640]{1,0:T(8,128)(2,1)S(1)}, u32[]{:S(2)}, u32[]{:S(2)}) collective-permute-start(bf16[128,640]{1,0:T(8,128)(2,1)S(1)} %get-tuple-element.43), channel_id=1, source_target_pairs={{0,1},{1,2},{2,3},{3,0},{4,5},{5,6},{6,7},{7,4},{8,9},{9,10},{10,1... | collective-permute-start | bytes 491528 | tf_op jit(solution)/shard_map/ppermute | solution.py:344
  59.1 5.6 %collective-permute-start.4 = (bf16[128,640]{1,0:T(8,128)(2,1)S(1)}, bf16[128,640]{1,0:T(8,128)(2,1)S(1)}, u32[]{:S(2)}, u32[]{:S(2)}) collective-permute-start(bf16[128,640]{1,0:T(8,128)(2,1)S(1)} %get-tuple-element.44), channel_id=1, source_target_pairs={{0,3},{1,0},{2,1},{3,2},{4,7},{5,4},{6,5},{7,6},{8,11},{9,8},{10,9... | collective-permute-start | bytes 491528 | tf_op jit(solution)/shard_map/ppermute | solution.py:344
  66.8 20.3 %all-to-all-start.3 = ((bf16[64,16,128]{2,1,0:T(8,128)(2,1)}), bf16[64,16,128]{2,1,0:T(8,128)(2,1)S(1)}, u32[]{:S(2)}, u32[]{:S(2)}) async-start(bf16[64,16,128]{2,1,0:T(8,128)(2,1)} %bitcast.4), calls=%async_computation.3 | async-start | bytes 524288 | tf_op jit(solution)/shard_map/all_to_all | solution.py:471
  74.0 6.9 %collective-permute-start.5 = (bf16[128,640]{1,0:T(8,128)(2,1)S(1)}, bf16[128,640]{1,0:T(8,128)(2,1)S(1)}, u32[]{:S(2)}, u32[]{:S(2)}) collective-permute-start(bf16[128,640]{1,0:T(8,128)(2,1)S(1)} %get-tuple-element.45), channel_id=1, source_target_pairs={{0,2},{1,3},{2,0},{3,1},{4,6},{5,7},{6,4},{7,5},{8,10},{9,11},{10,... | collective-permute-start | bytes 491528 | tf_op jit(solution)/shard_map/ppermute | solution.py:344
